TPU v7x, 32 devices: a whole 2x2x4 slice. The times are simulated.
32 devices in a mesh: dp: 8 (over y, x, core), tensor: 4 (over z).
Axes of the slice: x: 2, y: 2, z: 4, core: 2. Of those that a mesh axis runs over, the one named last changes fastest.
Arguments:
- tokens: bfloat16 [36928, 1024], P(('dp', 'tensor')), may hold values from -6 to 6
- cotangent: bfloat16 [36928, 1024], P(('dp', 'tensor')), may hold values from -14 to 14
- attn_master: float32 [1024, 4, 1024], P('dp', None, 'tensor'), may hold values from -2 to 2
- attn_first: float32 [1024, 4, 1024], P('dp', None, 'tensor'), may hold values from -0.00036621094 to 0.00036621094
- attn_second: float32 [1024, 4, 1024], P('dp', None, 'tensor'), may hold values from 2.9701488e-09 to 1.1768514e-08
- attn_ema: float32 [1024, 4, 1024], P('dp', None, 'tensor'), may hold values from -0.1875 to 0.1875
- mlp_master: float32 [1024, 2, 4096], P('dp', None, 'tensor'), may hold values from -0.1875 to 0.1875
- mlp_first: float32 [1024, 2, 4096], P('dp', None, 'tensor'), may hold values from -0.00036621094 to 0.00036621094
- mlp_second: float32 [1024, 2, 4096], P('dp', None, 'tensor'), may hold values from 2.9701488e-09 to 1.1768514e-08
- mlp_ema: float32 [1024, 2, 4096], P('dp', None, 'tensor'), may hold values from -0.1875 to 0.1875
- msg_master: float32 [1024, 5, 1024], P('dp'), may hold values from -0.1875 to 0.1875
- msg_first: float32 [1024, 5, 1024], P('dp'), may hold values from -4.5776367e-05 to 4.5776367e-05
- msg_second: float32 [1024, 5, 1024], P('dp'), may hold values from 4.1180573e-11 to 1.631683e-10
- msg_ema: float32 [1024, 5, 1024], P('dp'), may hold values from -0.1875 to 0.1875
- vec_master: float32 [1024, 18], P('dp'), may hold values from -3 to 3
- vec_first: float32 [1024, 18], P('dp'), may hold values from -0.0014648438 to 0.0014648438
- vec_second: float32 [1024, 18], P('dp'), may hold values from 4.7074057e-08 to 1.9053785e-07
- vec_ema: float32 [1024, 18], P('dp'), may hold values from 0.5 to 1.5
Outputs:
- block_output: float32 [36928, 1024], P(('dp', 'tensor'))
- input_grad: float32 [36928, 1024], P(('dp', 'tensor'))
- grad_norm: float32 [], replicated
- attn_grad: float32 [1024, 4, 1024], P('dp', None, 'tensor')
- attn_first_new: float32 [1024, 4, 1024], P('dp', None, 'tensor')
- attn_second_new: float32 [1024, 4, 1024], P('dp', None, 'tensor')
- attn_weight: float32 [1024, 4, 1024], P('dp', None, 'tensor')
- attn_average: float32 [1024, 4, 1024], P('dp', None, 'tensor')
- mlp_grad: float32 [1024, 2, 4096], P('dp', None, 'tensor')
- mlp_first_new: float32 [1024, 2, 4096], P('dp', None, 'tensor')
- mlp_second_new: float32 [1024, 2, 4096], P('dp', None, 'tensor')
- mlp_weight: float32 [1024, 2, 4096], P('dp', None, 'tensor')
- mlp_average: float32 [1024, 2, 4096], P('dp', None, 'tensor')
- msg_grad: float32 [1024, 5, 1024], P('dp')
- msg_first_new: float32 [1024, 5, 1024], P('dp')
- msg_second_new: float32 [1024, 5, 1024], P('dp')
- msg_weight: float32 [1024, 5, 1024], P('dp')
- msg_average: float32 [1024, 5, 1024], P('dp')
- vec_grad: float32 [1024, 18], P('dp')
- vec_first_new: float32 [1024, 18], P('dp')
- vec_second_new: float32 [1024, 18], P('dp')
- vec_weight: float32 [1024, 18], P('dp')
- vec_average: float32 [1024, 18], P('dp')
All inputs are finite; a program needn't handle non-finite values.
Results may differ from a plain program's by a relative error of at most 0.025.
The roundings to bfloat16 on the way count: a program that leaves them out, or rounds other values in their place, can miss the bound.
Values may be sent and summed in bfloat16 or wider, within the bound.
No kernel may reach another device: no remote copies, remote signals or barrier semaphores. Data moves between devices by JAX's collectives and lax.ppermute only.
A program may use at most 320 MiB of HBM per device.

v0:
```python
import functools

import jax
import jax.numpy as jnp
from jax import lax
from jax.experimental import pallas as pl
from jax.experimental.pallas import tpu as pltpu
from jax.sharding import PartitionSpec as P

D = 1024
HEADS = 16
HEAD = 64
FF = 4096
PATCHES = 577
FRAMES = 8
STEP = 10
ROWS = 592


norm_eps = 1e-05
beta_one = 0.9
beta_two = 0.95
adam_eps = 1e-08
decay_mat = 0.05
ema_keep = 0.7
clip_limit = 1.0
rate_mat = 0.02
rate_vec = 0.4
far_below = -1e30
COST_PART = 16
bf16 = jnp.bfloat16
f32 = jnp.float32
NN = (((1,), (0,)), ((), ()))
NT = (((1,), (1,)), ((), ()))
TN = (((0,), (0,)), ((), ()))


def dot(left_side, right_side, dims=NN):
    return lax.dot_general(left_side, right_side, dims, preferred_element_type=f32)


def norm_rows(values, gain_row, shift_row):
    centre = values - jnp.mean(values, -1, keepdims=True)
    spread = jnp.mean(centre * centre, -1, keepdims=True)
    inverse = lax.rsqrt(spread + norm_eps)
    scaled = centre * inverse
    return (scaled * gain_row + shift_row, scaled, inverse)


def norm_back(gradient, scaled, inverse, gain_row):
    inner = gradient * gain_row
    return inverse * (
        inner
        - jnp.mean(inner, -1, keepdims=True)
        - scaled * jnp.mean(inner * scaled, -1, keepdims=True)
    )


def pad_rows(values, count):
    if values.shape[0] == count:
        return values
    extra = jnp.zeros((count - values.shape[0],) + values.shape[1:], values.dtype)
    return jnp.concatenate([values, extra], 0)


def head_pair(queries, key_rows, head):
    lane = lax.broadcasted_iota(jnp.int32, queries.shape, 1)
    key_lane = lax.broadcasted_iota(jnp.int32, key_rows.shape, 1)
    key_row = lax.broadcasted_iota(jnp.int32, key_rows.shape, 0)
    spare = HEAD * (1 - head)
    mask = jnp.where(
        (key_lane == spare) & (key_row > PATCHES), jnp.asarray(far_below, bf16), jnp.asarray(0, bf16)
    )
    keys_one = jnp.where((key_lane // HEAD) == head, key_rows, mask)
    queries_one = jnp.where(lane == spare, jnp.asarray(1, bf16), queries)
    return queries_one, keys_one


def attend_forward_kernel(q_ref, k_ref, v_ref, out_ref, total_ref):
    rows = q_ref.shape[1]
    key_count = -(-rows // 128) * 128
    queries = q_ref[0] * jnp.asarray(HEAD**-0.5, bf16)
    key_rows = pad_rows(k_ref[0], key_count)
    value_rows = pad_rows(v_ref[0], key_count)
    lane = lax.broadcasted_iota(jnp.int32, (rows, 128), 1)
    outs, totals = [], []
    for head in range(2):
        queries_one, keys_one = head_pair(queries, key_rows, head)
        scores = dot(queries_one, keys_one, NT)
        highest = jnp.max(scores, 1, keepdims=True)
        shifted = jnp.exp(scores - highest)
        total = jnp.sum(shifted, 1, keepdims=True)
        probability = (shifted * (1.0 / total)).astype(bf16)
        outs.append(dot(probability, value_rows))
        totals.append(highest + jnp.log(total))
    out_ref[0] = jnp.where(lane < HEAD, outs[0], outs[1]).astype(bf16)
    both = jnp.where(lane < HEAD, totals[0], totals[1]).T
    total_ref[0, 0] = jnp.concatenate([both[0:1], both[HEAD : HEAD + 1]], 0)


def attend_backward_kernel(q_ref, k_ref, v_ref, total_ref, grad_ref, *rest):
    dq_ref, dk_ref, dv_ref = rest[-3:]
    rows = q_ref.shape[1]
    query_count = -(-rows // 128) * 128
    queries = pad_rows(q_ref[0], query_count) * jnp.asarray(HEAD**-0.5, bf16)
    grads = pad_rows(grad_ref[0], query_count)
    key_rows = k_ref[0]
    value_rows = v_ref[0]
    keys_t = pad_rows(key_rows, query_count).astype(f32).T.astype(bf16)
    lane = lax.broadcasted_iota(jnp.int32, (rows, 128), 1)
    grad_q, grad_k, grad_v = [], [], []
    for head in range(2):
        queries_one, keys_one = head_pair(queries, key_rows, head)
        total = total_ref[0, 0, head : head + 1, :]
        if query_count > rows:
            total = jnp.concatenate([total, jnp.zeros((1, query_count - rows), f32)], 1)
        probability = jnp.exp(dot(keys_one, queries_one, NT) - total)
        values_one = jnp.where((lane // HEAD) == head, value_rows, jnp.asarray(0, bf16))
        grad_prob = dot(values_one, grads, NT)
        inner = jnp.sum(grad_prob * probability, 0, keepdims=True)
        grad_scores = (probability * (grad_prob - inner)).astype(bf16)
        grad_v.append(dot(probability.astype(bf16), grads))
        grad_k.append(dot(grad_scores, queries))
        grad_q.append(dot(keys_t[HEAD * head : HEAD * (head + 1)], pad_rows(grad_scores, query_count)))
    grad_q = jnp.concatenate(grad_q, 0) * HEAD**-0.5
    dq_ref[0] = grad_q.T[:rows].astype(bf16)
    dk_ref[0] = jnp.where(lane < HEAD, grad_k[0], grad_k[1]).astype(bf16)
    dv_ref[0] = jnp.where(lane < HEAD, grad_v[0], grad_v[1]).astype(bf16)


def cost(flops, moved):
    return pl.CostEstimate(
        flops=flops // COST_PART, bytes_accessed=moved // COST_PART, transcendentals=0
    )


def attend_cost(frames, rows, width, matmuls):
    return cost(2 * matmuls * frames * rows * rows * width, 4 * matmuls * frames * rows * width)


def attend_forward(queries, key_rows, value_rows):
    frames, rows, width = queries.shape
    spec = pl.BlockSpec((1, rows, 128), lambda f, h: (f, 0, h))
    return pl.pallas_call(
        attend_forward_kernel,
        grid=(frames, width // 128),
        in_specs=[spec] * 3,
        out_specs=[spec, pl.BlockSpec((1, 1, 2, rows), lambda f, h: (f, h, 0, 0))],
        out_shape=[
            jax.ShapeDtypeStruct((frames, rows, width), bf16),
            jax.ShapeDtypeStruct((frames, width // 128, 2, rows), f32),
        ],
        compiler_params=pltpu.CompilerParams(vmem_limit_bytes=48 << 20),
        cost_estimate=attend_cost(frames, rows, width, 4),
        name="attend_forward",
    )(queries, key_rows, value_rows)


def attend_backward(queries, key_rows, value_rows, totals, grads, begin, count, earlier=()):
    frames, rows, width = queries.shape
    spec = pl.BlockSpec((1, rows, 128), lambda f, h: (f, 0, h + begin))
    total_spec = pl.BlockSpec((1, 1, 2, rows), lambda f, h: (f, h + begin, 0, 0))
    return pl.pallas_call(
        attend_backward_kernel,
        grid=(frames, count),
        in_specs=[spec] * 3 + [total_spec, spec] + [pl.BlockSpec(memory_space=pl.ANY)] * len(earlier),
        out_specs=[spec] * 3,
        out_shape=[jax.ShapeDtypeStruct((frames, rows, width), bf16)] * 3,
        input_output_aliases={5 + i: i for i in range(len(earlier))},
        compiler_params=pltpu.CompilerParams(vmem_limit_bytes=48 << 20),
        cost_estimate=attend_cost(frames, rows, count * 128, 8),
        name="attend_backward",
    )(queries, key_rows, value_rows, totals, grads, *earlier)


def feed_kernel(
    n2_ref,
    n2t_ref,
    g_ref,
    gt_ref,
    bias_ref,
    *refs,
):
    up_refs, down_refs = refs[:4], refs[4:8]
    out_ref, dn2_ref, dup_own_ref, dup_other_ref, ddown_own_ref, ddown_other_ref = refs[8:14]
    db_ref, act_ref, dpre_ref = refs[14:]
    frames, rows = n2_ref.shape[:2]
    blocks, _, part, chunk = dup_own_ref.shape
    half = blocks * part

    @pl.when(pl.program_id(0) == 0)
    def _():
        out_ref[...] = jnp.zeros_like(out_ref)
        dn2_ref[...] = jnp.zeros_like(dn2_ref)
        act_ref[...] = jnp.zeros_like(act_ref)
        dpre_ref[...] = jnp.zeros_like(dpre_ref)

    first = jnp.concatenate(halves(up_refs, 0, 0), 0)
    second = jnp.concatenate(halves(down_refs, 1, 0), 0)
    bias_sum = jnp.zeros((1, chunk), f32)
    for frame in range(frames):
        place = pl.ds(frame * rows, rows)
        pre = dot(n2_ref[frame], first) + bias_ref[0]
        sigma = 1.0 / (1.0 + jnp.exp(-1.702 * pre))
        act = (pre * sigma).astype(bf16)
        act_ref[place] = act
        out_ref[frame] += dot(act, second, NT)
        grad_act = dot(g_ref[frame], second)
        grad_pre = grad_act * (sigma + 1.702 * pre * sigma * (1.0 - sigma))
        grad_low = grad_pre.astype(bf16)
        dpre_ref[place] = grad_low
        bias_sum += jnp.sum(grad_low.astype(f32), 0, keepdims=True)
        dn2_ref[frame] += dot(grad_low, first, NT)
    db_ref[0] = bias_sum

    def place_grad(left_ref, right_ref, own_ref, other_ref):
        for at, ref in ((0, own_ref), (half, other_ref)):
            grad = dot(left_ref[at : at + half], right_ref[...]).astype(bf16)
            ref[:, 0] = grad.reshape(blocks, part, chunk)

    place_grad(n2t_ref, dpre_ref, dup_own_ref, dup_other_ref)
    place_grad(gt_ref, act_ref, ddown_own_ref, ddown_other_ref)


def feed_forward(n2, n2t, grads, grads_t, bias, weights):
    frames, rows, _ = n2.shape
    blocks, ff_blocks, part, local = weights[0].shape
    blocks = 2 * blocks
    chunk = min(512, local)
    per = local // chunk
    steps = ff_blocks * per
    deep = n2t.shape[1]
    whole3 = lambda n: (0, 0, 0)
    whole2 = lambda n: (0, 0)
    single = pl.Buffered(1)
    w_spec = pl.BlockSpec((blocks // 2, 1, part, chunk), lambda n: (0, n // per, 0, n % per))
    dw_spec = pl.BlockSpec((blocks, 1, part, chunk), lambda n: (0, n // per, 0, n % per))
    dw_shape = jax.ShapeDtypeStruct((blocks, ff_blocks, part, local), bf16)
    return pl.pallas_call(
        feed_kernel,
        grid=(steps,),
        in_specs=[
            pl.BlockSpec((frames, rows, D), whole3, pipeline_mode=single),
            pl.BlockSpec((D, deep), whole2, pipeline_mode=single),
            pl.BlockSpec((frames, rows, D), whole3, pipeline_mode=single),
            pl.BlockSpec((D, deep), whole2, pipeline_mode=single),
            pl.BlockSpec((1, 1, chunk), lambda n: (n, 0, 0)),
        ]
        + [w_spec] * 8,
        out_specs=[pl.BlockSpec((frames, rows, D), whole3)] * 2
        + [dw_spec] * 4
        + [pl.BlockSpec((1, 1, chunk), lambda n: (n, 0, 0))],
        out_shape=[jax.ShapeDtypeStruct((frames, rows, D), f32)] * 2
        + [dw_shape] * 4
        + [jax.ShapeDtypeStruct((steps, 1, chunk), f32)],
        scratch_shapes=[pltpu.VMEM((deep, chunk), bf16), pltpu.VMEM((deep, chunk), bf16)],
        compiler_params=pltpu.CompilerParams(vmem_limit_bytes=60 << 20),
        cost_estimate=cost(
            12 * frames * rows * D * ff_blocks * local,
            8 * D * ff_blocks * local + 16 * frames * rows * D,
        ),
        name="feed_forward",
    )(n2, n2t, grads, grads_t, bias.reshape(steps, 1, chunk), *weights)


BLOCK = 128
BLOCKS = D // BLOCK


def permuted(ref, info_ref, first):
    return jnp.concatenate(
        [
            ref[:, pl.ds(pl.multiple_of(info_ref[first + i] * BLOCK, BLOCK), BLOCK)]
            for i in range(BLOCKS)
        ],
        1,
    )


def call(
    kernel, info, args, grid, in_specs, out_specs, out_shape, name, scratch=(), flops=0, vmem=56, aliases=None
):
    moved = sum(a.size * a.dtype.itemsize for a in args)
    moved += sum(o.size * o.dtype.itemsize for o in out_shape)
    return pl.pallas_call(
        kernel,
        grid_spec=pltpu.PrefetchScalarGridSpec(
            num_scalar_prefetch=1,
            grid=grid,
            in_specs=in_specs,
            out_specs=out_specs,
            scratch_shapes=list(scratch),
        ),
        out_shape=out_shape,
        input_output_aliases=aliases or {},
        compiler_params=pltpu.CompilerParams(vmem_limit_bytes=vmem << 20),
        cost_estimate=cost(flops, moved),
        name=name,
    )(info, *args)


def shaped(dtype, *shape):
    return jax.ShapeDtypeStruct(shape, dtype)


def once(*block, at=None):
    index = at or (0,) * len(block)
    return pl.BlockSpec(block, lambda *_: index, pipeline_mode=pl.Buffered(1))


def kept(*block):
    index = (0,) * len(block)
    return pl.BlockSpec(block, lambda *_: index)


def row_count(frames):
    return -(-frames * ROWS // 128) * 128


def prepare_kernel(info_ref, tokens_ref, cot_ref, x_ref, g_ref, gt_ref, gsum_ref, hold_ref):
    frames = x_ref.shape[0]
    count = tokens_ref.shape[0]
    inside = lax.broadcasted_iota(jnp.int32, (ROWS, BLOCK), 0) < PATCHES
    hold_ref[...] = jnp.zeros_like(hold_ref)

    def padded(ref):
        hold_ref[0:count] = ref[...].astype(f32)
        return [
            jnp.where(inside, hold_ref[pl.ds(f * PATCHES, ROWS)], 0.0) for f in range(frames)
        ]

    for f, rows in enumerate(padded(tokens_ref)):
        x_ref[f] = rows.astype(bf16)
    grads = padded(cot_ref)
    for f, rows in enumerate(grads):
        g_ref[f] = rows.astype(bf16)
    full = pad_rows(jnp.concatenate(grads, 0), gt_ref.shape[1])
    gt_ref[...] = full.T.astype(bf16)
    gsum_ref[...] = jnp.sum(full, 0, keepdims=True)


def prepare(info, tokens, cotangent):
    count = tokens.shape[0]
    frames = count // PATCHES
    deep = row_count(frames)
    taken = pl.BlockSpec((count, BLOCK), lambda r, info_ref: (0, info_ref[r]))
    placed = pl.BlockSpec((frames, ROWS, BLOCK), lambda r, info_ref: (0, 0, r))
    return call(
        prepare_kernel,
        info,
        (tokens, cotangent),
        (BLOCKS,),
        [taken] * 2,
        [
            placed,
            placed,
            pl.BlockSpec((BLOCK, deep), lambda r, info_ref: (r, 0)),
            pl.BlockSpec((1, BLOCK), lambda r, info_ref: (0, r)),
        ],
        [
            shaped(bf16, frames, ROWS, D),
            shaped(bf16, frames, ROWS, D),
            shaped(bf16, D, deep),
            shaped(f32, 1, D),
        ],
        "prepare",
        [pltpu.VMEM((-(-((frames - 1) * PATCHES + ROWS) // 8) * 8, BLOCK), f32)],
    )


def plain_order_kernel(info_ref, in_ref, out_ref):
    out_ref[...] = permuted(in_ref, info_ref, BLOCKS)


def plain_order(info, values):
    return call(
        plain_order_kernel,
        info,
        (values,),
        (1,),
        [kept(*values.shape)],
        [kept(*values.shape)],
        [shaped(f32, *values.shape)],
        "plain_order",
    )[0]


def finish_kernel(count, info_ref, *refs):
    in_refs, row_ref, out_ref = refs[:count], refs[count], refs[-1]
    frames = in_refs[0].shape[0]
    for f in range(frames):
        rows = in_refs[0][f]
        for ref in in_refs[1:]:
            rows = rows + ref[f]
        if row_ref.shape[0] == 1:
            rows = rows + row_ref[...]
        else:
            class_row = row_ref[pl.ds(info_ref[2 * BLOCKS] * frames + f, 1)]
            first = lax.broadcasted_iota(jnp.int32, (ROWS, BLOCK), 0) == 0
            rows = rows + jnp.where(first, class_row, 0.0)
        out_ref[pl.ds(f * PATCHES, PATCHES)] = rows[:PATCHES]


def finish(info, parts, row, name, begin=0, count=BLOCKS, earlier=()):
    frames = parts[0].shape[0]
    at = lambda d, info_ref: info_ref[BLOCKS + begin + d]
    taken = pl.BlockSpec((frames, ROWS, BLOCK), lambda d, info_ref: (0, 0, at(d, info_ref)))
    row_spec = pl.BlockSpec((row.shape[0], BLOCK), lambda d, info_ref: (0, at(d, info_ref)))
    return call(
        functools.partial(finish_kernel, len(parts)),
        info,
        (*parts, row, *earlier),
        (count,),
        [taken] * len(parts) + [row_spec] + [pl.BlockSpec(memory_space=pl.ANY)] * len(earlier),
        [pl.BlockSpec((frames * PATCHES, BLOCK), lambda d, info_ref: (0, begin + d))],
        [shaped(f32, frames * PATCHES, D)],
        name,
        aliases={len(parts) + 2: 0} if earlier else {},
    )[0]


def with_message(x_ref, msg_ref, info_ref, f):
    frames = x_ref.shape[0]
    message = msg_ref[pl.ds(info_ref[2 * BLOCKS] * frames + f, 1)]
    place = lax.broadcasted_iota(jnp.int32, (ROWS, D), 0) == PATCHES
    return jnp.where(place, message, x_ref[f].astype(f32))


def put_transposed(ref, rows):
    for c in range(BLOCKS):
        block = pad_rows(rows[:, c * BLOCK : (c + 1) * BLOCK].astype(f32), ref.shape[1])
        ref[c * BLOCK : (c + 1) * BLOCK] = block.T.astype(bf16)


def halves(refs, which, *at):
    sides = []
    for pair in (refs[:2], refs[2:]):
        first, second = (ref[(slice(None), *at)] for ref in pair)
        part, width = first.shape[-2:]
        if which and part == BLOCK:
            blocks = [first[0], second[0], first[1], second[1]]
        else:
            blocks = [v.reshape(-1, width) for v in (first, second)]
        sides.append(jnp.concatenate(blocks, 0))
    return sides


def project_kernel(
    info_ref, x_ref, msg_ref, gain_ref, shift_ref, bq_ref, bv_ref, *refs
):
    a_refs, b_refs, (q_ref, k_ref, v_ref, ht_ref, h_ref) = refs[:4], refs[4:8], refs[8:]
    frames = x_ref.shape[0]

    @pl.when(pl.program_id(0) == 0)
    def _():
        for f in range(frames):
            rows = with_message(x_ref, msg_ref, info_ref, f)
            normed = norm_rows(rows, gain_ref[...], shift_ref[...])[0]
            h_ref[pl.ds(f * ROWS, ROWS)] = normed.astype(bf16)
        put_transposed(ht_ref, h_ref[...])

    sides = (slice(0, D // 2), slice(D // 2, D))
    for out_ref, weights, bias in (
        (q_ref, halves(a_refs, 0, 0, 0), bq_ref[...]),
        (k_ref, halves(a_refs, 0, 0, 1), 0.0),
        (v_ref, halves(b_refs, 1, 0, 0), bv_ref[...]),
    ):
        for f in range(frames):
            place = pl.ds(f * ROWS, ROWS)
            rows = dot(h_ref[place, sides[0]], weights[0]) + dot(h_ref[place, sides[1]], weights[1])
            out_ref[f] = (rows + bias).astype(bf16)


def project(info, x, message, vec_rel, vectors, attn):
    frames = x.shape[0]
    n, z, _, part, width = attn[0].shape
    deep = row_count(frames)
    bias = pl.BlockSpec((1, width), lambda j, info_ref: (0, j))
    a_spec = pl.BlockSpec((n, 1, 2, part, width), lambda j, info_ref: (0, j, 0, 0, 0))
    b_spec = pl.BlockSpec((n, 1, 1, part, width), lambda j, info_ref: (0, j, 0, 0, 0))
    out = pl.BlockSpec((frames, ROWS, width), lambda j, info_ref: (0, 0, j))
    return call(
        project_kernel,
        info,
        (x, message, vec_rel[0:1], vec_rel[1:2], vectors[10:11], vectors[11:12], *attn),
        (z,),
        [once(frames, ROWS, D), once(FRAMES, D), once(1, D), once(1, D), bias, bias]
        + [a_spec] * 4
        + [b_spec] * 4,
        [out] * 3 + [kept(D, deep)],
        [shaped(bf16, frames, ROWS, D)] * 3 + [shaped(bf16, D, deep)],
        "project",
        [pltpu.VMEM((frames * ROWS, D), bf16)],
        6 * frames * ROWS * D * D,
    )


def combine_kernel(
    info_ref, x_ref, a_ref, bias_ref, gain_ref, shift_ref, *refs
):
    b_refs, (mid_ref, n2_ref, n2t_ref, hold_ref) = refs[:4], refs[4:]
    frames = x_ref.shape[0]
    z, width = b_refs[0].shape[1], b_refs[0].shape[-1]
    weights = [halves(b_refs, 1, j, 0) for j in range(z)]
    for f in range(frames):
        for side in range(2):
            half = slice(side * D // 2, (side + 1) * D // 2)
            total = x_ref[f, :, half].astype(f32) + bias_ref[:, half]
            for j in range(z):
                total += dot(a_ref[f, :, j * width : (j + 1) * width], weights[j][side], NT)
            mid_ref[f, :, half] = total
        low = mid_ref[f].astype(bf16).astype(f32)
        normed = norm_rows(low, gain_ref[...], shift_ref[...])[0].astype(bf16)
        n2_ref[f] = normed
        hold_ref[pl.ds(f * ROWS, ROWS)] = normed
    put_transposed(n2t_ref, hold_ref[...])


def combine(info, x, attended, vec_rel, attn):
    frames = x.shape[0]
    n, z, _, part, width = attn[4].shape
    deep = row_count(frames)
    weight = once(n, z, 1, part, width, at=(0, 0, 1, 0, 0))
    return call(
        combine_kernel,
        info,
        (x, attended, vec_rel[12:13], vec_rel[2:3], vec_rel[3:4], *attn[4:]),
        (1,),
        [once(frames, ROWS, D)] * 2 + [once(1, D)] * 3 + [weight] * 4,
        [once(frames, ROWS, D), once(frames, ROWS, D), once(D, deep)],
        [shaped(f32, frames, ROWS, D), shaped(bf16, frames, ROWS, D), shaped(bf16, D, deep)],
        "combine",
        [pltpu.VMEM((frames * ROWS, D), bf16)],
        2 * frames * ROWS * D * D,
    )


def between_kernel(
    info_ref, ea_ref, eb_ref, mid_ref, g_ref, a_ref, gain_ref, *refs
):
    b_refs, (dmid_ref, da_ref, keep_ref, send_ref, sums_ref, total_ref, dmt_ref) = refs[:4], refs[4:]
    f = pl.program_id(0)
    n, z, part, width = keep_ref.shape
    grad = ea_ref[0] + eb_ref[0]
    low = mid_ref[0].astype(bf16).astype(f32)
    _, scaled, inverse = norm_rows(low, 1.0, 0.0)
    back = norm_back(grad, scaled, inverse, gain_ref[...])
    dmid = (g_ref[0].astype(f32) + back).astype(bf16)
    dmid_ref[0] = dmid
    sums = jnp.concatenate(
        [
            jnp.sum(grad * scaled, 0, keepdims=True),
            jnp.sum(grad, 0, keepdims=True),
            jnp.sum(dmid.astype(f32), 0, keepdims=True),
        ],
        0,
    )

    @pl.when(f == 0)
    def _():
        sums_ref[...] = jnp.zeros_like(sums_ref)
        total_ref[...] = jnp.zeros_like(total_ref)

    sums_ref[...] += sums
    for j in range(z):
        weights = halves(b_refs, 1, j, 0)
        rows = dot(dmid[:, : D // 2], weights[0]) + dot(dmid[:, D // 2 :], weights[1])
        da_ref[0, :, j * width : (j + 1) * width] = rows.astype(bf16)
    put_transposed(dmt_ref, dmid)
    attended = pad_rows(a_ref[0], dmt_ref.shape[1])
    for j in range(z):
        lanes = slice(j * width, (j + 1) * width)
        total_ref[:, lanes] += dot(dmt_ref[...], attended[:, lanes])

    @pl.when(f == pl.num_programs(0) - 1)
    def _():
        for j in range(z):
            lanes = slice(j * width, (j + 1) * width)
            for at, ref in ((0, keep_ref), (D // 2, send_ref)):
                ref[:, j] = total_ref[at : at + D // 2, lanes].astype(bf16).reshape(n, part, width)


def between(info, ea, eb, middle, grads, attended, vec_rel, attn):
    frames = ea.shape[0]
    n, z, _, part, width = attn[4].shape
    frame = pl.BlockSpec((1, ROWS, D), lambda f, info_ref: (f, 0, 0))
    weight = once(n, z, 1, part, width, at=(0, 0, 1, 0, 0))
    return call(
        between_kernel,
        info,
        (ea, eb, middle, grads, attended, vec_rel[2:3], *attn[4:]),
        (frames,),
        [frame] * 5 + [once(1, D)] + [weight] * 4,
        [frame, frame, kept(2 * n, z, part, width), kept(2 * n, z, part, width), kept(3, D)],
        [shaped(bf16, frames, ROWS, D)] * 2
        + [shaped(bf16, 2 * n, z, part, width)] * 2
        + [shaped(f32, 3, D)],
        "between",
        [pltpu.VMEM((D, D), f32), pltpu.VMEM((D, row_count(1)), bf16)],
        4 * frames * ROWS * D * D,
    )


def project_grads_kernel(
    info_ref, ht_ref, dq_ref, dk_ref, dv_ref, ok_ref, os_ref, ak_ref, as_ref, bk_ref, bs_ref, sq_ref, sv_ref
):
    frames = dq_ref.shape[0]
    deep = ht_ref.shape[1]
    n, _, _, part, width = bk_ref.shape
    bk_ref[:, 0, 1] = ok_ref[:, 0]
    bs_ref[:, 0, 1] = os_ref[:, 0]
    for w, ref in enumerate((dq_ref, dk_ref, dv_ref)):
        rows = pad_rows(jnp.concatenate([ref[f] for f in range(frames)], 0), deep)
        for at, a_ref, b_ref in ((0, ak_ref, bk_ref), (D // 2, as_ref, bs_ref)):
            grad = dot(ht_ref[at : at + D // 2], rows).astype(bf16).reshape(n, part, width)
            if w < 2:
                a_ref[:, 0, w] = grad
            else:
                b_ref[:, 0, 0] = grad
        if w != 1:
            (sq_ref if w == 0 else sv_ref)[...] = jnp.sum(rows.astype(f32), 0, keepdims=True)


def project_grads(info, normed_t, grads, out_grads, attn):
    frames = grads[0].shape[0]
    n, z, _, part, width = attn[0].shape
    n = 2 * n
    block = pl.BlockSpec((frames, ROWS, width), lambda j, info_ref: (0, 0, j))
    spec = pl.BlockSpec((n, 1, 2, part, width), lambda j, info_ref: (0, j, 0, 0, 0))
    o_spec = pl.BlockSpec((n, 1, part, width), lambda j, info_ref: (0, j, 0, 0))
    row = pl.BlockSpec((1, width), lambda j, info_ref: (0, j))
    return call(
        project_grads_kernel,
        info,
        (normed_t, *grads, *out_grads),
        (z,),
        [once(*normed_t.shape)] + [block] * 3 + [o_spec] * 2,
        [spec] * 4 + [row] * 2,
        [shaped(bf16, n, z, 2, part, width)] * 4 + [shaped(f32, 1, D)] * 2,
        "project_grads",
        (),
        6 * frames * ROWS * D * D,
    )


def project_back_kernel(
    info_ref, x_ref, msg_ref, dmid_ref, gain_ref, dq_ref, dk_ref, dv_ref, *refs
):
    a_refs, b_refs, (ing_ref, dmsg_ref, sums_ref, total_ref) = refs[:4], refs[4:8], refs[8:]
    frames = x_ref.shape[0]
    j = pl.program_id(0)

    @pl.when(j == 0)
    def _():
        total_ref[...] = jnp.zeros_like(total_ref)

    weights = [halves(a_refs, 0, 0, 0), halves(a_refs, 0, 0, 1), halves(b_refs, 1, 0, 0)]
    for side in range(2):
        half = slice(side * D // 2, (side + 1) * D // 2)
        for f in range(frames):
            rows = jnp.zeros((ROWS, D // 2), f32)
            for ref, weight in zip((dq_ref, dk_ref, dv_ref), weights):
                rows += dot(ref[f], weight[side], NT)
            total_ref[f, :, half] += rows

    @pl.when(j == pl.num_programs(0) - 1)
    def _():
        gain_sum, shift_sum = jnp.zeros((1, D), f32), jnp.zeros((1, D), f32)
        for f in range(frames):
            rows = with_message(x_ref, msg_ref, info_ref, f)
            _, scaled, inverse = norm_rows(rows, 1.0, 0.0)
            grad = total_ref[f]
            gain_sum += jnp.sum(grad * scaled, 0, keepdims=True)
            shift_sum += jnp.sum(grad, 0, keepdims=True)
            back = norm_back(grad, scaled, inverse, gain_ref[...])
            ing_ref[f] = dmid_ref[f].astype(f32) + back
            dmsg_ref[f] = back[PATCHES : PATCHES + 1]
        sums_ref[...] = jnp.concatenate([gain_sum, shift_sum], 0)


def project_back(info, x, message, dmid, vec_rel, grads, attn):
    frames = x.shape[0]
    n, z, _, part, width = attn[0].shape
    block = pl.BlockSpec((frames, ROWS, width), lambda j, info_ref: (0, 0, j))
    a_spec = pl.BlockSpec((n, 1, 2, part, width), lambda j, info_ref: (0, j, 0, 0, 0))
    b_spec = pl.BlockSpec((n, 1, 1, part, width), lambda j, info_ref: (0, j, 0, 0, 0))
    return call(
        project_back_kernel,
        info,
        (x, message, dmid, vec_rel[0:1], *grads, *attn),
        (z,),
        [once(frames, ROWS, D), once(FRAMES, D), once(frames, ROWS, D), once(1, D)]
        + [block] * 3
        + [a_spec] * 4
        + [b_spec] * 4,
        [once(frames, ROWS, D), kept(frames, 1, D), kept(2, D)],
        [shaped(f32, frames, ROWS, D), shaped(f32, frames, 1, D), shaped(f32, 2, D)],
        "project_back",
        [pltpu.VMEM((frames, ROWS, D), f32)],
        6 * frames * ROWS * D * D,
    )


def message_halves(refs, which, i):
    part = D // (4 * refs[0].shape[0])
    return halves([ref.at[:, i * part : (i + 1) * part] for ref in refs], which)


def message_times(rows, refs, i):
    own, other = rows[:, : D // 2], rows[:, D // 2 :]
    cols = []
    for which in range(2):
        weights = message_halves(refs[4 * which : 4 * which + 4], which, i)
        cols.append(dot(own, weights[0]) + dot(other, weights[1]))
    return jnp.concatenate(cols, 1)


def message_times_t(rows, refs, i):
    left, right = rows[:, : D // 2], rows[:, D // 2 :]
    first, second = message_halves(refs[:4], 0, i), message_halves(refs[4:], 1, i)
    return jnp.concatenate(
        [dot(left, first[s], NT) + dot(right, second[s], NT) for s in range(2)], 1
    )


def by_head(rows):
    full = jnp.concatenate([rows.astype(f32)] * HEADS, 0)
    return jnp.where(head_mask(), full, 0.0).astype(bf16)


def head_mask():
    shape = (HEADS * FRAMES, D)
    head = lax.broadcasted_iota(jnp.int32, shape, 0) // FRAMES
    return head == lax.broadcasted_iota(jnp.int32, shape, 1) // HEAD


def over_heads(rows):
    rows = jnp.where(head_mask(), rows, 0.0)
    return jnp.sum(rows.reshape(HEADS, FRAMES, D), 0)


def message_probability(queries, keys):
    scores = dot(by_head(queries), keys, NT) * HEAD**-0.5
    shifted = jnp.exp(scores - jnp.max(scores, 1, keepdims=True))
    return shifted * (1.0 / jnp.sum(shifted, 1, keepdims=True))


def message_forward_kernel(info_ref, cls_ref, vec_ref, *refs):
    weights, (msg_ref, first_ref, pack_ref, hold_ref) = refs[:8], refs[8:]

    def relative(rows):
        hold_ref[...] = rows
        return permuted(hold_ref, info_ref, 0)

    first = message_times(relative(cls_ref[...]).astype(bf16), weights, 0) + vec_ref[6:7]
    normed = norm_rows(first, vec_ref[4:5], vec_ref[5:6])[0].astype(bf16).astype(f32)
    normed_rel = relative(normed).astype(bf16)
    queries = (message_times(normed_rel, weights, 1) + vec_ref[7:8]).astype(bf16)
    keys = message_times(normed_rel, weights, 2).astype(bf16)
    values = (message_times(normed_rel, weights, 3) + vec_ref[8:9]).astype(bf16)
    probability = message_probability(queries, keys).astype(bf16)
    mixed = over_heads(dot(probability, values)).astype(bf16).astype(f32)
    message = first + message_times(relative(mixed).astype(bf16), weights, 4) + vec_ref[9:10]
    msg_ref[...] = relative(message)
    first_ref[...] = first
    for i, rows in enumerate((normed, mixed, queries, keys, values)):
        pack_ref[i] = rows.astype(f32)


def message_forward(info, class_rows, vectors, weights):
    one = kept(FRAMES, D)
    return call(
        message_forward_kernel,
        info,
        (class_rows, vectors, *weights),
        (1,),
        [one, kept(*vectors.shape)] + [once(*w.shape) for w in weights],
        [one, one, kept(5, FRAMES, D)],
        [shaped(f32, FRAMES, D), shaped(f32, FRAMES, D), shaped(f32, 5, FRAMES, D)],
        "message_forward",
        [pltpu.VMEM((FRAMES, D), f32)],
        10 * FRAMES * D * D,
    )


def message_backward_kernel(info_ref, dmsg_ref, first_ref, pack_ref, vec_ref, *refs):
    weights, (class_ref, sent_ref, sums_ref, hold_ref) = refs[:8], refs[8:]
    frames = dmsg_ref.shape[1]
    for i in range(dmsg_ref.shape[0]):
        place = lax.bitwise_xor(info_ref[2 * BLOCKS], i)
        for f in range(frames):
            hold_ref[i * frames + f : i * frames + f + 1] = dmsg_ref[place, f : f + 1]
    dmsg = permuted(hold_ref, info_ref, BLOCKS)

    def plain(rows):
        hold_ref[...] = rows
        return permuted(hold_ref, info_ref, BLOCKS)

    queries, keys, values = (pack_ref[i].astype(bf16) for i in (2, 3, 4))
    grad_mixed = plain(message_times_t(dmsg.astype(bf16), weights, 4)).astype(bf16)
    probability = message_probability(queries, keys)
    grads_big = by_head(grad_mixed)
    grad_prob = dot(grads_big, values, NT)
    inner = jnp.sum(grad_prob * probability, 1, keepdims=True)
    grad_scores = (probability * (grad_prob - inner)).astype(bf16)
    dq = (over_heads(dot(grad_scores, keys)) * HEAD**-0.5).astype(bf16)
    dk = (dot(grad_scores, by_head(queries), TN) * HEAD**-0.5).astype(bf16)
    dv = dot(probability.astype(bf16), grads_big, TN).astype(bf16)
    grad = plain(
        message_times_t(dq, weights, 1)
        + message_times_t(dk, weights, 2)
        + message_times_t(dv, weights, 3)
    )
    _, scaled, inverse = norm_rows(first_ref[...], 1.0, 0.0)
    back = norm_back(grad, scaled, inverse, vec_ref[4:5])
    dfirst = (dmsg + back).astype(bf16)
    class_ref[...] = message_times_t(dfirst, weights, 0)
    sent = [rows.astype(f32) for rows in (dfirst, dq, dk, dv, dmsg)]
    for i, rows in enumerate(sent):
        sent_ref[i] = rows
    sums = [grad * scaled, grad, sent[0], sent[1], sent[3], dmsg]
    sums_ref[...] = jnp.concatenate([jnp.sum(rows, 0, keepdims=True) for rows in sums], 0)


def message_backward(info, dmsg, first, pack, vectors, weights):
    one = kept(FRAMES, D)
    return call(
        message_backward_kernel,
        info,
        (dmsg, first, pack, vectors, *weights),
        (1,),
        [kept(*dmsg.shape), one, kept(*pack.shape), kept(*vectors.shape)]
        + [once(*w.shape) for w in weights],
        [one, kept(5, FRAMES, D), kept(6, D)],
        [shaped(f32, FRAMES, D), shaped(f32, 5, FRAMES, D), shaped(f32, 6, D)],
        "message_backward",
        [pltpu.VMEM((FRAMES, D), f32)],
        10 * FRAMES * D * D,
    )


def relative_order():
    return lax.axis_size("dp") * BLOCK == D


def make_info():
    place = lax.iota(jnp.int32, BLOCKS)
    if relative_order():
        mine = lax.axis_index("dp")
        differs = place ^ mine
        places = mine ^ (2 * (place % 4) + place // 4)
        blocks = (differs % 2) * 4 + differs // 2
    else:
        places = blocks = place
    return jnp.concatenate([places, blocks, lax.axis_index("tensor")[None]]).astype(jnp.int32)


def swap(values, axis, bit):
    pairs = [(i, i ^ bit) for i in range(lax.axis_size(axis))]
    return lax.ppermute(values, axis, pairs)


def bits_of(axis):
    size = lax.axis_size(axis)
    return [1 << i for i in range(size.bit_length() - 1)]


def after(values, *earlier):
    return lax.optimization_barrier((values, earlier))[0]


def join_kernel(*refs):
    count = len(refs) // 3
    for i in range(count):
        out_ref = refs[2 * count + i]
        out_ref[0] = refs[2 * i][...]
        out_ref[1] = refs[2 * i + 1][...]


def join(*pairs):
    flat = [v.reshape(-1, v.shape[-1]) for pair in pairs for v in pair]
    specs = [pl.BlockSpec((v.shape[0] // 2, v.shape[1]), lambda i: (i, 0)) for v in flat]
    out = pl.pallas_call(
        join_kernel,
        grid=(2,),
        in_specs=specs,
        out_specs=[
            pl.BlockSpec((2, v.shape[0] // 2, v.shape[1]), lambda i: (0, i, 0)) for v in flat[::2]
        ],
        out_shape=[shaped(bf16, 2, *v.shape) for v in flat[::2]],
        compiler_params=pltpu.CompilerParams(vmem_limit_bytes=48 << 20),
        cost_estimate=cost(0, sum(2 * v.size for v in flat)),
        name="join",
    )(*flat)
    return [v.reshape((2,) + pair[0].shape) for v, pair in zip(out, pairs)]


class Gather:
    def __init__(self, *values):
        self.own, self.place = list(values), 0
        if relative_order():
            self.arrived = [swap(v, "dp", bit) for v, bit in zip(values, (2, 4))]
            return
        self.pieces = []
        for v in values:
            everything = lax.all_gather(v, "dp", axis=0)
            count = everything.shape[0] // 4
            self.pieces += [everything[i * count : (i + 1) * count] for i in range(4)]
        self.arrived = self.pieces

    def step(self):
        if not relative_order():
            return self.pieces
        self.place += 1
        if self.place == 1:
            self.own = join(*zip(self.own, self.arrived))
            self.arrived = [swap(v, "dp", bit) for v, bit in zip(self.own, (4, 2))]
            return self.own
        self.pieces = [v for pair in zip(self.own, self.arrived) for v in pair]
        self.arrived = [swap(v, "dp", 1) for v in self.pieces]
        return self.pieces

    def result(self):
        if not relative_order():
            return self.pieces
        return [v for i in (0, 2) for v in self.pieces[i : i + 2] + self.arrived[i : i + 2]]


def beside(outputs, *transfers):
    outputs, arrived = lax.optimization_barrier((outputs, [t.arrived for t in transfers]))
    for t, values in zip(transfers, arrived):
        t.arrived = values
    return outputs


def add_low(left_side, right_side):
    return (left_side.astype(f32) + right_side.astype(f32)).astype(bf16)


def add_kernel(axes, *refs):
    ins, outs = refs[: 2 * len(axes)], refs[2 * len(axes) :]
    for i, axis in enumerate(axes):
        for side in range(2):
            at = (side,) if axis == 0 else (slice(None), side)
            outs[2 * i + side][...] = add_low(ins[2 * i][at], ins[2 * i + 1][at])


def add_and_split(pairs, axes):
    lead = pairs[0][0].shape[:-2]
    rows, width = pairs[0][0].shape[-2:]
    steps = 4 if rows % 64 == 0 else 1
    zeros = (0,) * len(lead)
    spec = pl.BlockSpec((*lead, rows // steps, width), lambda i: (*zeros, i, 0))
    out = pl.BlockSpec((*lead[1:], rows // steps, width), lambda i: (*zeros[1:], i, 0))
    return pl.pallas_call(
        functools.partial(add_kernel, axes),
        grid=(steps,),
        in_specs=[spec] * (2 * len(pairs)),
        out_specs=[out] * (2 * len(pairs)),
        out_shape=[shaped(bf16, *lead[1:], rows, width)] * (2 * len(pairs)),
        compiler_params=pltpu.CompilerParams(vmem_limit_bytes=48 << 20),
        cost_estimate=cost(0, sum(4 * a.size for a, _ in pairs)),
        name="add",
    )(*[v for pair in pairs for v in pair])


class Scatter:
    def __init__(self, keep, send):
        self.place, self.shape = 0, keep[0].shape[1:]
        if not relative_order():
            self.held = [
                lax.psum_scatter(jnp.concatenate(v, 0), "dp", scatter_dimension=0, tiled=False)
                for v in zip(keep, send)
            ]
            self.arrived = [jnp.zeros_like(v) for v in self.held]
            return
        width = self.shape[-1]
        self.held = [v.reshape(2, 2, -1, width) for v in keep]
        self.arrived = [swap(v, "dp", 1).reshape(2, 2, -1, width) for v in send]

    def step(self):
        if not relative_order():
            return self.held
        axes, bits = ((0, 1), (4, 2)) if self.place == 0 else ((0, 0), (2, 4))
        self.place += 1
        sums = list(add_and_split(list(zip(self.held, self.arrived)), axes))
        self.held, going = sums[::2], sums[1::2]
        self.arrived = [swap(v, "dp", bit) for v, bit in zip(going, bits)]
        return going


def pair_kernel(info_ref, *refs):
    ins, outs = refs[:8], refs[8:]
    rows = ins[0].shape[1]
    for side in range(2):
        for i in range(2):
            total = add_low(ins[4 * i + side][0], ins[4 * i + 2 + side][0])
            outs[side][0, i * rows : (i + 1) * rows] = total


def add_and_pair(info, held, arrived):
    rows, width = held[0][0].size // held[0].shape[-1], held[0].shape[-1]
    own = pl.BlockSpec((1, rows, width), lambda h, ref: (2 * h + ref[2 * BLOCKS] % 2, 0, 0))
    other = pl.BlockSpec((1, rows, width), lambda h, ref: (2 * h + 1 - ref[2 * BLOCKS] % 2, 0, 0))
    flat = [v.reshape(4, rows, width) for pair in zip(held, arrived) for v in pair for _ in range(2)]
    out = pl.BlockSpec((1, 2 * rows, width), lambda h, ref: (h, 0, 0))
    return call(
        pair_kernel,
        info,
        flat,
        (2,),
        [own, other] * 4,
        [out] * 2,
        [shaped(bf16, 2, 2 * rows, width)] * 2,
        "add_and_pair",
    )


def single_kernel(info_ref, ho_ref, hp_ref, ao_ref, ap_ref, held_ref, going_ref):
    held_ref[...] = add_low(ho_ref[0], ao_ref[0])
    going_ref[...] = add_low(hp_ref[0], ap_ref[0])


def add_and_single(info, held, arrived):
    _, rows, width = held.shape
    own = pl.BlockSpec((1, rows, width), lambda i, ref: (ref[2 * BLOCKS] // 2, 0, 0))
    other = pl.BlockSpec((1, rows, width), lambda i, ref: (1 - ref[2 * BLOCKS] // 2, 0, 0))
    return call(
        single_kernel,
        info,
        (held, held, arrived, arrived),
        (1,),
        [own, other] * 2,
        [kept(rows, width)] * 2,
        [shaped(bf16, rows, width)] * 2,
        "add_and_single",
    )


class ScatterVideos:
    def __init__(self, info, sums):
        self.info, self.shape = info, sums.shape
        self.direct = lax.axis_size("tensor") != 4
        if self.direct:
            values = jnp.stack([add_low(h, a) for h, a in zip(sums.held, sums.arrived)], 1)
            self.held = lax.psum_scatter(values, "tensor", scatter_dimension=0, tiled=False)
            self.going, self.arrived = self.held, jnp.zeros_like(self.held)
            return
        held = [v.reshape(self.shape) for v in sums.held]
        arrived = [v.reshape(self.shape) for v in sums.arrived]
        self.held, self.going = add_and_pair(info, held, arrived)
        self.arrived = swap(self.going, "tensor", 1)

    def step(self):
        if self.direct:
            return self.held
        self.held, going = add_and_single(self.info, self.held, self.arrived)
        self.arrived = swap(going, "tensor", 2)
        return going

    def result(self):
        return add_low(self.held, self.arrived).reshape((2,) + self.shape[1:])


class GatherSmall:
    def __init__(self, values):
        self.values, self.bits = values[None], [2, 4, 1]
        if relative_order():
            self.arrived = swap(self.values, "dp", 2)
        else:
            self.values = self.arrived = lax.all_gather(values, "dp", axis=0)

    def step(self):
        if not relative_order():
            return self.values
        self.values = jnp.concatenate([self.values, self.arrived], 0)
        self.bits = self.bits[1:]
        if self.bits:
            self.arrived = swap(self.values, "dp", self.bits[0])
        return self.values


def sum_everywhere(values):
    for axis in ("dp", "tensor"):
        for bit in bits_of(axis):
            values = values + swap(values, axis, bit)
    return values


def gather_and_sum_videos(values, sums):
    values, count = values[None], sums.shape[0]
    for bit in bits_of("tensor"):
        rows = jnp.concatenate([sums, values.reshape(-1, D)], 0)
        arrived = swap(rows, "tensor", bit)
        sums = sums + arrived[:count]
        values = jnp.concatenate([values, arrived[count:].reshape(values.shape)], 0)
    return values, sums


def adam_step(weight, first_moment, second_moment, gradient, factor, step_rate, decay_rate):
    clipped = gradient * factor
    first_new = beta_one * first_moment + (1.0 - beta_one) * clipped
    second_new = beta_two * second_moment + (1.0 - beta_two) * clipped * clipped
    update = (
        first_new
        / (1.0 - beta_one**STEP)
        / (jnp.sqrt(second_new / (1.0 - beta_two**STEP)) + adam_eps)
    )
    weight_new = weight - step_rate * (update + decay_rate * weight)
    return (first_new, second_new, weight_new)


def on_device(
    tokens,
    cotangent,
    attn_master,
    attn_first,
    attn_second,
    attn_ema,
    mlp_master,
    mlp_first,
    mlp_second,
    mlp_ema,
    msg_master,
    msg_first,
    msg_second,
    msg_ema,
    vec_master,
    vec_first,
    vec_second,
    vec_ema,
):
    z_index = lax.axis_index("tensor")
    z_count = lax.axis_size("tensor")
    dp_index = lax.axis_index("dp")
    part = attn_master.shape[0]
    local_width = attn_master.shape[2]
    local_ff = mlp_master.shape[2]
    frames = tokens.shape[0] // PATCHES
    half_ff = local_ff // 2
    info = make_info()

    class_own = jnp.concatenate(
        [tokens[f * PATCHES : f * PATCHES + 1] for f in range(frames)], 0
    ).reshape(-1, local_width)
    attn_low = jnp.swapaxes(attn_master, 0, 1).astype(bf16).reshape(4 * part, local_width)
    attn_rows = pad_rows(jnp.concatenate([attn_low, class_own], 0), 4 * part + 16)
    attn_z = lax.all_gather(attn_rows, "tensor", axis=0)
    mlp_z = lax.all_gather(jnp.swapaxes(mlp_master, 0, 1).astype(bf16), "tensor", axis=0)
    class_rows = attn_z[:, 4 * part : 4 * part + class_own.shape[0]].reshape(FRAMES, D)
    attn_z = attn_z[:, : 4 * part].reshape(z_count, 4, part, local_width)

    msg_low = jnp.swapaxes(msg_master, 0, 1).astype(bf16).reshape(5 * part, D)
    vec_count = vec_master.shape[1]
    vec_low = jnp.pad(vec_master.astype(bf16).T, ((0, 32 - vec_count), (0, D // 2 - part)))
    msg_go = Gather(jnp.concatenate([msg_low[:, : D // 2], vec_low], 0), msg_low[:, D // 2 :])
    prepared = prepare(info, tokens, cotangent)
    x, grads, grads_t, grad_sum = beside(prepared, msg_go)
    sent_msg = msg_go.step()
    attn_z = after(attn_z, *sent_msg)
    attn_go = Gather(attn_z[:, :2], attn_z[:, 2:])
    sent_attn = attn_go.step()
    beside(sent_attn, msg_go)
    sent_msg = msg_go.step()
    mlp_z = after(mlp_z, *sent_msg)
    mlp_go = [
        Gather(*[mlp_z[:, i, :, j * half_ff : (j + 1) * half_ff] for i in range(2)])
        for j in range(2)
    ]
    msg_w = msg_go.result()
    vec_rel = jnp.concatenate(msg_w[:4], 0)[:, 5 * part : 5 * part + vec_count, :part]
    vec_rel = jnp.moveaxis(vec_rel, 0, 1).reshape(-1, D).astype(f32)
    vectors = plain_order(info, vec_rel)
    ff_bias = vectors[14:].reshape(z_count, 2, half_ff)

    sent_mlp = mlp_go[0].own + mlp_go[1].own
    message, first_msg, msg_pack = beside(
        message_forward(info, after(class_rows, *sent_mlp).astype(f32), vectors, msg_w), attn_go
    )
    attn_go.step()
    attn_w = attn_go.result()
    projected = project(info, x, message, vec_rel, vectors, attn_w)
    queries, key_rows, value_rows, normed_t = beside(projected, *mlp_go)
    sent_mlp = mlp_go[0].step() + mlp_go[1].step()
    attended, totals = beside(
        attend_forward(after(queries, *sent_mlp), key_rows, value_rows), mlp_go[0]
    )
    sent_mlp = mlp_go[0].step()
    middle, n2, n2_t = beside(
        combine(info, x, after(attended, *sent_mlp), vec_rel, attn_w), mlp_go[1]
    )
    sent_mlp = mlp_go[1].step()
    n2 = after(n2, *sent_mlp)

    def feed(j, n2):
        return feed_forward(n2, n2_t, grads, grads_t, ff_bias[:, j], mlp_go[j].result())

    out_0, dn2_0, *dw_0, db_0 = beside(feed(0, n2), mlp_go[1])
    sums_0 = Scatter(dw_0[::2], dw_0[1::2])
    out_1, dn2_1, *dw_1, db_1 = beside(feed(1, after(n2, db_0)), sums_0)
    sums_1 = Scatter(dw_1[::2], dw_1[1::2])
    going = sums_0.step()
    dmid, grad_attended, *grad_out_w, sums_two = beside(
        between(info, after(dn2_0, *going), dn2_1, middle, grads, attended, vec_rel, attn_w), sums_1
    )
    going = sums_1.step()
    pairs = HEADS // 2
    back = (queries, key_rows, value_rows, totals)
    grad_qkv = beside(
        attend_backward(*back, after(grad_attended, *going), 0, pairs // 2), sums_0
    )
    going = sums_0.step()
    grad_qkv = beside(
        attend_backward(
            *back, after(grad_attended, *going), pairs // 2, pairs - pairs // 2, grad_qkv
        ),
        sums_0,
        sums_1,
    )
    going = sums_1.step()
    mlp_0 = ScatterVideos(info, sums_0)
    dqk_keep, dqk_send, dvo_keep, dvo_send, sum_q, sum_v = beside(
        project_grads(
            info, after(normed_t, mlp_0.going, *going), grad_qkv, grad_out_w, attn_w
        ),
        sums_1,
        mlp_0,
    )
    sums_attn = Scatter([dqk_keep, dvo_keep], [dqk_send, dvo_send])
    going = mlp_0.step()
    mlp_1 = ScatterVideos(info, sums_1)
    block_output = beside(
        finish(
            info,
            [after(middle, going, mlp_1.going), out_0, out_1],
            vec_rel[13:14],
            "block_output",
        ),
        sums_attn,
        mlp_0,
        mlp_1,
    )
    going = sums_attn.step()
    going.append(mlp_1.step())
    mlp_0 = mlp_0.result()
    ing, dmsg, sums_one = beside(
        project_back(info, after(x, mlp_0, *going), message, dmid, vec_rel, grad_qkv, attn_w),
        sums_attn,
        mlp_1,
    )
    going = sums_attn.step()
    mlp_1 = mlp_1.result()

    ff_bias_grad = jnp.stack(
        [db.reshape(z_count, half_ff) for db in (db_0, db_1)], 1
    ).reshape(FF // D, D)
    table = jnp.concatenate([sums_one, sums_two, grad_sum, sum_q, sum_v, ff_bias_grad], 0)
    dmsg = dmsg[:, 0].astype(bf16).astype(f32)
    dmsg, table = beside(
        gather_and_sum_videos(after(dmsg, mlp_1, *going), table), sums_attn
    )
    attn_go = ScatterVideos(info, sums_attn)
    grad_class, sent, sums_msg = beside(
        message_backward(info, after(dmsg, attn_go.going), first_msg, msg_pack, vectors, msg_w),
        attn_go,
    )
    going = attn_go.step()

    plain = plain_order(info, table[:6])
    table = jnp.concatenate([plain[:4], sums_msg, table[6:8], plain[4:], table[8:]], 0)
    sent = jnp.concatenate([msg_pack[:2], sent], 0).astype(bf16).reshape(7 * FRAMES, D)
    sent = jnp.concatenate([class_rows, sent, table.astype(bf16)], 0)
    small = GatherSmall(after(sent, going))
    middle_block = BLOCKS // 2
    input_grad = beside(
        finish(info, [after(ing, small.values)], grad_class, "input_grad", 0, middle_block), small
    )
    rows = small.step()
    input_grad = beside(
        finish(
            info,
            [after(ing, rows)],
            grad_class,
            "input_grad",
            middle_block,
            BLOCKS - middle_block,
            [input_grad],
        ),
        small,
        attn_go,
    )
    small.step()
    attn_grad = attn_go.result()
    everyone = small.step()
    tables = lax.dynamic_slice_in_dim(everyone[:, 8 * FRAMES :], dp_index * part, part, 2)
    vec_grad = jnp.sum(tables.astype(f32), 0).T
    everyone = everyone[:, : 8 * FRAMES].reshape(-1, 8, FRAMES, D)
    everyone = jnp.moveaxis(everyone, 0, 1).reshape(8, -1, D)
    mine = lax.dynamic_slice_in_dim(everyone[:3], dp_index * part, part, 2)
    msg_grad = jnp.stack(
        [
            dot(mine[0], everyone[3], TN),
            dot(mine[1], everyone[4], TN),
            dot(mine[1], everyone[5], TN),
            dot(mine[1], everyone[6], TN),
            dot(mine[2], everyone[7], TN),
        ],
        1,
    )

    attn_grad = jnp.swapaxes(attn_grad.reshape(4, part, local_width), 0, 1).astype(f32)
    mlp_grad = jnp.swapaxes(jnp.concatenate([mlp_0, mlp_1], 2), 0, 1).astype(f32)

    keep_share = (z_index == 0).astype(f32)
    squares = (
        jnp.sum(attn_grad * attn_grad)
        + jnp.sum(mlp_grad * mlp_grad)
        + keep_share * (jnp.sum(msg_grad * msg_grad) + jnp.sum(vec_grad * vec_grad))
    )
    squares = sum_everywhere(jnp.broadcast_to(squares, (8, 128)))[0, 0]
    grad_norm = jnp.sqrt(squares)
    factor = clip_limit / jnp.maximum(grad_norm, clip_limit)

    def update(master, first, second, ema, grad, rate, decay):
        first_new, second_new, weight = adam_step(master, first, second, grad, factor, rate, decay)
        return grad, first_new, second_new, weight, ema_keep * ema + (1.0 - ema_keep) * weight

    return (
        block_output,
        input_grad,
        grad_norm,
        *update(attn_master, attn_first, attn_second, attn_ema, attn_grad, rate_mat, decay_mat),
        *update(mlp_master, mlp_first, mlp_second, mlp_ema, mlp_grad, rate_mat, decay_mat),
        *update(msg_master, msg_first, msg_second, msg_ema, msg_grad, rate_mat, decay_mat),
        *update(vec_master, vec_first, vec_second, vec_ema, vec_grad, rate_vec, 0.0),
    )


def solution(mesh):
    rows = P(("dp", "tensor"), None)
    split = P("dp", None, "tensor")
    copied = P("dp", None, None)
    table = P("dp", None)
    in_specs = (rows,) * 2 + (split,) * 8 + (copied,) * 4 + (table,) * 4
    out_specs = (rows,) * 2 + (P(),) + (split,) * 10 + (copied,) * 5 + (table,) * 5
    return jax.shard_map(
        on_device, mesh=mesh, in_specs=in_specs, out_specs=out_specs, check_vma=False
    )
```

profile of v0, /device:TPU:0, one launch (start us, length us, event | category | flops | bytes accessed | tf_op | source)
XLA Modules:
  0.0 564.0 jit_solution(18282422460549160913)
XLA Ops:
  10.3 2.3 copy.105
  13.1 3.0 collective-permute-start
  16.1 1.5 collective-permute-start.1
  18.2 8.7 %prepare.1 = (bf16[2,592,1024]{2,1,0:T(8,128)(2,1)}, bf16[2,592,1024]{2,1,0:T(8,128)(2,1)}, bf16[1024,1280]{1,0:T(8,128)(2,1)}, f32[1,1024]{1,0:T(1,128)}) custom-call(s32[17]{0:T(128)} %pad_add_fusion.info_ref, bf16[1154,1024]{1,0:T(8,128)(2,1)} %tokens_ref.1, bf16[1154,1024]{1,0:T(8,128)(2,1)} %cot_ref.1), custom_call_target="tpu_custom_call" | custom-call | bytes 762624 | tf_op jit(solution)/shard_map/prepare/pallas_call | solution.py:285
  26.9 5.4 collective-permute-done.1.refs_3_
  35.4 1.5 collective-permute-start.4
  37.4 4.2 all-gather.5.cloned.1.call-done
  43.0 1.5 collective-permute-start.2
  46.0 31.5 %collective-permute-done.2 = bf16[4,2,128,256]{3,2,1,0:T(8,128)(2,1)S(1)} collective-permute-done((bf16[4,2,128,256]{3,2,1,0:T(8,128)(2,1)S(1)}, bf16[4,2,128,256]{3,2,1,0:T(8,128)(2,1)S(1)}, u32[]{:S(2)}, u32[]{:S(2)}) %collective-permute-start.2) | collective-permute-done | bytes 524320 | tf_op jit(solution)/shard_map/ppermute | solution.py:860
  81.3 7.9 %all-gather.7.cloned.1.call-done = bf16[8,128,1024]{2,1,0:T(8,128)(2,1)} async-done(((bf16[2,128,1024]{2,1,0:T(8,128)(2,1)}), bf16[8,128,1024]{2,1,0:T(8,128)(2,1)}) %all-gather.7.cloned.1.call-update) | async-done | bytes 2097168 | tf_op jit(solution)/shard_map/all_gather | solution.py:1149
  89.2 3.1 fusion.32
  94.4 2.2 plain_order.2.vec_ref
  97.2 7.8 %message_forward.1 = (f32[8,1024]{1,0:T(8,128)}, f32[8,1024]{1,0:T(8,128)}, f32[5,8,1024]{2,1,0:T(8,128)}) custom-call(s32[17]{0:T(128)} %pad_add_fusion.info_ref, f32[8,1024]{1,0:T(8,128)} %convert_element_type.102.cls_ref, f32[18,1024]{1,0:T(8,128)} %plain_order.2.vec_ref, bf16[2,672,512]{2,1,0:T(8,128)(2,1)} %copy-done.4, ...), custom_call_target="tpu_custom_call" | custom-call | flops 5242880 | bytes 692736 | tf_op jit(solution)/shard_map/message_forward/pallas_call | solution.py:285
  111.7 1.6 slice_bitcast_fusion.12
  114.2 15.7 %project.1 = (bf16[2,592,1024]{2,1,0:T(8,128)(2,1)}, bf16[2,592,1024]{2,1,0:T(8,128)(2,1)}, bf16[2,592,1024]{2,1,0:T(8,128)(2,1)}, bf16[1024,1280]{1,0:T(8,128)(2,1)}) custom-call(s32[17]{0:T(128)} %pad_add_fusion.info_ref, bf16[2,592,1024]{2,1,0:T(8,128)(2,1)} %get-tuple-element.407.x_ref, f32[8,1024]{1,0:T(8,128)} %get-tuple-element.259.msg_ref, ...), custom_call_target="tpu_custom_call" | custom-call | flops 465567744 | bytes 1297408 | tf_op jit(solution)/shard_map/project/pallas_call | solution.py:285
  141.0 32.8 %attend_forward.1 = (bf16[2,592,1024]{2,1,0:T(8,128)(2,1)S(1)}, f32[2,8,2,592]{3,2,1,0:T(2,128)S(1)}) custom-call(bf16[2,592,1024]{2,1,0:T(8,128)(2,1)S(1)} %copy-done, bf16[2,592,1024]{2,1,0:T(8,128)(2,1)} %get-tuple-element.276.k_ref, bf16[2,592,1024]{2,1,0:T(8,128)(2,1)} %get-tuple-element.277.v_ref), custom_call_target="tpu_custom_call" | custom-call | flops 358875136 | bytes 1212416 | tf_op jit(solution)/shard_map/attend_forward/pallas_call | solution.py:144
  175.7 5.9 %collective-permute-done.22.refs_1_ = bf16[2,4,128,512]{3,2,1,0:T(8,128)(2,1)S(1)} collective-permute-done((bf16[2,4,128,512]{3,2,1,0:T(8,128)(2,1)S(1)}, bf16[2,4,128,512]{3,2,1,0:T(8,128)(2,1)S(1)}, u32[]{:S(2)}, u32[]{:S(2)}) %collective-permute-start.22) | collective-permute-done | bytes 1048608 | tf_op jit(solution)/shard_map/ppermute | solution.py:860
  181.6 10.8 %combine.1 = (f32[2,592,1024]{2,1,0:T(8,128)}, bf16[2,592,1024]{2,1,0:T(8,128)(2,1)}, bf16[1024,1280]{1,0:T(8,128)(2,1)}) custom-call(s32[17]{0:T(128)} %pad_add_fusion.info_ref, bf16[2,592,1024]{2,1,0:T(8,128)(2,1)} %get-tuple-element.407.x_ref, bf16[2,592,1024]{2,1,0:T(8,128)(2,1)} %copy-done.5, f32[1,1024]{1,0:T(1,128)} %get-tuple-element.494.bias_ref, ...), custom_call_target="tpu_custom_call" | custom-call | flops 155189248 | bytes 1184512 | tf_op jit(solution)/shard_map/combine/pallas_call | solution.py:285
  196.2 40.9 %feed_forward.2 = (f32[2,592,1024]{2,1,0:T(8,128)}, f32[2,592,1024]{2,1,0:T(8,128)}, bf16[4,4,128,512]{3,2,1,0:T(8,128)(2,1)}, bf16[4,4,128,512]{3,2,1,0:T(8,128...) custom-call(bf16[2,592,1024]{2,1,0:T(8,128)(2,1)} %get-tuple-element.304.n2_ref, ...), custom_call_target="tpu_custom_call" | custom-call | flops 1862270976 | bytes 2260992 | tf_op jit(solution)/shard_map/feed_forward/pallas_call | solution.py:239
  237.7 40.5 %feed_forward.3 = (f32[2,592,1024]{2,1,0:T(8,128)}, f32[2,592,1024]{2,1,0:T(8,128)}, bf16[4,4,128,512]{3,2,1,0:T(8,128)(2,1)}, bf16[4,4,128,512]{3,2,1,0:T(8,128...) custom-call(bf16[2,592,1024]{2,1,0:T(8,128)(2,1)} %get-tuple-element.304.n2_ref, ...), custom_call_target="tpu_custom_call" | custom-call | flops 1862270976 | bytes 2260992 | tf_op jit(solution)/shard_map/feed_forward/pallas_call | solution.py:239
  279.6 5.5 add.260
  285.1 1.6 collective-permute-start.36
  287.1 18.5 %between.1 = (bf16[2,592,1024]{2,1,0:T(8,128)(2,1)}, bf16[2,592,1024]{2,1,0:T(8,128)(2,1)}, bf16[4,4,128,256]{3,2,1,0:T(8,128)(2,1)}, bf16[4,4,128,256]{3,2,1,0:T(8,128)(2,1)}, f32[3,1024]{1,0:T(4,128)}) custom-call(s32[17]{0:T(128)} %pad_add_fusion.info_ref, f32[2,592,1024]{2,1,0:T(8,128)} %get-tuple-element.326.ea_ref, ...), custom_call_target="tpu_custom_call" | custom-call | flops 310378496 | bytes 1909760 | tf_op jit(solution)/shard_map/between/pallas_call | solution.py:285
  307.0 4.4 add.261
  313.5 23.6 %attend_backward.2 = (bf16[2,592,1024]{2,1,0:T(8,128)(2,1)S(1)}, bf16[2,592,1024]{2,1,0:T(8,128)(2,1)S(1)}, bf16[2,592,1024]{2,1,0:T(8,128)(2,1)}) custom-call(bf16[2,592,1024]{2,1,0:T(8,128)(2,1)} %get-tuple-element.275.q_ref, bf16[2,592,1024]{2,1,0:T(8,128)(2,1)} %get-tuple-element.276.k_ref, bf16[2,592,1024]{2,1,0:T(8,128)(2,1)} %get-tuple-element.277.v_ref, ...), custom_call_target="tpu_custom_call" | custom-call | flops 358875136 | bytes 1212416 | tf_op jit(solution)/shard_map/attend_backward/pallas_call | solution.py:163
  337.2 2.5 add.262
  341.8 23.7 %attend_backward.3 = (bf16[2,592,1024]{2,1,0:T(8,128)(2,1)S(1)}, bf16[2,592,1024]{2,1,0:T(8,128)(2,1)S(1)}, bf16[2,592,1024]{2,1,0:T(8,128)(2,1)}) custom-call(bf16[2,592,1024]{2,1,0:T(8,128)(2,1)} %get-tuple-element.275.q_ref, bf16[2,592,1024]{2,1,0:T(8,128)(2,1)} %get-tuple-element.276.k_ref, ...), custom_call_target="tpu_custom_call", output_to_operand_aliasing={{0}: (5, {}), {1}: (6, {}), {2}: (7, {})} | custom-call | flops 358875136 | bytes 1212416 | tf_op jit(solution)/shard_map/attend_backward/pallas_call | solution.py:163
  366.6 2.8 add.263
  371.0 1.6 collective-permute-start.42
  373.0 3.2 add_and_pair.3
  376.2 1.7 collective-permute-start.44
  378.0 13.9 %project_grads.1 = (bf16[4,4,2,128,256]{4,3,2,1,0:T(8,128)(2,1)}, bf16[4,4,2,128,256]{4,3,2,1,0:T(8,128)(2,1)}, bf16[4,4,2,128,256]{4,3,2,1,0:T(8,128)(2,1)}, bf...) custom-call(s32[17]{0:T(128)} %pad_add_fusion.info_ref, ...), custom_call_target="tpu_custom_call" | custom-call | flops 465567744 | bytes 1274368 | tf_op jit(solution)/shard_map/project_grads/pallas_call | solution.py:285
  392.9 3.2 add_and_pair.4
  396.4 2.7 add_and_single.3
  399.1 2.6 collective-permute-start.47
  401.8 9.9 %block_output.1 = f32[1154,1024]{1,0:T(8,128)} custom-call(s32[17]{0:T(128)} %pad_add_fusion.info_ref, f32[2,592,1024]{2,1,0:T(8,128)} %get-tuple-element.390.mid_ref.refs_0_, f32[2,592,1024]{2,1,0:T(8,128)} %get-tuple-element.391.refs_1_, f32[2,592,1024]{2,1,0:T(8,128)} %get-tuple-element.392.refs_2_, f32[1,1024]{1,0:T(1,128)} %get-tuple-element.491.refs_3_), custom_call_target="tpu_custom_call" | custom-call | bytes 1204992 | tf_op jit(solution)/shard_map/block_output/pallas_call | solution.py:285
  411.7 1.8 collective-permute-done.47
  413.5 2.0 collective-permute-done.48.ao_ref.ap_ref
  417.5 4.5 add.264
  422.1 1.6 collective-permute-start.49
  424.2 2.7 add_and_single.4
  429.2 19.1 %project_back.1 = (f32[2,592,1024]{2,1,0:T(8,128)}, f32[2,1,1024]{2,1,0:T(1,128)}, f32[2,1024]{1,0:T(2,128)}) custom-call(s32[17]{0:T(128)} %pad_add_fusion.info_ref, bf16[2,592,1024]{2,1,0:T(8,128)(2,1)} %get-tuple-element.407.x_ref, f32[8,1024]{1,0:T(8,128)} %get-tuple-element.259.msg_ref, bf16[2,592,1024]{2,1,0:T(8,128)(2,1)} %get-tuple-element.408.dmid_ref, ...), custom_call_target="tpu_custom_call" | custom-call | flops 465567744 | bytes 1588480 | tf_op jit(solution)/shard_map/project_back/pallas_call | solution.py:285
  449.3 2.5 add.265
  453.5 1.8 collective-permute-start.52
  457.9 2.3 collective-permute-start.53
  460.2 3.0 collective-permute-done.53
  463.9 3.2 collective-permute-done.54
  469.0 3.4 add_and_pair.5
  474.4 2.0 plain_order.3
  477.2 9.1 %message_backward.1 = (f32[8,1024]{1,0:T(8,128)}, f32[5,8,1024]{2,1,0:T(8,128)}, f32[6,1024]{1,0:T(8,128)}) custom-call(s32[17]{0:T(128)} %pad_add_fusion.info_ref, f32[4,2,1024]{2,1,0:T(2,128)} %pad_maximum_fusion.7.dmsg_ref, f32[8,1024]{1,0:T(8,128)} %get-tuple-element.437.first_ref, f32[5,8,1024]{2,1,0:T(8,128)} %get-tuple-element.413.pack_ref, ...), custom_call_target="tpu_custom_call" | custom-call | flops 5242880 | bytes 704512 | tf_op jit(solution)/shard_map/message_backward/pallas_call | solution.py:285
  488.3 2.7 add_and_single.5
  491.8 4.6 input_grad.2.refs_2_
  497.9 2.0 collective-permute-start.59
  500.0 4.6 input_grad.3
  504.5 3.8 collective-permute-done.59
  509.6 2.6 multiply_reduce_fusion.1
  522.9 2.9 collective-permute-done.62
  526.7 2.7 collective-permute-done.63
  529.6 3.4 collective-permute-done.64
  533.0 1.5 collective-permute-start.65
  534.5 3.0 collective-permute-done.65
  538.9 7.9 %multiply_add_fusion = (f32[128,5,1024]{2,0,1:T(8,128)}, f32[128,5,1024]{2,0,1:T(8,128)}, f32[128,5,1024]{2,0,1:T(8,128)}, f32[128,5,1024]{2,0,1:T(8,128)}) fusion(f32[128,5,1024]{2,0,1:T(8,128)} %param.31, f32[128,5,1024]{2,0,1:T(8,128)} %param.28, f32[128,5,1024]{2,0,1:T(8,128)S(1)} %fusion.2, f32[]{:T(128)S(6)} %div.81, f32[128,5,1024]{2,0,1:T(8,128)} %param.30, ...), kind=kLoop, calls=%fused_computation.2 | loop fusion | flops 12451840 | bytes 23592964 | tf_op jit(solution)/shard_map/add | solution.py:1326
  547.6 2.3 multiply_add_fusion.4
  549.9 5.7 %multiply_add_fusion.2 = (f32[128,2,1024]{2,1,0:T(2,128)}, f32[128,2,1024]{2,1,0:T(2,128)}, f32[128,2,1024]{2,1,0:T(2,128)}, f32[128,2,1024]{2,1,0:T(2,128)}) fusion(f32[128,2,1024]{2,1,0:T(2,128)S(1)} %copy-done.45, f32[128,2,1024]{2,1,0:T(2,128)S(1)} %copy-done.28, f32[128,2,1024]{2,1,0:T(2,128)S(1)} %copy-done.29, f32[]{:T(128)S(6)} %div.81, ...), kind=kLoop, calls=%fused_computation.24 | loop fusion | flops 4980736 | bytes 9437188 | tf_op jit(solution)/shard_map/add | solution.py:1326
  (358 shorter events, 84.8 us)
Async XLA Ops:
  7.2 34.4 %all-gather.5.cloned.1.call-start = ((), (), s32[]{:S(2)}) async-start(), calls=%async_computation | async-start | bytes 1351680 | tf_op jit(solution)/shard_map/all_gather | solution.py:1148
  10.3 78.9 %all-gather.7.cloned.1.call-start = ((), (), s32[]{:S(2)}) async-start(), calls=%async_computation.1 | async-start | bytes 2621440 | tf_op jit(solution)/shard_map/all_gather | solution.py:1149
  13.1 20.0 %collective-permute-start = (bf16[672,512]{1,0:T(8,128)(2,1)S(1)}, bf16[672,512]{1,0:T(8,128)(2,1)S(1)}, u32[]{:S(2)}, u32[]{:S(2)}) collective-permute-start(bf16[672,512]{1,0:T(8,128)(2,1)S(1)} %fusion.8.refs_0_), channel_id=1, source_target_pairs={{0,8},{4,12},{8,0},{12,4},{16,24},{20,28},{24,16},{28,20},{1,9},{5... | collective-permute-start | bytes 2064392 | tf_op jit(solution)/shard_map/ppermute | solution.py:860
  16.1 16.2 %collective-permute-start.1 = (bf16[640,512]{1,0:T(8,128)(2,1)S(1)}, bf16[640,512]{1,0:T(8,128)(2,1)S(1)}, u32[]{:S(2)}, u32[]{:S(2)}) collective-permute-start(bf16[640,512]{1,0:T(8,128)(2,1)S(1)} %get-tuple-element.487.refs_2_), channel_id=1, source_target_pairs={{0,16},{4,20},{8,24},{12,28},{16,0},{20,4},{24,8},{28,12},{1,17},{... | collective-permute-start | bytes 1966088 | tf_op jit(solution)/shard_map/ppermute | solution.py:860
  35.4 42.5 %collective-permute-start.4 = (bf16[2,672,512]{2,1,0:T(8,128)(2,1)S(1)}, bf16[2,672,512]{2,1,0:T(8,128)(2,1)}, u32[]{:S(2)}, u32[]{:S(2)}) collective-permute-start(bf16[2,672,512]{2,1,0:T(8,128)(2,1)S(1)} %get-tuple-element.247.refs_0_), channel_id=1, source_target_pairs={{0,16},{4,20},{8,24},{12,28},{16,0},{20,4},{24,8},{28,12},{1,17},{... | collective-permute-start | bytes 4128776 | tf_op jit(solution)/shard_map/ppermute | solution.py:860
  36.9 40.9 %collective-permute-start.5 = (bf16[2,640,512]{2,1,0:T(8,128)(2,1)}, bf16[2,640,512]{2,1,0:T(8,128)(2,1)}, u32[]{:S(2)}, u32[]{:S(2)}) collective-permute-start(bf16[2,640,512]{2,1,0:T(8,128)(2,1)} %get-tuple-element.248.refs_4_), channel_id=1, source_target_pairs={{0,8},{4,12},{8,0},{12,4},{16,24},{20,28},{24,16},{28,20},{1,9},{5... | collective-permute-start | bytes 3932168 | tf_op jit(solution)/shard_map/ppermute | solution.py:860
  37.4 42.5 %collective-permute-start.6 = (bf16[2,672,512]{2,1,0:T(8,128)(2,1)S(1)}, bf16[2,672,512]{2,1,0:T(8,128)(2,1)}, u32[]{:S(2)}, u32[]{:S(2)}) collective-permute-start(bf16[2,672,512]{2,1,0:T(8,128)(2,1)S(1)} %get-tuple-element.247.refs_0_), channel_id=1, source_target_pairs={{0,4},{4,0},{8,12},{12,8},{16,20},{20,16},{24,28},{28,24},{1,5},{5... | collective-permute-start | bytes 4128776 | tf_op jit(solution)/shard_map/ppermute | solution.py:860
  43.0 34.5 %collective-permute-start.2 = (bf16[4,2,128,256]{3,2,1,0:T(8,128)(2,1)S(1)}, bf16[4,2,128,256]{3,2,1,0:T(8,128)(2,1)S(1)}, u32[]{:S(2)}, u32[]{:S(2)}) collective-permute-start(bf16[4,2,128,256]{3,2,1,0:T(8,128)(2,1)S(1)} %get-tuple-element.490), channel_id=1, source_target_pairs={{0,8},{4,12},{8,0},{12,4},{16,24},{20,28},{24,16},{28,20},{1,9},{5... | collective-permute-start | bytes 1572872 | tf_op jit(solution)/shard_map/ppermute | solution.py:860
  44.5 33.0 %collective-permute-start.3 = (bf16[4,2,128,256]{3,2,1,0:T(8,128)(2,1)S(1)}, bf16[4,2,128,256]{3,2,1,0:T(8,128)(2,1)S(1)}, u32[]{:S(2)}, u32[]{:S(2)}) collective-permute-start(bf16[4,2,128,256]{3,2,1,0:T(8,128)(2,1)S(1)} %get-tuple-element.489), channel_id=1, source_target_pairs={{0,16},{4,20},{8,24},{12,28},{16,0},{20,4},{24,8},{28,12},{1,17},{... | collective-permute-start | bytes 1572872 | tf_op jit(solution)/shard_map/ppermute | solution.py:860
  77.9 15.1 %collective-permute-start.7 = (bf16[2,672,512]{2,1,0:T(8,128)(2,1)}, bf16[2,672,512]{2,1,0:T(8,128)(2,1)}, u32[]{:S(2)}, u32[]{:S(2)}) collective-permute-start(bf16[2,672,512]{2,1,0:T(8,128)(2,1)} %collective-permute-done.4.refs_1_), channel_id=1, source_target_pairs={{0,4},{4,0},{8,12},{12,8},{16,20},{20,16},{24,28},{28,24},{1,5},{5... | collective-permute-start | bytes 4128776 | tf_op jit(solution)/shard_map/ppermute | solution.py:860
  77.9 18.7 %collective-permute-start.8 = (bf16[2,640,512]{2,1,0:T(8,128)(2,1)}, bf16[2,640,512]{2,1,0:T(8,128)(2,1)}, u32[]{:S(2)}, u32[]{:S(2)}) collective-permute-start(bf16[2,640,512]{2,1,0:T(8,128)(2,1)} %get-tuple-element.248.refs_4_), channel_id=1, source_target_pairs={{0,4},{4,0},{8,12},{12,8},{16,20},{20,16},{24,28},{28,24},{1,5},{5... | collective-permute-start | bytes 3932168 | tf_op jit(solution)/shard_map/ppermute | solution.py:860
  78.4 18.8 %collective-permute-start.9 = (bf16[2,640,512]{2,1,0:T(8,128)(2,1)}, bf16[2,640,512]{2,1,0:T(8,128)(2,1)}, u32[]{:S(2)}, u32[]{:S(2)}) collective-permute-start(bf16[2,640,512]{2,1,0:T(8,128)(2,1)} %collective-permute-done.5.refs_5_), channel_id=1, source_target_pairs={{0,4},{4,0},{8,12},{12,8},{16,20},{20,16},{24,28},{28,24},{1,5},{5... | collective-permute-start | bytes 3932168 | tf_op jit(solution)/shard_map/ppermute | solution.py:860
  78.5 26.5 %collective-permute-start.10 = (bf16[2,4,2,128,256]{4,3,2,1,0:T(8,128)(2,1)S(1)}, bf16[2,4,2,128,256]{4,3,2,1,0:T(8,128)(2,1)}, u32[]{:S(2)}, u32[]{:S(2)}) collective-permute-start(bf16[2,4,2,128,256]{4,3,2,1,0:T(8,128)(2,1)S(1)} %bitcast.169), channel_id=1, source_target_pairs={{0,16},{4,20},{8,24},{12,28},{16,0},{20,4},{24,8},{28,12},{1,17},{... | collective-permute-start | bytes 3145736 | tf_op jit(solution)/shard_map/ppermute | solution.py:860
  80.0 25.3 %collective-permute-start.11 = (bf16[2,4,2,128,256]{4,3,2,1,0:T(8,128)(2,1)S(1)}, bf16[2,4,2,128,256]{4,3,2,1,0:T(8,128)(2,1)}, u32[]{:S(2)}, u32[]{:S(2)}) collective-permute-start(bf16[2,4,2,128,256]{4,3,2,1,0:T(8,128)(2,1)S(1)} %bitcast.163), channel_id=1, source_target_pairs={{0,8},{4,12},{8,0},{12,4},{16,24},{20,28},{24,16},{28,20},{1,9},{5... | collective-permute-start | bytes 3145736 | tf_op jit(solution)/shard_map/ppermute | solution.py:860
  92.9 14.1 %collective-permute-start.12 = (bf16[2,4,2,128,256]{4,3,2,1,0:T(8,128)(2,1)S(1)}, bf16[2,4,2,128,256]{4,3,2,1,0:T(8,128)(2,1)}, u32[]{:S(2)}, u32[]{:S(2)}) collective-permute-start(bf16[2,4,2,128,256]{4,3,2,1,0:T(8,128)(2,1)S(1)} %bitcast.170), channel_id=1, source_target_pairs={{0,4},{4,0},{8,12},{12,8},{16,20},{20,16},{24,28},{28,24},{1,5},{5... | collective-permute-start | bytes 3145736 | tf_op jit(solution)/shard_map/ppermute | solution.py:860
  96.6 11.9 %collective-permute-start.14 = (bf16[2,4,2,128,256]{4,3,2,1,0:T(8,128)(2,1)S(1)}, bf16[2,4,2,128,256]{4,3,2,1,0:T(8,128)(2,1)S(1)}, u32[]{:S(2)}, u32[]{:S(2)}) collective-permute-start(bf16[2,4,2,128,256]{4,3,2,1,0:T(8,128)(2,1)S(1)} %bitcast.164), channel_id=1, source_target_pairs={{0,4},{4,0},{8,12},{12,8},{16,20},{20,16},{24,28},{28,24},{1,5},{5... | collective-permute-start | bytes 3145736 | tf_op jit(solution)/shard_map/ppermute | solution.py:860
  105.3 4.5 collective-permute-start.13
  105.3 7.9 %collective-permute-start.15 = (bf16[2,4,2,128,256]{4,3,2,1,0:T(8,128)(2,1)}, bf16[2,4,2,128,256]{4,3,2,1,0:T(8,128)(2,1)S(1)}, u32[]{:S(2)}, u32[]{:S(2)}) collective-permute-start(bf16[2,4,2,128,256]{4,3,2,1,0:T(8,128)(2,1)} %collective-permute-done.11.refs_5_.refs_1_), channel_id=1, source_target_pairs={{0,4},{4,0},{8,12},{12,8},{16,20},{20,16},{24,28},{28,24},{1,5},{5... | collective-permute-start | bytes 3145736 | tf_op jit(solution)/shard_map/ppermute | solution.py:860
  105.8 24.1 %collective-permute-start.16 = (bf16[4,128,512]{2,1,0:T(8,128)(2,1)}, bf16[4,128,512]{2,1,0:T(8,128)(2,1)S(1)}, u32[]{:S(2)}, u32[]{:S(2)}) collective-permute-start(bf16[4,128,512]{2,1,0:T(8,128)(2,1)} %get-tuple-element.480), channel_id=1, source_target_pairs={{0,8},{4,12},{8,0},{12,4},{16,24},{20,28},{24,16},{28,20},{1,9},{5... | collective-permute-start | bytes 1572872 | tf_op jit(solution)/shard_map/ppermute | solution.py:860
  107.1 23.7 %collective-permute-start.17 = (bf16[4,128,512]{2,1,0:T(8,128)(2,1)}, bf16[4,128,512]{2,1,0:T(8,128)(2,1)S(1)}, u32[]{:S(2)}, u32[]{:S(2)}) collective-permute-start(bf16[4,128,512]{2,1,0:T(8,128)(2,1)} %get-tuple-element.481), channel_id=1, source_target_pairs={{0,16},{4,20},{8,24},{12,28},{16,0},{20,4},{24,8},{28,12},{1,17},{... | collective-permute-start | bytes 1572872 | tf_op jit(solution)/shard_map/ppermute | solution.py:860
  108.5 23.0 %collective-permute-start.18 = (bf16[4,128,512]{2,1,0:T(8,128)(2,1)}, bf16[4,128,512]{2,1,0:T(8,128)(2,1)S(1)}, u32[]{:S(2)}, u32[]{:S(2)}) collective-permute-start(bf16[4,128,512]{2,1,0:T(8,128)(2,1)} %get-tuple-element.482), channel_id=1, source_target_pairs={{0,8},{4,12},{8,0},{12,4},{16,24},{20,28},{24,16},{28,20},{1,9},{5... | collective-permute-start | bytes 1572872 | tf_op jit(solution)/shard_map/ppermute | solution.py:860
  109.8 22.3 %collective-permute-start.19 = (bf16[4,128,512]{2,1,0:T(8,128)(2,1)}, bf16[4,128,512]{2,1,0:T(8,128)(2,1)S(1)}, u32[]{:S(2)}, u32[]{:S(2)}) collective-permute-start(bf16[4,128,512]{2,1,0:T(8,128)(2,1)} %get-tuple-element.483), channel_id=1, source_target_pairs={{0,16},{4,20},{8,24},{12,28},{16,0},{20,4},{24,8},{28,12},{1,17},{... | collective-permute-start | bytes 1572872 | tf_op jit(solution)/shard_map/ppermute | solution.py:860
  134.7 40.5 %collective-permute-start.20 = (bf16[2,4,128,512]{3,2,1,0:T(8,128)(2,1)S(1)}, bf16[2,4,128,512]{3,2,1,0:T(8,128)(2,1)}, u32[]{:S(2)}, u32[]{:S(2)}) collective-permute-start(bf16[2,4,128,512]{3,2,1,0:T(8,128)(2,1)S(1)} %bitcast.194), channel_id=1, source_target_pairs={{0,16},{4,20},{8,24},{12,28},{16,0},{20,4},{24,8},{28,12},{1,17},{... | collective-permute-start | bytes 3145736 | tf_op jit(solution)/shard_map/ppermute | solution.py:860
  136.3 39.2 %collective-permute-start.21 = (bf16[2,4,128,512]{3,2,1,0:T(8,128)(2,1)S(1)}, bf16[2,4,128,512]{3,2,1,0:T(8,128)(2,1)}, u32[]{:S(2)}, u32[]{:S(2)}) collective-permute-start(bf16[2,4,128,512]{3,2,1,0:T(8,128)(2,1)S(1)} %bitcast.197), channel_id=1, source_target_pairs={{0,8},{4,12},{8,0},{12,4},{16,24},{20,28},{24,16},{28,20},{1,9},{5... | collective-permute-start | bytes 3145736 | tf_op jit(solution)/shard_map/ppermute | solution.py:860
  139.0 42.6 %collective-permute-start.22 = (bf16[2,4,128,512]{3,2,1,0:T(8,128)(2,1)S(1)}, bf16[2,4,128,512]{3,2,1,0:T(8,128)(2,1)S(1)}, u32[]{:S(2)}, u32[]{:S(2)}) collective-permute-start(bf16[2,4,128,512]{3,2,1,0:T(8,128)(2,1)S(1)} %bitcast.191), channel_id=1, source_target_pairs={{0,16},{4,20},{8,24},{12,28},{16,0},{20,4},{24,8},{28,12},{1,17},{... | collective-permute-start | bytes 3145736 | tf_op jit(solution)/shard_map/ppermute | solution.py:860
  139.8 53.2 %collective-permute-start.24 = (bf16[2,4,128,512]{3,2,1,0:T(8,128)(2,1)S(1)}, bf16[2,4,128,512]{3,2,1,0:T(8,128)(2,1)S(1)}, u32[]{:S(2)}, u32[]{:S(2)}) collective-permute-start(bf16[2,4,128,512]{3,2,1,0:T(8,128)(2,1)S(1)} %bitcast.195), channel_id=1, source_target_pairs={{0,4},{4,0},{8,12},{12,8},{16,20},{20,16},{24,28},{28,24},{1,5},{5... | collective-permute-start | bytes 3145736 | tf_op jit(solution)/shard_map/ppermute | solution.py:860
  139.8 52.6 %collective-permute-start.23 = (bf16[2,4,128,512]{3,2,1,0:T(8,128)(2,1)}, bf16[2,4,128,512]{3,2,1,0:T(8,128)(2,1)S(1)}, u32[]{:S(2)}, u32[]{:S(2)}) collective-permute-start(bf16[2,4,128,512]{3,2,1,0:T(8,128)(2,1)} %bitcast.35.refs_4_), channel_id=1, source_target_pairs={{0,8},{4,12},{8,0},{12,4},{16,24},{20,28},{24,16},{28,20},{1,9},{5... | collective-permute-start | bytes 3145736 | tf_op jit(solution)/shard_map/ppermute | solution.py:860
  175.2 17.9 %collective-permute-start.26 = (bf16[2,4,128,512]{3,2,1,0:T(8,128)(2,1)S(1)}, bf16[2,4,128,512]{3,2,1,0:T(8,128)(2,1)S(1)}, u32[]{:S(2)}, u32[]{:S(2)}) collective-permute-start(bf16[2,4,128,512]{3,2,1,0:T(8,128)(2,1)S(1)} %bitcast.198), channel_id=1, source_target_pairs={{0,4},{4,0},{8,12},{12,8},{16,20},{20,16},{24,28},{28,24},{1,5},{5... | collective-permute-start | bytes 3145736 | tf_op jit(solution)/shard_map/ppermute | solution.py:860
  175.4 18.6 %collective-permute-start.25 = (bf16[2,4,128,512]{3,2,1,0:T(8,128)(2,1)}, bf16[2,4,128,512]{3,2,1,0:T(8,128)(2,1)}, u32[]{:S(2)}, u32[]{:S(2)}) collective-permute-start(bf16[2,4,128,512]{3,2,1,0:T(8,128)(2,1)} %collective-permute-done.20.refs_1_), channel_id=1, source_target_pairs={{0,4},{4,0},{8,12},{12,8},{16,20},{20,16},{24,28},{28,24},{1,5},{5... | collective-permute-start | bytes 3145736 | tf_op jit(solution)/shard_map/ppermute | solution.py:860
  181.6 14.6 %collective-permute-start.27 = (bf16[2,4,128,512]{3,2,1,0:T(8,128)(2,1)}, bf16[2,4,128,512]{3,2,1,0:T(8,128)(2,1)}, u32[]{:S(2)}, u32[]{:S(2)}) collective-permute-start(bf16[2,4,128,512]{3,2,1,0:T(8,128)(2,1)} %collective-permute-done.21.refs_5_), channel_id=1, source_target_pairs={{0,4},{4,0},{8,12},{12,8},{16,20},{20,16},{24,28},{28,24},{1,5},{5... | collective-permute-start | bytes 3145736 | tf_op jit(solution)/shard_map/ppermute | solution.py:860
  192.4 44.7 %collective-permute-start.28 = (bf16[2,4,128,512]{3,2,1,0:T(8,128)(2,1)S(1)}, bf16[2,4,128,512]{3,2,1,0:T(8,128)(2,1)}, u32[]{:S(2)}, u32[]{:S(2)}) collective-permute-start(bf16[2,4,128,512]{3,2,1,0:T(8,128)(2,1)S(1)} %bitcast.192), channel_id=1, source_target_pairs={{0,4},{4,0},{8,12},{12,8},{16,20},{20,16},{24,28},{28,24},{1,5},{5... | collective-permute-start | bytes 3145736 | tf_op jit(solution)/shard_map/ppermute | solution.py:860
  193.0 44.1 %collective-permute-start.30 = (bf16[2,4,128,512]{3,2,1,0:T(8,128)(2,1)}, bf16[2,4,128,512]{3,2,1,0:T(8,128)(2,1)}, u32[]{:S(2)}, u32[]{:S(2)}) collective-permute-start(bf16[2,4,128,512]{3,2,1,0:T(8,128)(2,1)} %bitcast.35.refs_4_), channel_id=1, source_target_pairs={{0,4},{4,0},{8,12},{12,8},{16,20},{20,16},{24,28},{28,24},{1,5},{5... | collective-permute-start | bytes 3145736 | tf_op jit(solution)/shard_map/ppermute | solution.py:860
  193.1 44.0 %collective-permute-start.29 = (bf16[2,4,128,512]{3,2,1,0:T(8,128)(2,1)S(1)}, bf16[2,4,128,512]{3,2,1,0:T(8,128)(2,1)}, u32[]{:S(2)}, u32[]{:S(2)}) collective-permute-start(bf16[2,4,128,512]{3,2,1,0:T(8,128)(2,1)S(1)} %collective-permute-done.22.refs_1_), channel_id=1, source_target_pairs={{0,4},{4,0},{8,12},{12,8},{16,20},{20,16},{24,28},{28,24},{1,5},{5... | collective-permute-start | bytes 3145736 | tf_op jit(solution)/shard_map/ppermute | solution.py:860
  194.4 42.7 %collective-permute-start.31 = (bf16[2,4,128,512]{3,2,1,0:T(8,128)(2,1)S(1)}, bf16[2,4,128,512]{3,2,1,0:T(8,128)(2,1)}, u32[]{:S(2)}, u32[]{:S(2)}) collective-permute-start(bf16[2,4,128,512]{3,2,1,0:T(8,128)(2,1)S(1)} %collective-permute-done.23.refs_5_), channel_id=1, source_target_pairs={{0,4},{4,0},{8,12},{12,8},{16,20},{20,16},{24,28},{28,24},{1,5},{5... | collective-permute-start | bytes 3145736 | tf_op jit(solution)/shard_map/ppermute | solution.py:860
  237.1 41.1 %collective-permute-start.32 = (bf16[4,4,128,512]{3,2,1,0:T(8,128)(2,1)}, bf16[4,4,128,512]{3,2,1,0:T(8,128)(2,1)S(1)}, u32[]{:S(2)}, u32[]{:S(2)}) collective-permute-start(bf16[4,4,128,512]{3,2,1,0:T(8,128)(2,1)} %get-tuple-element.316), channel_id=1, source_target_pairs={{0,4},{4,0},{8,12},{12,8},{16,20},{20,16},{24,28},{28,24},{1,5},{5... | collective-permute-start | bytes 6291464 | tf_op jit(solution)/shard_map/ppermute | solution.py:860
  237.4 40.9 %collective-permute-start.33 = (bf16[4,4,128,512]{3,2,1,0:T(8,128)(2,1)}, bf16[4,4,128,512]{3,2,1,0:T(8,128)(2,1)}, u32[]{:S(2)}, u32[]{:S(2)}) collective-permute-start(bf16[4,4,128,512]{3,2,1,0:T(8,128)(2,1)} %get-tuple-element.317), channel_id=1, source_target_pairs={{0,4},{4,0},{8,12},{12,8},{16,20},{20,16},{24,28},{28,24},{1,5},{5... | collective-permute-start | bytes 6291464 | tf_op jit(solution)/shard_map/ppermute | solution.py:860
  278.3 27.4 %collective-permute-start.34 = (bf16[4,4,128,512]{3,2,1,0:T(8,128)(2,1)}, bf16[4,4,128,512]{3,2,1,0:T(8,128)(2,1)S(1)}, u32[]{:S(2)}, u32[]{:S(2)}) collective-permute-start(bf16[4,4,128,512]{3,2,1,0:T(8,128)(2,1)} %get-tuple-element.333), channel_id=1, source_target_pairs={{0,4},{4,0},{8,12},{12,8},{16,20},{20,16},{24,28},{28,24},{1,5},{5... | collective-permute-start | bytes 6291464 | tf_op jit(solution)/shard_map/ppermute | solution.py:860
  278.6 27.1 %collective-permute-start.35 = (bf16[4,4,128,512]{3,2,1,0:T(8,128)(2,1)}, bf16[4,4,128,512]{3,2,1,0:T(8,128)(2,1)}, u32[]{:S(2)}, u32[]{:S(2)}) collective-permute-start(bf16[4,4,128,512]{3,2,1,0:T(8,128)(2,1)} %get-tuple-element.334), channel_id=1, source_target_pairs={{0,4},{4,0},{8,12},{12,8},{16,20},{20,16},{24,28},{28,24},{1,5},{5... | collective-permute-start | bytes 6291464 | tf_op jit(solution)/shard_map/ppermute | solution.py:860
  285.1 52.0 %collective-permute-start.36 = (bf16[2,512,512]{2,1,0:T(8,128)(2,1)}, bf16[2,512,512]{2,1,0:T(8,128)(2,1)S(1)}, u32[]{:S(2)}, u32[]{:S(2)}) collective-permute-start(bf16[2,512,512]{2,1,0:T(8,128)(2,1)} %get-tuple-element.324), channel_id=1, source_target_pairs={{0,16},{4,20},{8,24},{12,28},{16,0},{20,4},{24,8},{28,12},{1,17},{... | collective-permute-start | bytes 3145736 | tf_op jit(solution)/shard_map/ppermute | solution.py:860
  286.7 50.5 %collective-permute-start.37 = (bf16[2,512,512]{2,1,0:T(8,128)(2,1)}, bf16[2,512,512]{2,1,0:T(8,128)(2,1)}, u32[]{:S(2)}, u32[]{:S(2)}) collective-permute-start(bf16[2,512,512]{2,1,0:T(8,128)(2,1)} %get-tuple-element.325), channel_id=1, source_target_pairs={{0,8},{4,12},{8,0},{12,4},{16,24},{20,28},{24,16},{28,20},{1,9},{5... | collective-permute-start | bytes 3145736 | tf_op jit(solution)/shard_map/ppermute | solution.py:860
  311.4 54.1 %collective-permute-start.40 = (bf16[2,512,512]{2,1,0:T(8,128)(2,1)S(1)}, bf16[2,512,512]{2,1,0:T(8,128)(2,1)S(1)}, u32[]{:S(2)}, u32[]{:S(2)}) collective-permute-start(bf16[2,512,512]{2,1,0:T(8,128)(2,1)S(1)} %get-tuple-element.340), channel_id=1, source_target_pairs={{0,16},{4,20},{8,24},{12,28},{16,0},{20,4},{24,8},{28,12},{1,17},{... | collective-permute-start | bytes 3145736 | tf_op jit(solution)/shard_map/ppermute | solution.py:860
  312.9 52.6 %collective-permute-start.41 = (bf16[2,512,512]{2,1,0:T(8,128)(2,1)S(1)}, bf16[2,512,512]{2,1,0:T(8,128)(2,1)S(1)}, u32[]{:S(2)}, u32[]{:S(2)}) collective-permute-start(bf16[2,512,512]{2,1,0:T(8,128)(2,1)S(1)} %get-tuple-element.341), channel_id=1, source_target_pairs={{0,8},{4,12},{8,0},{12,4},{16,24},{20,28},{24,16},{28,20},{1,9},{5... | collective-permute-start | bytes 3145736 | tf_op jit(solution)/shard_map/ppermute | solution.py:860
  339.7 25.8 %collective-permute-start.38 = (bf16[512,512]{1,0:T(8,128)(2,1)S(1)}, bf16[512,512]{1,0:T(8,128)(2,1)S(1)}, u32[]{:S(2)}, u32[]{:S(2)}) collective-permute-start(bf16[512,512]{1,0:T(8,128)(2,1)S(1)} %get-tuple-element.350), channel_id=1, source_target_pairs={{0,8},{4,12},{8,0},{12,4},{16,24},{20,28},{24,16},{28,20},{1,9},{5... | collective-permute-start | bytes 1572872 | tf_op jit(solution)/shard_map/ppermute | solution.py:860
  341.2 24.3 %collective-permute-start.39 = (bf16[512,512]{1,0:T(8,128)(2,1)S(1)}, bf16[512,512]{1,0:T(8,128)(2,1)S(1)}, u32[]{:S(2)}, u32[]{:S(2)}) collective-permute-start(bf16[512,512]{1,0:T(8,128)(2,1)S(1)} %get-tuple-element.351), channel_id=1, source_target_pairs={{0,16},{4,20},{8,24},{12,28},{16,0},{20,4},{24,8},{28,12},{1,17},{... | collective-permute-start | bytes 1572872 | tf_op jit(solution)/shard_map/ppermute | solution.py:860
  371.0 20.9 %collective-permute-start.42 = (bf16[512,512]{1,0:T(8,128)(2,1)S(1)}, bf16[512,512]{1,0:T(8,128)(2,1)S(1)}, u32[]{:S(2)}, u32[]{:S(2)}) collective-permute-start(bf16[512,512]{1,0:T(8,128)(2,1)S(1)} %get-tuple-element.369), channel_id=1, source_target_pairs={{0,8},{4,12},{8,0},{12,4},{16,24},{20,28},{24,16},{28,20},{1,9},{5... | collective-permute-start | bytes 1572872 | tf_op jit(solution)/shard_map/ppermute | solution.py:860
  372.6 19.4 %collective-permute-start.43 = (bf16[512,512]{1,0:T(8,128)(2,1)S(1)}, bf16[512,512]{1,0:T(8,128)(2,1)S(1)}, u32[]{:S(2)}, u32[]{:S(2)}) collective-permute-start(bf16[512,512]{1,0:T(8,128)(2,1)S(1)} %get-tuple-element.370), channel_id=1, source_target_pairs={{0,16},{4,20},{8,24},{12,28},{16,0},{20,4},{24,8},{28,12},{1,17},{... | collective-permute-start | bytes 1572872 | tf_op jit(solution)/shard_map/ppermute | solution.py:860
  376.2 15.7 %collective-permute-start.44 = (bf16[2,256,512]{2,1,0:T(8,128)(2,1)}, bf16[2,256,512]{2,1,0:T(8,128)(2,1)S(1)}, u32[]{:S(2)}, u32[]{:S(2)}) collective-permute-start(bf16[2,256,512]{2,1,0:T(8,128)(2,1)} %get-tuple-element.364), channel_id=1, source_target_pairs={{0,1},{1,0},{2,3},{3,2},{4,5},{5,4},{6,7},{7,6},{8,9},{9,8},{10,11... | collective-permute-start | bytes 1572872 | tf_op jit(solution)/shard_map/ppermute | solution.py:860
  392.0 23.5 %collective-permute-start.45 = (bf16[4,4,2,128,256]{4,3,2,1,0:T(8,128)(2,1)}, bf16[4,4,2,128,256]{4,3,2,1,0:T(8,128)(2,1)S(1)}, u32[]{:S(2)}, u32[]{:S(2)}) collective-permute-start(bf16[4,4,2,128,256]{4,3,2,1,0:T(8,128)(2,1)} %get-tuple-element.393), channel_id=1, source_target_pairs={{0,4},{4,0},{8,12},{12,8},{16,20},{20,16},{24,28},{28,24},{1,5},{5... | collective-permute-start | bytes 6291464 | tf_op jit(solution)/shard_map/ppermute | solution.py:860
  392.0 23.5 %collective-permute-start.46 = (bf16[4,4,2,128,256]{4,3,2,1,0:T(8,128)(2,1)}, bf16[4,4,2,128,256]{4,3,2,1,0:T(8,128)(2,1)S(1)}, u32[]{:S(2)}, u32[]{:S(2)}) collective-permute-start(bf16[4,4,2,128,256]{4,3,2,1,0:T(8,128)(2,1)} %get-tuple-element.394), channel_id=1, source_target_pairs={{0,4},{4,0},{8,12},{12,8},{16,20},{20,16},{24,28},{28,24},{1,5},{5... | collective-permute-start | bytes 6291464 | tf_op jit(solution)/shard_map/ppermute | solution.py:860
  396.1 19.4 %collective-permute-start.48 = (bf16[2,256,512]{2,1,0:T(8,128)(2,1)}, bf16[2,256,512]{2,1,0:T(8,128)(2,1)S(1)}, u32[]{:S(2)}, u32[]{:S(2)}) collective-permute-start(bf16[2,256,512]{2,1,0:T(8,128)(2,1)} %get-tuple-element.389), channel_id=1, source_target_pairs={{0,1},{1,0},{2,3},{3,2},{4,5},{5,4},{6,7},{7,6},{8,9},{9,8},{10,11... | collective-permute-start | bytes 1572872 | tf_op jit(solution)/shard_map/ppermute | solution.py:860
  399.1 14.3 %collective-permute-start.47 = (bf16[256,512]{1,0:T(8,128)(2,1)}, bf16[256,512]{1,0:T(8,128)(2,1)S(1)}, u32[]{:S(2)}, u32[]{:S(2)}) collective-permute-start(bf16[256,512]{1,0:T(8,128)(2,1)} %get-tuple-element.384), channel_id=1, source_target_pairs={{0,2},{1,3},{2,0},{3,1},{4,6},{5,7},{6,4},{7,5},{8,10},{9,11},{10,... | collective-permute-start | bytes 786440 | tf_op jit(solution)/shard_map/ppermute | solution.py:860
  422.1 26.3 %collective-permute-start.49 = (bf16[2,1024,256]{2,1,0:T(8,128)(2,1)S(1)}, bf16[2,1024,256]{2,1,0:T(8,128)(2,1)S(1)}, u32[]{:S(2)}, u32[]{:S(2)}) collective-permute-start(bf16[2,1024,256]{2,1,0:T(8,128)(2,1)S(1)} %get-tuple-element.402), channel_id=1, source_target_pairs={{0,16},{4,20},{8,24},{12,28},{16,0},{20,4},{24,8},{28,12},{1,17},{... | collective-permute-start | bytes 3145736 | tf_op jit(solution)/shard_map/ppermute | solution.py:860
  423.6 24.7 %collective-permute-start.50 = (bf16[2,1024,256]{2,1,0:T(8,128)(2,1)S(1)}, bf16[2,1024,256]{2,1,0:T(8,128)(2,1)S(1)}, u32[]{:S(2)}, u32[]{:S(2)}) collective-permute-start(bf16[2,1024,256]{2,1,0:T(8,128)(2,1)S(1)} %get-tuple-element.403), channel_id=1, source_target_pairs={{0,8},{4,12},{8,0},{12,4},{16,24},{20,28},{24,16},{28,20},{1,9},{5... | collective-permute-start | bytes 3145736 | tf_op jit(solution)/shard_map/ppermute | solution.py:860
  426.9 21.5 %collective-permute-start.51 = (bf16[256,512]{1,0:T(8,128)(2,1)}, bf16[256,512]{1,0:T(8,128)(2,1)S(1)}, u32[]{:S(2)}, u32[]{:S(2)}) collective-permute-start(bf16[256,512]{1,0:T(8,128)(2,1)} %get-tuple-element.406), channel_id=1, source_target_pairs={{0,2},{1,3},{2,0},{3,1},{4,6},{5,7},{6,4},{7,5},{8,10},{9,11},{10,... | collective-permute-start | bytes 786440 | tf_op jit(solution)/shard_map/ppermute | solution.py:860
  453.5 4.3 collective-permute-start.52
  455.4 11.6 %collective-permute-start.54 = (bf16[1024,256]{1,0:T(8,128)(2,1)S(1)}, bf16[1024,256]{1,0:T(8,128)(2,1)S(1)}, u32[]{:S(2)}, u32[]{:S(2)}) collective-permute-start(bf16[1024,256]{1,0:T(8,128)(2,1)S(1)} %get-tuple-element.421), channel_id=1, source_target_pairs={{0,8},{4,12},{8,0},{12,4},{16,24},{20,28},{24,16},{28,20},{1,9},{5... | collective-permute-start | bytes 1572872 | tf_op jit(solution)/shard_map/ppermute | solution.py:860
  456.9 11.3 %collective-permute-start.55 = (bf16[1024,256]{1,0:T(8,128)(2,1)S(1)}, bf16[1024,256]{1,0:T(8,128)(2,1)S(1)}, u32[]{:S(2)}, u32[]{:S(2)}) collective-permute-start(bf16[1024,256]{1,0:T(8,128)(2,1)S(1)} %get-tuple-element.422), channel_id=1, source_target_pairs={{0,16},{4,20},{8,24},{12,28},{16,0},{20,4},{24,8},{28,12},{1,17},{... | collective-permute-start | bytes 1572872 | tf_op jit(solution)/shard_map/ppermute | solution.py:860
  457.9 5.2 collective-permute-start.53
  472.4 13.9 %collective-permute-start.56 = (bf16[2,512,256]{2,1,0:T(8,128)(2,1)}, bf16[2,512,256]{2,1,0:T(8,128)(2,1)S(1)}, u32[]{:S(2)}, u32[]{:S(2)}) collective-permute-start(bf16[2,512,256]{2,1,0:T(8,128)(2,1)} %get-tuple-element.435), channel_id=1, source_target_pairs={{0,1},{1,0},{2,3},{3,2},{4,5},{5,4},{6,7},{7,6},{8,9},{9,8},{10,11... | collective-permute-start | bytes 1572872 | tf_op jit(solution)/shard_map/ppermute | solution.py:860
  491.3 5.6 collective-permute-start.57
  496.9 11.5 %collective-permute-start.58 = (bf16[2,82,1024]{2,1,0:T(8,128)(2,1)S(1)}, bf16[2,82,1024]{2,1,0:T(8,128)(2,1)S(1)}, u32[]{:S(2)}, u32[]{:S(2)}) collective-permute-start(bf16[2,82,1024]{2,1,0:T(8,128)(2,1)S(1)} %pad_maximum_fusion.2), channel_id=1, source_target_pairs={{0,16},{4,20},{8,24},{12,28},{16,0},{20,4},{24,8},{28,12},{1,17},{... | collective-permute-start | bytes 1007624 | tf_op jit(solution)/shard_map/ppermute | solution.py:860
  497.9 10.4 %collective-permute-start.59 = (bf16[512,256]{1,0:T(8,128)(2,1)S(1)}, bf16[512,256]{1,0:T(8,128)(2,1)S(1)}, u32[]{:S(2)}, u32[]{:S(2)}) collective-permute-start(bf16[512,256]{1,0:T(8,128)(2,1)S(1)} %copy-done.79), channel_id=1, source_target_pairs={{0,2},{1,3},{2,0},{3,1},{4,6},{5,7},{6,4},{7,5},{8,10},{9,11},{10,... | collective-permute-start | bytes 786440 | tf_op jit(solution)/shard_map/ppermute | solution.py:860
  509.0 5.6 collective-permute-start.60
  533.0 4.5 collective-permute-start.65
  (86 other events, 777.7 us)
Sparse Core Ops, SparseCore 0:
  10.4 31.1 all-gather.4
  43.7 45.4 all-gather.6
where the time goes:
time: 575 us; the launch traced here: 564 us
  Pallas kernels  331 us (58%)
  waiting for transfers between devices  85.2 us (15%)
  starting transfers between devices  55.4 us (10%)
  local copies, waits for them, and re-layouts  39.7 us (7%)
  other arithmetic  30.7 us (5%)
  between operations  20.3 us (4%)
    pallas_call x19, Pallas kernels, call(): pl.pallas_call(kernel, grid_spec=pltpu.PrefetchScalarGridSpec(num_scalar_...  145 us
    pallas_call x2, Pallas kernels, feed_forward(): pl.pallas_call(feed_kernel, grid=(steps,), in_specs=[pl.BlockSpec((frames...  81.4 us
    ppermute x66, waiting for transfers between devices, swap(): return lax.ppermute(values, axis, pairs)  73.1 us
    ppermute x66, starting transfers between devices, swap(): return lax.ppermute(values, axis, pairs)  55.4 us
    pallas_call x2, Pallas kernels, attend_backward(): pl.pallas_call(attend_backward_kernel, grid=(frames, count), in_specs=[sp...  47.3 us
    pallas_call x1, Pallas kernels, attend_forward(): pl.pallas_call(attend_forward_kernel, grid=(frames, width // 128), in_spe...  32.8 us
    unnamed x165, local copies, waits for them, and re-layouts  23.9 us
    pallas_call x6, Pallas kernels, add_and_split(): pl.pallas_call(functools.partial(add_kernel, axes), grid=(steps,), in_spe...  22.3 us
  transfers between devices with their start and end apart: 68, of which 21 were waited for; matrix products, arithmetic and copies ran while one was open for 4% of the time, Pallas kernels for 56%

commit v1 on v0

--- a/solution.py
+++ b/solution.py
@@ -76,56 +76,104 @@
     return queries_one, keys_one
 
 
+def each_head(values):
+    lane = lax.broadcasted_iota(jnp.int32, values.shape, 1)
+    zero = jnp.zeros_like(values)
+    return jnp.concatenate(
+        [jnp.where(lane < HEAD, values, zero), jnp.where(lane < HEAD, zero, values)], 0
+    )
+
+
 def attend_forward_kernel(q_ref, k_ref, v_ref, out_ref, total_ref):
-    rows = q_ref.shape[1]
+    rows, width = q_ref.shape[1:]
     key_count = -(-rows // 128) * 128
-    queries = q_ref[0] * jnp.asarray(HEAD**-0.5, bf16)
-    key_rows = pad_rows(k_ref[0], key_count)
-    value_rows = pad_rows(v_ref[0], key_count)
     lane = lax.broadcasted_iota(jnp.int32, (rows, 128), 1)
-    outs, totals = [], []
-    for head in range(2):
-        queries_one, keys_one = head_pair(queries, key_rows, head)
-        scores = dot(queries_one, keys_one, NT)
-        highest = jnp.max(scores, 1, keepdims=True)
-        shifted = jnp.exp(scores - highest)
-        total = jnp.sum(shifted, 1, keepdims=True)
-        probability = (shifted * (1.0 / total)).astype(bf16)
-        outs.append(dot(probability, value_rows))
-        totals.append(highest + jnp.log(total))
-    out_ref[0] = jnp.where(lane < HEAD, outs[0], outs[1]).astype(bf16)
-    both = jnp.where(lane < HEAD, totals[0], totals[1]).T
-    total_ref[0, 0] = jnp.concatenate([both[0:1], both[HEAD : HEAD + 1]], 0)
+    out_of = lax.broadcasted_iota(jnp.int32, (rows, 128), 1) > PATCHES - (key_count - 128)
+    pairs = width // 128
+
+    def score(pair):
+        lanes = slice(pair * 128, (pair + 1) * 128)
+        queries = q_ref[0, :, lanes] * jnp.asarray(HEAD**-0.5, bf16)
+        return dot(queries, each_head(pad_rows(k_ref[0, :, lanes], key_count)), NT)
+
+    waiting = [score(0)]
+    for pair in range(pairs):
+        if pair + 1 < pairs:
+            waiting.append(score(pair + 1))
+        both = waiting.pop(0)
+        shares, totals, sums = [], [], []
+        for head in range(2):
+            scores = both[:, head * key_count : (head + 1) * key_count]
+            tail = jnp.where(out_of, far_below, scores[:, key_count - 128 :])
+            scores = jnp.concatenate([scores[:, : key_count - 128], tail], 1)
+            highest = jnp.max(scores, 1, keepdims=True)
+            shifted = jnp.exp(scores - highest)
+            total = jnp.sum(shifted, 1, keepdims=True)
+            shares.append(shifted.astype(bf16))
+            sums.append(1.0 / total)
+            totals.append(highest + jnp.log(total))
+        lanes = slice(pair * 128, (pair + 1) * 128)
+        out = dot(jnp.concatenate(shares, 1), each_head(pad_rows(v_ref[0, :, lanes], key_count)))
+        out_ref[0, :, lanes] = (out * jnp.where(lane < HEAD, *sums)).astype(bf16)
+        logs = jnp.where(lane < HEAD, *totals).T
+        total_ref[0, pair] = jnp.concatenate([logs[0:1], logs[HEAD : HEAD + 1]], 0)
 
 
 def attend_backward_kernel(q_ref, k_ref, v_ref, total_ref, grad_ref, *rest):
     dq_ref, dk_ref, dv_ref = rest[-3:]
-    rows = q_ref.shape[1]
-    query_count = -(-rows // 128) * 128
-    queries = pad_rows(q_ref[0], query_count) * jnp.asarray(HEAD**-0.5, bf16)
-    grads = pad_rows(grad_ref[0], query_count)
-    key_rows = k_ref[0]
-    value_rows = v_ref[0]
-    keys_t = pad_rows(key_rows, query_count).astype(f32).T.astype(bf16)
-    lane = lax.broadcasted_iota(jnp.int32, (rows, 128), 1)
-    grad_q, grad_k, grad_v = [], [], []
-    for head in range(2):
-        queries_one, keys_one = head_pair(queries, key_rows, head)
-        total = total_ref[0, 0, head : head + 1, :]
-        if query_count > rows:
-            total = jnp.concatenate([total, jnp.zeros((1, query_count - rows), f32)], 1)
-        probability = jnp.exp(dot(keys_one, queries_one, NT) - total)
-        values_one = jnp.where((lane // HEAD) == head, value_rows, jnp.asarray(0, bf16))
-        grad_prob = dot(values_one, grads, NT)
-        inner = jnp.sum(grad_prob * probability, 0, keepdims=True)
-        grad_scores = (probability * (grad_prob - inner)).astype(bf16)
-        grad_v.append(dot(probability.astype(bf16), grads))
-        grad_k.append(dot(grad_scores, queries))
-        grad_q.append(dot(keys_t[HEAD * head : HEAD * (head + 1)], pad_rows(grad_scores, query_count)))
-    grad_q = jnp.concatenate(grad_q, 0) * HEAD**-0.5
-    dq_ref[0] = grad_q.T[:rows].astype(bf16)
-    dk_ref[0] = jnp.where(lane < HEAD, grad_k[0], grad_k[1]).astype(bf16)
-    dv_ref[0] = jnp.where(lane < HEAD, grad_v[0], grad_v[1]).astype(bf16)
+    rows, width = q_ref.shape[1:]
+    count = -(-rows // 128) * 128
+    pairs = width // 128
+    tail = rows // 16 * 16 - 16
+    out_of = lax.broadcasted_iota(jnp.int32, (rows - tail, count), 0) > PATCHES - tail
+
+    def swapped(values):
+        return jnp.concatenate([values[:, HEAD:], values[:, :HEAD]], 1)
+
+    def load(pair):
+        lanes = slice(pair * 128, (pair + 1) * 128)
+        queries = pad_rows(q_ref[0, :, lanes], count) * jnp.asarray(HEAD**-0.5, bf16)
+        return lanes, queries, pad_rows(grad_ref[0, :, lanes], count)
+
+    def start(pair):
+        lanes, queries, grads = load(pair)
+        keys, values = k_ref[0, :, lanes], swapped(v_ref[0, :, lanes])
+        first = lax.broadcasted_iota(jnp.int32, (rows, 128), 1) < HEAD
+        queries, grads = each_head(queries), each_head(swapped(grads))
+        products = []
+        for head in range(2):
+            mixed = jnp.where(first, keys, values) if head == 0 else jnp.where(first, values, keys)
+            right = [
+                queries[head * count : (head + 1) * count],
+                grads[(1 - head) * count : (2 - head) * count],
+            ]
+            products.append(dot(mixed, jnp.concatenate(right, 0), NT))
+        return products
+
+    waiting = [start(0)]
+    for pair in range(pairs):
+        if pair + 1 < pairs:
+            waiting.append(start(pair + 1))
+        products = waiting.pop(0)
+        lanes, queries, grads = load(pair)
+        shares, grad_scores = [], []
+        for head in range(2):
+            total = total_ref[0, pair, head : head + 1, :]
+            total = jnp.concatenate([total, jnp.zeros((1, count - rows), f32)], 1)
+            share = jnp.exp(products[head][:, :count] - total)
+            share = jnp.concatenate([share[:tail], jnp.where(out_of, 0.0, share[tail:])], 0)
+            grad_share = products[head][:, count:]
+            inner = jnp.sum(grad_share * share, 0, keepdims=True)
+            grad_scores.append((share * (grad_share - inner)).astype(bf16))
+            shares.append(share.astype(bf16))
+        dv_ref[0, :, lanes] = dot(jnp.concatenate(shares, 1), each_head(grads)).astype(bf16)
+        dk_ref[0, :, lanes] = dot(jnp.concatenate(grad_scores, 1), each_head(queries)).astype(bf16)
+        keys_t = pad_rows(k_ref[0, :, lanes], count).astype(f32).T.astype(bf16)
+        back = [
+            dot(keys_t[HEAD * head : HEAD * (head + 1)], pad_rows(grad_scores[head], count))
+            for head in range(2)
+        ]
+        dq_ref[0, :, lanes] = (jnp.concatenate(back, 0) * HEAD**-0.5).T[:rows].astype(bf16)
 
 
 def cost(flops, moved):
@@ -140,12 +188,12 @@
 
 def attend_forward(queries, key_rows, value_rows):
     frames, rows, width = queries.shape
-    spec = pl.BlockSpec((1, rows, 128), lambda f, h: (f, 0, h))
+    spec = pl.BlockSpec((1, rows, width), lambda f: (f, 0, 0))
     return pl.pallas_call(
         attend_forward_kernel,
-        grid=(frames, width // 128),
+        grid=(frames,),
         in_specs=[spec] * 3,
-        out_specs=[spec, pl.BlockSpec((1, 1, 2, rows), lambda f, h: (f, h, 0, 0))],
+        out_specs=[spec, pl.BlockSpec((1, width // 128, 2, rows), lambda f: (f, 0, 0, 0))],
         out_shape=[
             jax.ShapeDtypeStruct((frames, rows, width), bf16),
             jax.ShapeDtypeStruct((frames, width // 128, 2, rows), f32),
@@ -158,11 +206,12 @@
 
 def attend_backward(queries, key_rows, value_rows, totals, grads, begin, count, earlier=()):
     frames, rows, width = queries.shape
-    spec = pl.BlockSpec((1, rows, 128), lambda f, h: (f, 0, h + begin))
-    total_spec = pl.BlockSpec((1, 1, 2, rows), lambda f, h: (f, h + begin, 0, 0))
+    at = begin // count
+    spec = pl.BlockSpec((1, rows, 128 * count), lambda f: (f, 0, at))
+    total_spec = pl.BlockSpec((1, count, 2, rows), lambda f: (f, at, 0, 0))
     return pl.pallas_call(
         attend_backward_kernel,
-        grid=(frames, count),
+        grid=(frames,),
         in_specs=[spec] * 3 + [total_spec, spec] + [pl.BlockSpec(memory_space=pl.ANY)] * len(earlier),
         out_specs=[spec] * 3,
         out_shape=[jax.ShapeDtypeStruct((frames, rows, width), bf16)] * 3,
@@ -199,14 +248,14 @@
     second = jnp.concatenate(halves(down_refs, 1, 0), 0)
     bias_sum = jnp.zeros((1, chunk), f32)
     for frame in range(frames):
-        place = pl.ds(frame * rows, rows)
+        place = pl.ds(frame * FRAME_LANES, rows)
         pre = dot(n2_ref[frame], first) + bias_ref[0]
-        sigma = 1.0 / (1.0 + jnp.exp(-1.702 * pre))
+        sigma = 0.5 + 0.5 * jnp.tanh(0.851 * pre)
         act = (pre * sigma).astype(bf16)
         act_ref[place] = act
         out_ref[frame] += dot(act, second, NT)
         grad_act = dot(g_ref[frame], second)
-        grad_pre = grad_act * (sigma + 1.702 * pre * sigma * (1.0 - sigma))
+        grad_pre = grad_act * (sigma * (1.0 + 1.702 * pre * (1.0 - sigma)))
         grad_low = grad_pre.astype(bf16)
         dpre_ref[place] = grad_low
         bias_sum += jnp.sum(grad_low.astype(f32), 0, keepdims=True)
@@ -214,9 +263,9 @@
     db_ref[0] = bias_sum
 
     def place_grad(left_ref, right_ref, own_ref, other_ref):
-        for at, ref in ((0, own_ref), (half, other_ref)):
-            grad = dot(left_ref[at : at + half], right_ref[...]).astype(bf16)
-            ref[:, 0] = grad.reshape(blocks, part, chunk)
+        grad = dot(left_ref[...], right_ref[...]).astype(bf16)
+        own_ref[:, 0] = grad[:half].reshape(blocks, part, chunk)
+        other_ref[:, 0] = grad[half:].reshape(blocks, part, chunk)
 
     place_grad(n2t_ref, dpre_ref, dup_own_ref, dup_other_ref)
     place_grad(gt_ref, act_ref, ddown_own_ref, ddown_other_ref)
@@ -313,8 +362,11 @@
     return pl.BlockSpec(block, lambda *_: index)
 
 
+FRAME_LANES = -(-ROWS // 128) * 128
+
+
 def row_count(frames):
-    return -(-frames * ROWS // 128) * 128
+    return frames * FRAME_LANES
 
 
 def prepare_kernel(info_ref, tokens_ref, cot_ref, x_ref, g_ref, gt_ref, gsum_ref, hold_ref):
@@ -334,7 +386,7 @@
     grads = padded(cot_ref)
     for f, rows in enumerate(grads):
         g_ref[f] = rows.astype(bf16)
-    full = pad_rows(jnp.concatenate(grads, 0), gt_ref.shape[1])
+    full = jnp.concatenate([pad_rows(rows, FRAME_LANES) for rows in grads], 0)
     gt_ref[...] = full.T.astype(bf16)
     gsum_ref[...] = jnp.sum(full, 0, keepdims=True)
 
@@ -426,10 +478,11 @@
     return jnp.where(place, message, x_ref[f].astype(f32))
 
 
-def put_transposed(ref, rows):
+def put_transposed(ref, rows, f):
     for c in range(BLOCKS):
-        block = pad_rows(rows[:, c * BLOCK : (c + 1) * BLOCK].astype(f32), ref.shape[1])
-        ref[c * BLOCK : (c + 1) * BLOCK] = block.T.astype(bf16)
+        block = pad_rows(rows[:, c * BLOCK : (c + 1) * BLOCK].astype(f32), FRAME_LANES)
+        place = slice(f * FRAME_LANES, (f + 1) * FRAME_LANES)
+        ref[c * BLOCK : (c + 1) * BLOCK, place] = block.T.astype(bf16)
 
 
 def halves(refs, which, *at):
@@ -448,33 +501,29 @@
 def project_kernel(
     info_ref, x_ref, msg_ref, gain_ref, shift_ref, bq_ref, bv_ref, *refs
 ):
-    a_refs, b_refs, (q_ref, k_ref, v_ref, ht_ref, h_ref) = refs[:4], refs[4:8], refs[8:]
+    a_refs, b_refs, (q_ref, k_ref, v_ref, h_ref) = refs[:4], refs[4:8], refs[8:]
     frames = x_ref.shape[0]
 
     @pl.when(pl.program_id(0) == 0)
     def _():
         for f in range(frames):
             rows = with_message(x_ref, msg_ref, info_ref, f)
-            normed = norm_rows(rows, gain_ref[...], shift_ref[...])[0]
-            h_ref[pl.ds(f * ROWS, ROWS)] = normed.astype(bf16)
-        put_transposed(ht_ref, h_ref[...])
-
-    sides = (slice(0, D // 2), slice(D // 2, D))
+            normed = norm_rows(rows, gain_ref[...], shift_ref[...])[0].astype(bf16)
+            h_ref[pl.ds(f * ROWS, ROWS)] = normed
+
     for out_ref, weights, bias in (
         (q_ref, halves(a_refs, 0, 0, 0), bq_ref[...]),
         (k_ref, halves(a_refs, 0, 0, 1), 0.0),
         (v_ref, halves(b_refs, 1, 0, 0), bv_ref[...]),
     ):
+        rows = dot(h_ref[...], jnp.concatenate(weights, 0)) + bias
         for f in range(frames):
-            place = pl.ds(f * ROWS, ROWS)
-            rows = dot(h_ref[place, sides[0]], weights[0]) + dot(h_ref[place, sides[1]], weights[1])
-            out_ref[f] = (rows + bias).astype(bf16)
+            out_ref[f] = rows[f * ROWS : (f + 1) * ROWS].astype(bf16)
 
 
 def project(info, x, message, vec_rel, vectors, attn):
     frames = x.shape[0]
     n, z, _, part, width = attn[0].shape
-    deep = row_count(frames)
     bias = pl.BlockSpec((1, width), lambda j, info_ref: (0, j))
     a_spec = pl.BlockSpec((n, 1, 2, part, width), lambda j, info_ref: (0, j, 0, 0, 0))
     b_spec = pl.BlockSpec((n, 1, 1, part, width), lambda j, info_ref: (0, j, 0, 0, 0))
@@ -487,50 +536,69 @@
         [once(frames, ROWS, D), once(FRAMES, D), once(1, D), once(1, D), bias, bias]
         + [a_spec] * 4
         + [b_spec] * 4,
-        [out] * 3 + [kept(D, deep)],
-        [shaped(bf16, frames, ROWS, D)] * 3 + [shaped(bf16, D, deep)],
+        [out] * 3 + [kept(frames * ROWS, D)],
+        [shaped(bf16, frames, ROWS, D)] * 3 + [shaped(bf16, frames * ROWS, D)],
         "project",
-        [pltpu.VMEM((frames * ROWS, D), bf16)],
+        (),
         6 * frames * ROWS * D * D,
     )
+
+
+def transpose_kernel(info_ref, in_ref, out_ref):
+    put_transposed(out_ref, in_ref[...], 0)
+
+
+def transposed(info, rows):
+    frames = rows.shape[0] // ROWS
+    return call(
+        transpose_kernel,
+        info,
+        (rows,),
+        (frames,),
+        [pl.BlockSpec((ROWS, D), lambda f, info_ref: (f, 0))],
+        [pl.BlockSpec((D, FRAME_LANES), lambda f, info_ref: (0, f))],
+        [shaped(bf16, D, row_count(frames))],
+        "transposed",
+    )[0]
 
 
 def combine_kernel(
     info_ref, x_ref, a_ref, bias_ref, gain_ref, shift_ref, *refs
 ):
-    b_refs, (mid_ref, n2_ref, n2t_ref, hold_ref) = refs[:4], refs[4:]
-    frames = x_ref.shape[0]
-    z, width = b_refs[0].shape[1], b_refs[0].shape[-1]
-    weights = [halves(b_refs, 1, j, 0) for j in range(z)]
-    for f in range(frames):
-        for side in range(2):
-            half = slice(side * D // 2, (side + 1) * D // 2)
-            total = x_ref[f, :, half].astype(f32) + bias_ref[:, half]
-            for j in range(z):
-                total += dot(a_ref[f, :, j * width : (j + 1) * width], weights[j][side], NT)
-            mid_ref[f, :, half] = total
-        low = mid_ref[f].astype(bf16).astype(f32)
-        normed = norm_rows(low, gain_ref[...], shift_ref[...])[0].astype(bf16)
-        n2_ref[f] = normed
-        hold_ref[pl.ds(f * ROWS, ROWS)] = normed
-    put_transposed(n2t_ref, hold_ref[...])
+    b_refs, (mid_ref, n2_ref, n2t_ref) = refs[:4], refs[4:]
+    weight = whole_out(b_refs)
+    middle = x_ref[0].astype(f32) + bias_ref[...] + dot(a_ref[0], weight, NT)
+    mid_ref[0] = middle
+    low = middle.astype(bf16).astype(f32)
+    normed = norm_rows(low, gain_ref[...], shift_ref[...])[0].astype(bf16)
+    n2_ref[0] = normed
+    put_transposed(n2t_ref, normed, 0)
+
+
+def whole_out(b_refs):
+    parts = [jnp.concatenate(halves(b_refs, 1, j, 0), 0) for j in range(b_refs[0].shape[1])]
+    return jnp.concatenate(parts, 1)
 
 
 def combine(info, x, attended, vec_rel, attn):
     frames = x.shape[0]
     n, z, _, part, width = attn[4].shape
-    deep = row_count(frames)
+    frame = pl.BlockSpec((1, ROWS, D), lambda f, info_ref: (f, 0, 0))
     weight = once(n, z, 1, part, width, at=(0, 0, 1, 0, 0))
     return call(
         combine_kernel,
         info,
         (x, attended, vec_rel[12:13], vec_rel[2:3], vec_rel[3:4], *attn[4:]),
-        (1,),
-        [once(frames, ROWS, D)] * 2 + [once(1, D)] * 3 + [weight] * 4,
-        [once(frames, ROWS, D), once(frames, ROWS, D), once(D, deep)],
-        [shaped(f32, frames, ROWS, D), shaped(bf16, frames, ROWS, D), shaped(bf16, D, deep)],
+        (frames,),
+        [frame] * 2 + [once(1, D)] * 3 + [weight] * 4,
+        [frame, frame, pl.BlockSpec((D, FRAME_LANES), lambda f, info_ref: (0, f))],
+        [
+            shaped(f32, frames, ROWS, D),
+            shaped(bf16, frames, ROWS, D),
+            shaped(bf16, D, row_count(frames)),
+        ],
         "combine",
-        [pltpu.VMEM((frames * ROWS, D), bf16)],
+        (),
         2 * frames * ROWS * D * D,
     )
 
@@ -562,15 +630,9 @@
         total_ref[...] = jnp.zeros_like(total_ref)
 
     sums_ref[...] += sums
-    for j in range(z):
-        weights = halves(b_refs, 1, j, 0)
-        rows = dot(dmid[:, : D // 2], weights[0]) + dot(dmid[:, D // 2 :], weights[1])
-        da_ref[0, :, j * width : (j + 1) * width] = rows.astype(bf16)
-    put_transposed(dmt_ref, dmid)
-    attended = pad_rows(a_ref[0], dmt_ref.shape[1])
-    for j in range(z):
-        lanes = slice(j * width, (j + 1) * width)
-        total_ref[:, lanes] += dot(dmt_ref[...], attended[:, lanes])
+    da_ref[0] = dot(dmid, whole_out(b_refs)).astype(bf16)
+    put_transposed(dmt_ref, dmid, 0)
+    total_ref[...] += dot(dmt_ref[...], pad_rows(a_ref[0], FRAME_LANES))
 
     @pl.when(f == pl.num_programs(0) - 1)
     def _():
@@ -605,14 +667,14 @@
     info_ref, ht_ref, dq_ref, dk_ref, dv_ref, ok_ref, os_ref, ak_ref, as_ref, bk_ref, bs_ref, sq_ref, sv_ref
 ):
     frames = dq_ref.shape[0]
-    deep = ht_ref.shape[1]
     n, _, _, part, width = bk_ref.shape
     bk_ref[:, 0, 1] = ok_ref[:, 0]
     bs_ref[:, 0, 1] = os_ref[:, 0]
     for w, ref in enumerate((dq_ref, dk_ref, dv_ref)):
-        rows = pad_rows(jnp.concatenate([ref[f] for f in range(frames)], 0), deep)
+        rows = jnp.concatenate([pad_rows(ref[f], FRAME_LANES) for f in range(frames)], 0)
+        full = dot(ht_ref[...], rows).astype(bf16)
         for at, a_ref, b_ref in ((0, ak_ref, bk_ref), (D // 2, as_ref, bs_ref)):
-            grad = dot(ht_ref[at : at + D // 2], rows).astype(bf16).reshape(n, part, width)
+            grad = full[at : at + D // 2].reshape(n, part, width)
             if w < 2:
                 a_ref[:, 0, w] = grad
             else:
@@ -654,14 +716,11 @@
     def _():
         total_ref[...] = jnp.zeros_like(total_ref)
 
-    weights = [halves(a_refs, 0, 0, 0), halves(a_refs, 0, 0, 1), halves(b_refs, 1, 0, 0)]
-    for side in range(2):
-        half = slice(side * D // 2, (side + 1) * D // 2)
-        for f in range(frames):
-            rows = jnp.zeros((ROWS, D // 2), f32)
-            for ref, weight in zip((dq_ref, dk_ref, dv_ref), weights):
-                rows += dot(ref[f], weight[side], NT)
-            total_ref[f, :, half] += rows
+    parts = [halves(a_refs, 0, 0, 0), halves(a_refs, 0, 0, 1), halves(b_refs, 1, 0, 0)]
+    weight = jnp.concatenate([jnp.concatenate(v, 0) for v in parts], 1)
+    for f in range(frames):
+        rows = jnp.concatenate([dq_ref[f], dk_ref[f], dv_ref[f]], 1)
+        total_ref[f] += dot(rows, weight, NT)
 
     @pl.when(j == pl.num_programs(0) - 1)
     def _():
@@ -745,8 +804,9 @@
     return shifted * (1.0 / jnp.sum(shifted, 1, keepdims=True))
 
 
-def message_forward_kernel(info_ref, cls_ref, vec_ref, *refs):
-    weights, (msg_ref, first_ref, pack_ref, hold_ref) = refs[:8], refs[8:]
+def message_forward_kernel(info_ref, cls_ref, rel_ref, *refs):
+    weights, (vec_ref, msg_ref, first_ref, pack_ref, hold_ref) = refs[:8], refs[8:]
+    vec_ref[...] = permuted(rel_ref, info_ref, BLOCKS)
 
     def relative(rows):
         hold_ref[...] = rows
@@ -767,16 +827,21 @@
         pack_ref[i] = rows.astype(f32)
 
 
-def message_forward(info, class_rows, vectors, weights):
+def message_forward(info, class_rows, vec_rel, weights):
     one = kept(FRAMES, D)
     return call(
         message_forward_kernel,
         info,
-        (class_rows, vectors, *weights),
+        (class_rows, vec_rel, *weights),
         (1,),
-        [one, kept(*vectors.shape)] + [once(*w.shape) for w in weights],
-        [one, one, kept(5, FRAMES, D)],
-        [shaped(f32, FRAMES, D), shaped(f32, FRAMES, D), shaped(f32, 5, FRAMES, D)],
+        [one, kept(*vec_rel.shape)] + [once(*w.shape) for w in weights],
+        [kept(*vec_rel.shape), one, one, kept(5, FRAMES, D)],
+        [
+            shaped(f32, *vec_rel.shape),
+            shaped(f32, FRAMES, D),
+            shaped(f32, FRAMES, D),
+            shaped(f32, 5, FRAMES, D),
+        ],
         "message_forward",
         [pltpu.VMEM((FRAMES, D), f32)],
         10 * FRAMES * D * D,
@@ -948,7 +1013,7 @@
 def add_and_split(pairs, axes):
     lead = pairs[0][0].shape[:-2]
     rows, width = pairs[0][0].shape[-2:]
-    steps = 4 if rows % 64 == 0 else 1
+    steps = 2 if rows % 32 == 0 else 1
     zeros = (0,) * len(lead)
     spec = pl.BlockSpec((*lead, rows // steps, width), lambda i: (*zeros, i, 0))
     out = pl.BlockSpec((*lead[1:], rows // steps, width), lambda i: (*zeros[1:], i, 0))
@@ -980,7 +1045,7 @@
 
     def step(self):
         if not relative_order():
-            return self.held
+            return list(self.held)
         axes, bits = ((0, 1), (4, 2)) if self.place == 0 else ((0, 0), (2, 4))
         self.place += 1
         sums = list(add_and_split(list(zip(self.held, self.arrived)), axes))
@@ -990,28 +1055,29 @@
 
 
 def pair_kernel(info_ref, *refs):
-    ins, outs = refs[:8], refs[8:]
+    ins, outs = refs[:-2], refs[-2:]
     rows = ins[0].shape[1]
     for side in range(2):
-        for i in range(2):
+        for i in range(len(ins) // 4):
             total = add_low(ins[4 * i + side][0], ins[4 * i + 2 + side][0])
             outs[side][0, i * rows : (i + 1) * rows] = total
 
 
 def add_and_pair(info, held, arrived):
+    count = len(held)
     rows, width = held[0][0].size // held[0].shape[-1], held[0].shape[-1]
     own = pl.BlockSpec((1, rows, width), lambda h, ref: (2 * h + ref[2 * BLOCKS] % 2, 0, 0))
     other = pl.BlockSpec((1, rows, width), lambda h, ref: (2 * h + 1 - ref[2 * BLOCKS] % 2, 0, 0))
     flat = [v.reshape(4, rows, width) for pair in zip(held, arrived) for v in pair for _ in range(2)]
-    out = pl.BlockSpec((1, 2 * rows, width), lambda h, ref: (h, 0, 0))
+    out = pl.BlockSpec((1, count * rows, width), lambda h, ref: (h, 0, 0))
     return call(
         pair_kernel,
         info,
         flat,
         (2,),
-        [own, other] * 4,
+        [own, other] * (2 * count),
         [out] * 2,
-        [shaped(bf16, 2, 2 * rows, width)] * 2,
+        [shaped(bf16, 2, count * rows, width)] * 2,
         "add_and_pair",
     )
 
@@ -1038,16 +1104,16 @@
 
 
 class ScatterVideos:
-    def __init__(self, info, sums):
-        self.info, self.shape = info, sums.shape
+    def __init__(self, info, *scatters):
+        self.info, self.shape = info, scatters[0].shape
         self.direct = lax.axis_size("tensor") != 4
+        held = [v.reshape(self.shape) for s in scatters for v in s.held]
+        arrived = [v.reshape(self.shape) for s in scatters for v in s.arrived]
         if self.direct:
-            values = jnp.stack([add_low(h, a) for h, a in zip(sums.held, sums.arrived)], 1)
+            values = jnp.stack([add_low(h, a) for h, a in zip(held, arrived)], 1)
             self.held = lax.psum_scatter(values, "tensor", scatter_dimension=0, tiled=False)
             self.going, self.arrived = self.held, jnp.zeros_like(self.held)
             return
-        held = [v.reshape(self.shape) for v in sums.held]
-        arrived = [v.reshape(self.shape) for v in sums.arrived]
         self.held, self.going = add_and_pair(info, held, arrived)
         self.arrived = swap(self.going, "tensor", 1)
 
@@ -1059,7 +1125,7 @@
         return going
 
     def result(self):
-        return add_low(self.held, self.arrived).reshape((2,) + self.shape[1:])
+        return add_low(self.held, self.arrived).reshape((-1,) + self.shape[1:])
 
 
 class GatherSmall:
@@ -1081,9 +1147,15 @@
 
 
 def sum_everywhere(values):
-    for axis in ("dp", "tensor"):
-        for bit in bits_of(axis):
-            values = values + swap(values, axis, bit)
+    rounds = [("dp", bits_of("dp")[:1])]
+    for axis, bits in (("dp", bits_of("dp")[1:]), ("tensor", bits_of("tensor"))):
+        rounds += [(axis, bits[i : i + 2]) for i in range(0, len(bits), 2)]
+    for axis, bits in rounds:
+        if len(bits) == 1:
+            values = values + swap(values, axis, bits[0])
+            continue
+        first, second, both = (swap(values, axis, b) for b in (*bits, sum(bits)))
+        values = (values + first) + (second + both)
     return values
 
 
@@ -1170,34 +1242,34 @@
     msg_w = msg_go.result()
     vec_rel = jnp.concatenate(msg_w[:4], 0)[:, 5 * part : 5 * part + vec_count, :part]
     vec_rel = jnp.moveaxis(vec_rel, 0, 1).reshape(-1, D).astype(f32)
-    vectors = plain_order(info, vec_rel)
+
+    sent_mlp = mlp_go[0].own + mlp_go[1].own
+    vectors, message, first_msg, msg_pack = beside(
+        message_forward(info, after(class_rows, *sent_mlp).astype(f32), vec_rel, msg_w), attn_go
+    )
     ff_bias = vectors[14:].reshape(z_count, 2, half_ff)
-
-    sent_mlp = mlp_go[0].own + mlp_go[1].own
-    message, first_msg, msg_pack = beside(
-        message_forward(info, after(class_rows, *sent_mlp).astype(f32), vectors, msg_w), attn_go
-    )
     attn_go.step()
     attn_w = attn_go.result()
     projected = project(info, x, message, vec_rel, vectors, attn_w)
-    queries, key_rows, value_rows, normed_t = beside(projected, *mlp_go)
-    sent_mlp = mlp_go[0].step() + mlp_go[1].step()
+    queries, key_rows, value_rows, normed = beside(projected, *mlp_go)
+    sent_mlp = mlp_go[0].step()
     attended, totals = beside(
         attend_forward(after(queries, *sent_mlp), key_rows, value_rows), mlp_go[0]
     )
-    sent_mlp = mlp_go[0].step()
+    sent_mlp = mlp_go[0].step() + mlp_go[1].step()
     middle, n2, n2_t = beside(
-        combine(info, x, after(attended, *sent_mlp), vec_rel, attn_w), mlp_go[1]
-    )
-    sent_mlp = mlp_go[1].step()
-    n2 = after(n2, *sent_mlp)
+        combine(info, x, after(attended, *sent_mlp), vec_rel, attn_w), mlp_go[0]
+    )
 
     def feed(j, n2):
         return feed_forward(n2, n2_t, grads, grads_t, ff_bias[:, j], mlp_go[j].result())
 
     out_0, dn2_0, *dw_0, db_0 = beside(feed(0, n2), mlp_go[1])
+    sent_mlp = mlp_go[1].step()
+    normed_t = beside(transposed(info, after(normed, *sent_mlp)), mlp_go[1])
+    dw_0 = after(dw_0, normed_t)
     sums_0 = Scatter(dw_0[::2], dw_0[1::2])
-    out_1, dn2_1, *dw_1, db_1 = beside(feed(1, after(n2, db_0)), sums_0)
+    out_1, dn2_1, *dw_1, db_1 = beside(feed(1, after(n2, normed_t)), sums_0)
     sums_1 = Scatter(dw_1[::2], dw_1[1::2])
     going = sums_0.step()
     dmid, grad_attended, *grad_out_w, sums_two = beside(
@@ -1218,52 +1290,39 @@
         sums_1,
     )
     going = sums_1.step()
-    mlp_0 = ScatterVideos(info, sums_0)
     dqk_keep, dqk_send, dvo_keep, dvo_send, sum_q, sum_v = beside(
-        project_grads(
-            info, after(normed_t, mlp_0.going, *going), grad_qkv, grad_out_w, attn_w
-        ),
-        sums_1,
-        mlp_0,
+        project_grads(info, after(normed_t, *going), grad_qkv, grad_out_w, attn_w), sums_1
     )
     sums_attn = Scatter([dqk_keep, dvo_keep], [dqk_send, dvo_send])
-    going = mlp_0.step()
-    mlp_1 = ScatterVideos(info, sums_1)
+    mlp_go = ScatterVideos(info, sums_0, sums_1)
     block_output = beside(
-        finish(
-            info,
-            [after(middle, going, mlp_1.going), out_0, out_1],
-            vec_rel[13:14],
-            "block_output",
-        ),
+        finish(info, [after(middle, mlp_go.going), out_0, out_1], vec_rel[13:14], "block_output"),
         sums_attn,
-        mlp_0,
-        mlp_1,
     )
     going = sums_attn.step()
-    going.append(mlp_1.step())
-    mlp_0 = mlp_0.result()
     ing, dmsg, sums_one = beside(
-        project_back(info, after(x, mlp_0, *going), message, dmid, vec_rel, grad_qkv, attn_w),
+        project_back(info, after(x, *going), message, dmid, vec_rel, grad_qkv, attn_w),
         sums_attn,
-        mlp_1,
+        mlp_go,
     )
     going = sums_attn.step()
-    mlp_1 = mlp_1.result()
 
     ff_bias_grad = jnp.stack(
         [db.reshape(z_count, half_ff) for db in (db_0, db_1)], 1
     ).reshape(FF // D, D)
     table = jnp.concatenate([sums_one, sums_two, grad_sum, sum_q, sum_v, ff_bias_grad], 0)
     dmsg = dmsg[:, 0].astype(bf16).astype(f32)
-    dmsg, table = beside(
-        gather_and_sum_videos(after(dmsg, mlp_1, *going), table), sums_attn
-    )
+    dmsg, table = gather_and_sum_videos(after(dmsg, *going), table)
+    mlp_go.arrived = after(mlp_go.arrived, dmsg)
+    sent_mlp = mlp_go.step()
+    dmsg = beside(after(dmsg, sent_mlp), sums_attn)
     attn_go = ScatterVideos(info, sums_attn)
     grad_class, sent, sums_msg = beside(
         message_backward(info, after(dmsg, attn_go.going), first_msg, msg_pack, vectors, msg_w),
         attn_go,
-    )
+        mlp_go,
+    )
+    mlp_sum = mlp_go.result()
     going = attn_go.step()
 
     plain = plain_order(info, table[:6])
@@ -1271,26 +1330,12 @@
     sent = jnp.concatenate([msg_pack[:2], sent], 0).astype(bf16).reshape(7 * FRAMES, D)
     sent = jnp.concatenate([class_rows, sent, table.astype(bf16)], 0)
     small = GatherSmall(after(sent, going))
-    middle_block = BLOCKS // 2
     input_grad = beside(
-        finish(info, [after(ing, small.values)], grad_class, "input_grad", 0, middle_block), small
-    )
-    rows = small.step()
-    input_grad = beside(
-        finish(
-            info,
-            [after(ing, rows)],
-            grad_class,
-            "input_grad",
-            middle_block,
-            BLOCKS - middle_block,
-            [input_grad],
-        ),
-        small,
-        attn_go,
+        finish(info, [after(ing, small.values)], grad_class, "input_grad"), small, attn_go
     )
     small.step()
     attn_grad = attn_go.result()
+    small.step()
     everyone = small.step()
     tables = lax.dynamic_slice_in_dim(everyone[:, 8 * FRAMES :], dp_index * part, part, 2)
     vec_grad = jnp.sum(tables.astype(f32), 0).T
@@ -1309,7 +1354,8 @@
     )
 
     attn_grad = jnp.swapaxes(attn_grad.reshape(4, part, local_width), 0, 1).astype(f32)
-    mlp_grad = jnp.swapaxes(jnp.concatenate([mlp_0, mlp_1], 2), 0, 1).astype(f32)
+    mlp_grad = jnp.concatenate([mlp_sum[:2], mlp_sum[2:]], 2)
+    mlp_grad = jnp.swapaxes(mlp_grad, 0, 1).astype(f32)
 
     keep_share = (z_index == 0).astype(f32)
     squares = (

time: 575 us -> 544 us (0.946)
  Pallas kernels: 331 us -> 300 us
    pallas_call x3, Pallas kernels: 80.1 us -> 58.4 us  [the longest x2 40 us: attend_backward(): pl.pallas_call(attend_backward_kernel, grid=(frames,), in_specs=[spec] *...]
    ppermute x66, waiting for transfers between devices: 73.1 us -> 81.1 us  [swap(): return lax.ppermute(values, axis, pairs)]
    pallas_call x19 -> x16, Pallas kernels: 145 us -> 139 us  [call(): pl.pallas_call(kernel, grid_spec=pltpu.PrefetchScalarGridSpec(num_scalar_...]
    unnamed x165 -> x145, local copies, waits for them, and re-layouts: 23.9 us -> 24.9 us
  transfers between devices with their start and end apart: 68 -> 68, of which waited for: 21 -> 23; matrix products, arithmetic and copies ran while one was open for 4% -> 4% of each run, Pallas kernels for 56% -> 55%
where the time goes in v1:
time: 544 us; the launch traced here: 535 us
  Pallas kernels  300 us (55%)
  waiting for transfers between devices  88.5 us (16%)
  starting transfers between devices  55.6 us (10%)
  local copies, waits for them, and re-layouts  39.6 us (7%)
  other arithmetic  29.9 us (5%)
  between operations  20.2 us (4%)
    pallas_call x16, Pallas kernels, call(): pl.pallas_call(kernel, grid_spec=pltpu.PrefetchScalarGridSpec(num_scalar_...  139 us
    ppermute x66, waiting for transfers between devices, swap(): return lax.ppermute(values, axis, pairs)  81.1 us
    pallas_call x2, Pallas kernels, feed_forward(): pl.pallas_call(feed_kernel, grid=(steps,), in_specs=[pl.BlockSpec((frames...  81.1 us
    ppermute x66, starting transfers between devices, swap(): return lax.ppermute(values, axis, pairs)  55.6 us
    pallas_call x2, Pallas kernels, attend_backward(): pl.pallas_call(attend_backward_kernel, grid=(frames,), in_specs=[spec] *...  40 us
    unnamed x145, local copies, waits for them, and re-layouts  24.9 us
    pallas_call x6, Pallas kernels, add_and_split(): pl.pallas_call(functools.partial(add_kernel, axes), grid=(steps,), in_spe...  19 us
    pallas_call x1, Pallas kernels, attend_forward(): pl.pallas_call(attend_forward_kernel, grid=(frames,), in_specs=[spec] * 3...  18.5 us
  transfers between devices with their start and end apart: 68, of which 23 were waited for; matrix products, arithmetic and copies ran while one was open for 4% of the time, Pallas kernels for 55%

profile of v1, /device:TPU:0, one launch (start us, length us, event | category | flops | bytes accessed | tf_op | source)
XLA Modules:
  0.0 535.1 jit_solution(15884570016603363568)
XLA Ops:
  10.3 2.3 copy.104
  13.4 3.0 collective-permute-start
  16.4 1.5 collective-permute-start.1
  18.6 8.6 %prepare.1 = (bf16[2,592,1024]{2,1,0:T(8,128)(2,1)}, bf16[2,592,1024]{2,1,0:T(8,128)(2,1)}, bf16[1024,1280]{1,0:T(8,128)(2,1)}, f32[1,1024]{1,0:T(1,128)}) custom-call(s32[17]{0:T(128)} %pad_add_fusion.info_ref, bf16[1154,1024]{1,0:T(8,128)(2,1)} %tokens_ref.1, bf16[1154,1024]{1,0:T(8,128)(2,1)} %cot_ref.1), custom_call_target="tpu_custom_call" | custom-call | bytes 762624 | tf_op jit(solution)/shard_map/prepare/pallas_call | solution.py:334
  27.3 5.4 %collective-permute-done.1.refs_3_ = bf16[640,512]{1,0:T(8,128)(2,1)S(1)} collective-permute-done((bf16[640,512]{1,0:T(8,128)(2,1)S(1)}, bf16[640,512]{1,0:T(8,128)(2,1)S(1)}, u32[]{:S(2)}, u32[]{:S(2)}) %collective-permute-start.1) | collective-permute-done | bytes 655392 | tf_op jit(solution)/shard_map/ppermute | solution.py:925
  37.7 1.5 collective-permute-start.4
  39.8 1.8 all-gather.5.cloned.1.call-done
  43.0 1.5 collective-permute-start.2
  46.0 33.8 %collective-permute-done.2 = bf16[4,2,128,256]{3,2,1,0:T(8,128)(2,1)S(1)} collective-permute-done((bf16[4,2,128,256]{3,2,1,0:T(8,128)(2,1)S(1)}, bf16[4,2,128,256]{3,2,1,0:T(8,128)(2,1)S(1)}, u32[]{:S(2)}, u32[]{:S(2)}) %collective-permute-start.2) | collective-permute-done | bytes 524320 | tf_op jit(solution)/shard_map/ppermute | solution.py:925
  83.6 5.6 %all-gather.7.cloned.1.call-done = bf16[8,128,1024]{2,1,0:T(8,128)(2,1)} async-done(((bf16[2,128,1024]{2,1,0:T(8,128)(2,1)}), bf16[8,128,1024]{2,1,0:T(8,128)(2,1)}) %all-gather.7.cloned.1.call-update) | async-done | bytes 2097168 | tf_op jit(solution)/shard_map/all_gather | solution.py:1221
  89.2 3.1 fusion.33
  94.9 8.0 %message_forward.1 = (f32[18,1024]{1,0:T(8,128)}, f32[8,1024]{1,0:T(8,128)}, f32[8,1024]{1,0:T(8,128)}, f32[5,8,1024]{2,1,0:T(8,128)}) custom-call(s32[17]{0:T(128)} %pad_add_fusion.info_ref, f32[8,1024]{1,0:T(8,128)} %convert_element_type.93.cls_ref, f32[18,1024]{1,0:T(8,128)} %bitcast.241, bf16[2,672,512]{2,1,0:T(8,128)(2,1)} %copy-done.4, ...), custom_call_target="tpu_custom_call" | custom-call | flops 5242880 | bytes 697344 | tf_op jit(solution)/shard_map/message_forward/pallas_call | solution.py:334
  102.9 3.6 collective-permute-done.10.refs_1_
  109.7 1.5 collective-permute-start.18
  113.8 1.6 slice_bitcast_fusion.12
  115.3 14.7 %project.1 = (bf16[2,592,1024]{2,1,0:T(8,128)(2,1)}, bf16[2,592,1024]{2,1,0:T(8,128)(2,1)}, bf16[2,592,1024]{2,1,0:T(8,128)(2,1)}, bf16[1184,1024]{1,0:T(8,128)(2,1)}) custom-call(s32[17]{0:T(128)} %pad_add_fusion.info_ref, bf16[2,592,1024]{2,1,0:T(8,128)(2,1)} %get-tuple-element.411.x_ref, f32[8,1024]{1,0:T(8,128)} %get-tuple-element.263.msg_ref, ...), custom_call_target="tpu_custom_call" | custom-call | flops 465567744 | bytes 1285120 | tf_op jit(solution)/shard_map/project/pallas_call | solution.py:334
  130.0 3.5 collective-permute-done.18
  137.4 1.7 copy-done
  139.0 18.5 %attend_forward.1 = (bf16[2,592,1024]{2,1,0:T(8,128)(2,1)S(1)}, f32[2,8,2,592]{3,2,1,0:T(2,128)S(1)}) custom-call(bf16[2,592,1024]{2,1,0:T(8,128)(2,1)S(1)} %copy-done, bf16[2,592,1024]{2,1,0:T(8,128)(2,1)} %get-tuple-element.277.k_ref, bf16[2,592,1024]{2,1,0:T(8,128)(2,1)} %get-tuple-element.278.v_ref), custom_call_target="tpu_custom_call" | custom-call | flops 358875136 | bytes 1212416 | tf_op jit(solution)/shard_map/attend_forward/pallas_call | solution.py:192
  160.2 1.5 collective-permute-start.26
  165.7 10.1 %combine.1 = (f32[2,592,1024]{2,1,0:T(8,128)}, bf16[2,592,1024]{2,1,0:T(8,128)(2,1)}, bf16[1024,1280]{1,0:T(8,128)(2,1)}) custom-call(s32[17]{0:T(128)} %pad_add_fusion.info_ref, bf16[2,592,1024]{2,1,0:T(8,128)(2,1)} %get-tuple-element.411.x_ref, bf16[2,592,1024]{2,1,0:T(8,128)(2,1)} %copy-done.5, f32[1,1024]{1,0:T(1,128)} %get-tuple-element.504.bias_ref, ...), custom_call_target="tpu_custom_call" | custom-call | flops 155189248 | bytes 1184512 | tf_op jit(solution)/shard_map/combine/pallas_call | solution.py:334
  176.4 40.5 %feed_forward.2 = (f32[2,592,1024]{2,1,0:T(8,128)}, f32[2,592,1024]{2,1,0:T(8,128)}, bf16[4,4,128,512]{3,2,1,0:T(8,128)(2,1)}, bf16[4,4,128,512]{3,2,1,0:T(8,128...) custom-call(bf16[2,592,1024]{2,1,0:T(8,128)(2,1)} %get-tuple-element.318.n2_ref, ...), custom_call_target="tpu_custom_call" | custom-call | flops 1862270976 | bytes 2260992 | tf_op jit(solution)/shard_map/feed_forward/pallas_call | solution.py:288
  217.5 3.9 transposed.1.ht_ref
  223.9 40.6 %feed_forward.3 = (f32[2,592,1024]{2,1,0:T(8,128)}, f32[2,592,1024]{2,1,0:T(8,128)}, bf16[4,4,128,512]{3,2,1,0:T(8,128)(2,1)}, bf16[4,4,128,512]{3,2,1,0:T(8,128...) custom-call(bf16[2,592,1024]{2,1,0:T(8,128)(2,1)} %get-tuple-element.318.n2_ref, ...), custom_call_target="tpu_custom_call" | custom-call | flops 1862270976 | bytes 2260992 | tf_op jit(solution)/shard_map/feed_forward/pallas_call | solution.py:288
  265.8 4.9 add.269
  271.9 18.6 %between.1 = (bf16[2,592,1024]{2,1,0:T(8,128)(2,1)}, bf16[2,592,1024]{2,1,0:T(8,128)(2,1)}, bf16[4,4,128,256]{3,2,1,0:T(8,128)(2,1)}, bf16[4,4,128,256]{3,2,1,0:T(8,128)(2,1)}, f32[3,1024]{1,0:T(4,128)}) custom-call(s32[17]{0:T(128)} %pad_add_fusion.info_ref, f32[2,592,1024]{2,1,0:T(8,128)} %get-tuple-element.340.ea_ref, ...), custom_call_target="tpu_custom_call" | custom-call | flops 310378496 | bytes 1909760 | tf_op jit(solution)/shard_map/between/pallas_call | solution.py:334
  290.5 4.1 add.270
  294.6 1.5 collective-permute-start.40
  297.5 20.1 %attend_backward.2 = (bf16[2,592,1024]{2,1,0:T(8,128)(2,1)S(1)}, bf16[2,592,1024]{2,1,0:T(8,128)(2,1)S(1)}, bf16[2,592,1024]{2,1,0:T(8,128)(2,1)}) custom-call(bf16[2,592,1024]{2,1,0:T(8,128)(2,1)} %get-tuple-element.276.q_ref, bf16[2,592,1024]{2,1,0:T(8,128)(2,1)} %get-tuple-element.277.k_ref, bf16[2,592,1024]{2,1,0:T(8,128)(2,1)} %get-tuple-element.278.v_ref, ...), custom_call_target="tpu_custom_call" | custom-call | flops 358875136 | bytes 1212416 | tf_op jit(solution)/shard_map/attend_backward/pallas_call | solution.py:212
  318.6 1.7 add.271
  321.6 19.8 %attend_backward.3 = (bf16[2,592,1024]{2,1,0:T(8,128)(2,1)S(1)}, bf16[2,592,1024]{2,1,0:T(8,128)(2,1)S(1)}, bf16[2,592,1024]{2,1,0:T(8,128)(2,1)}) custom-call(bf16[2,592,1024]{2,1,0:T(8,128)(2,1)} %get-tuple-element.276.q_ref, bf16[2,592,1024]{2,1,0:T(8,128)(2,1)} %get-tuple-element.277.k_ref, ...), custom_call_target="tpu_custom_call", output_to_operand_aliasing={{0}: (5, {}), {1}: (6, {}), {2}: (7, {})} | custom-call | flops 358875136 | bytes 1212416 | tf_op jit(solution)/shard_map/attend_backward/pallas_call | solution.py:212
  342.9 2.4 add.272
  349.7 13.7 %project_grads.1 = (bf16[4,4,2,128,256]{4,3,2,1,0:T(8,128)(2,1)}, bf16[4,4,2,128,256]{4,3,2,1,0:T(8,128)(2,1)}, bf16[4,4,2,128,256]{4,3,2,1,0:T(8,128)(2,1)}, bf...) custom-call(s32[17]{0:T(128)} %pad_add_fusion.info_ref, ...), custom_call_target="tpu_custom_call" | custom-call | flops 465567744 | bytes 1274368 | tf_op jit(solution)/shard_map/project_grads/pallas_call | solution.py:334
  364.4 4.2 add_and_pair.2
  368.6 1.6 collective-permute-start.48
  370.2 9.9 %block_output.1 = f32[1154,1024]{1,0:T(8,128)} custom-call(s32[17]{0:T(128)} %pad_add_fusion.info_ref, f32[2,592,1024]{2,1,0:T(8,128)} %get-tuple-element.399.mid_ref.refs_0_, f32[2,592,1024]{2,1,0:T(8,128)} %get-tuple-element.400.refs_1_, f32[2,592,1024]{2,1,0:T(8,128)} %get-tuple-element.401.refs_2_, f32[1,1024]{1,0:T(1,128)} %get-tuple-element.501.refs_3_), custom_call_target="tpu_custom_call" | custom-call | bytes 1204992 | tf_op jit(solution)/shard_map/block_output/pallas_call | solution.py:334
  382.2 4.2 add.273
  387.7 19.0 %project_back.1 = (f32[2,592,1024]{2,1,0:T(8,128)}, f32[2,1,1024]{2,1,0:T(1,128)}, f32[2,1024]{1,0:T(2,128)}) custom-call(s32[17]{0:T(128)} %pad_add_fusion.info_ref, bf16[2,592,1024]{2,1,0:T(8,128)(2,1)} %get-tuple-element.411.x_ref, f32[8,1024]{1,0:T(8,128)} %get-tuple-element.263.msg_ref, bf16[2,592,1024]{2,1,0:T(8,128)(2,1)} %get-tuple-element.412.dmid_ref, ...), custom_call_target="tpu_custom_call" | custom-call | flops 465567744 | bytes 1588480 | tf_op jit(solution)/shard_map/project_back/pallas_call | solution.py:334
  406.7 4.3 collective-permute-done.46.refs_1_
  412.3 1.7 add.274
  418.3 1.6 collective-permute-done.49
  420.0 2.7 collective-permute-start.50
  422.7 3.1 collective-permute-done.50
  426.5 3.3 add_and_single.2
  429.8 2.0 collective-permute-start.54
  432.8 3.2 add_and_pair.3
  437.9 2.0 plain_order.1
  440.8 9.1 %message_backward.1 = (f32[8,1024]{1,0:T(8,128)}, f32[5,8,1024]{2,1,0:T(8,128)}, f32[6,1024]{1,0:T(8,128)}) custom-call(s32[17]{0:T(128)} %pad_add_fusion.info_ref, f32[4,2,1024]{2,1,0:T(2,128)} %pad_maximum_fusion.7.dmsg_ref, f32[8,1024]{1,0:T(8,128)} %get-tuple-element.445.first_ref, f32[5,8,1024]{2,1,0:T(8,128)} %get-tuple-element.417.pack_ref, ...), custom_call_target="tpu_custom_call" | custom-call | flops 5242880 | bytes 704512 | tf_op jit(solution)/shard_map/message_backward/pallas_call | solution.py:334
  449.8 1.6 collective-permute-done.54
  451.4 5.4 %collective-permute-done.53.ao_ref.ap_ref = bf16[2,512,256]{2,1,0:T(8,128)(2,1)S(1)} collective-permute-done((bf16[2,512,256]{2,1,0:T(8,128)(2,1)}, bf16[2,512,256]{2,1,0:T(8,128)(2,1)S(1)}, u32[]{:S(2)}, u32[]{:S(2)}) %collective-permute-start.53) | collective-permute-done | bytes 524320 | tf_op jit(solution)/shard_map/ppermute | solution.py:925
  458.7 2.7 add_and_single.3
  462.6 7.9 %input_grad.1 = f32[1154,1024]{1,0:T(8,128)} custom-call(s32[17]{0:T(128)} %pad_add_fusion.info_ref, f32[2,592,1024]{2,1,0:T(8,128)} %get-tuple-element.455.refs_0_, f32[8,1024]{1,0:T(8,128)} %get-tuple-element.456.refs_1_), custom_call_target="tpu_custom_call" | custom-call | bytes 600576 | tf_op jit(solution)/shard_map/input_grad/pallas_call | solution.py:334
  470.5 2.0 collective-permute-done.56
  472.5 1.5 collective-permute-start.57
  474.2 7.5 %collective-permute-done.57 = bf16[2,82,1024]{2,1,0:T(8,128)(2,1)S(1)} collective-permute-done((bf16[2,82,1024]{2,1,0:T(8,128)(2,1)S(1)}, bf16[2,82,1024]{2,1,0:T(8,128)(2,1)S(1)}, u32[]{:S(2)}, u32[]{:S(2)}) %collective-permute-start.57) | collective-permute-done | bytes 335904 | tf_op jit(solution)/shard_map/ppermute | solution.py:925
  483.0 2.6 multiply_reduce_fusion.1
  494.8 1.7 collective-permute-start.61
  498.4 2.6 collective-permute-done.62
  501.1 2.1 collective-permute-start.64
  503.2 2.3 collective-permute-start.65
  505.7 2.9 collective-permute-done.65
  510.5 8.1 %multiply_add_fusion = (f32[128,5,1024]{2,0,1:T(8,128)}, f32[128,5,1024]{2,0,1:T(8,128)}, f32[128,5,1024]{2,0,1:T(8,128)}, f32[128,5,1024]{2,0,1:T(8,128)}) fusion(f32[128,5,1024]{2,0,1:T(8,128)} %param.31, f32[128,5,1024]{2,0,1:T(8,128)} %param.28, f32[128,5,1024]{2,0,1:T(8,128)S(1)} %fusion.2, f32[]{:T(128)S(6)} %div.81, f32[128,5,1024]{2,0,1:T(8,128)} %param.30, ...), kind=kLoop, calls=%fused_computation.2 | loop fusion | flops 12451840 | bytes 23592964 | tf_op jit(solution)/shard_map/add | solution.py:1372
  518.7 5.7 %multiply_add_fusion.2 = (f32[128,2,1024]{2,1,0:T(2,128)}, f32[128,2,1024]{2,1,0:T(2,128)}, f32[128,2,1024]{2,1,0:T(2,128)}, f32[128,2,1024]{2,1,0:T(2,128)}) fusion(f32[128,2,1024]{2,1,0:T(2,128)S(1)} %copy-done.39, f32[128,2,1024]{2,1,0:T(2,128)S(1)} %copy-done.24, f32[128,2,1024]{2,1,0:T(2,128)S(1)} %copy-done.25, f32[]{:T(128)S(6)} %div.81, ...), kind=kLoop, calls=%fused_computation.24 | loop fusion | flops 4980736 | bytes 9437188 | tf_op jit(solution)/shard_map/add | solution.py:1372
  524.4 2.3 multiply_add_fusion.4
  (331 shorter events, 79.5 us)
Async XLA Ops:
  7.2 34.4 %all-gather.5.cloned.1.call-start = ((), (), s32[]{:S(2)}) async-start(), calls=%async_computation | async-start | bytes 1351680 | tf_op jit(solution)/shard_map/all_gather | solution.py:1220
  10.3 78.9 %all-gather.7.cloned.1.call-start = ((), (), s32[]{:S(2)}) async-start(), calls=%async_computation.1 | async-start | bytes 2621440 | tf_op jit(solution)/shard_map/all_gather | solution.py:1221
  13.4 20.0 %collective-permute-start = (bf16[672,512]{1,0:T(8,128)(2,1)S(1)}, bf16[672,512]{1,0:T(8,128)(2,1)S(1)}, u32[]{:S(2)}, u32[]{:S(2)}) collective-permute-start(bf16[672,512]{1,0:T(8,128)(2,1)S(1)} %fusion.8.refs_0_), channel_id=1, source_target_pairs={{0,8},{4,12},{8,0},{12,4},{16,24},{20,28},{24,16},{28,20},{1,9},{5... | collective-permute-start | bytes 2064392 | tf_op jit(solution)/shard_map/ppermute | solution.py:925
  16.4 16.2 %collective-permute-start.1 = (bf16[640,512]{1,0:T(8,128)(2,1)S(1)}, bf16[640,512]{1,0:T(8,128)(2,1)S(1)}, u32[]{:S(2)}, u32[]{:S(2)}) collective-permute-start(bf16[640,512]{1,0:T(8,128)(2,1)S(1)} %get-tuple-element.495.refs_2_), channel_id=1, source_target_pairs={{0,16},{4,20},{8,24},{12,28},{16,0},{20,4},{24,8},{28,12},{1,17},{... | collective-permute-start | bytes 1966088 | tf_op jit(solution)/shard_map/ppermute | solution.py:925
  37.7 42.5 %collective-permute-start.4 = (bf16[2,672,512]{2,1,0:T(8,128)(2,1)S(1)}, bf16[2,672,512]{2,1,0:T(8,128)(2,1)}, u32[]{:S(2)}, u32[]{:S(2)}) collective-permute-start(bf16[2,672,512]{2,1,0:T(8,128)(2,1)S(1)} %get-tuple-element.250.refs_0_), channel_id=1, source_target_pairs={{0,16},{4,20},{8,24},{12,28},{16,0},{20,4},{24,8},{28,12},{1,17},{... | collective-permute-start | bytes 4128776 | tf_op jit(solution)/shard_map/ppermute | solution.py:925
  39.2 40.9 %collective-permute-start.5 = (bf16[2,640,512]{2,1,0:T(8,128)(2,1)}, bf16[2,640,512]{2,1,0:T(8,128)(2,1)}, u32[]{:S(2)}, u32[]{:S(2)}) collective-permute-start(bf16[2,640,512]{2,1,0:T(8,128)(2,1)} %get-tuple-element.251.refs_4_), channel_id=1, source_target_pairs={{0,8},{4,12},{8,0},{12,4},{16,24},{20,28},{24,16},{28,20},{1,9},{5... | collective-permute-start | bytes 3932168 | tf_op jit(solution)/shard_map/ppermute | solution.py:925
  39.8 42.6 %collective-permute-start.6 = (bf16[2,672,512]{2,1,0:T(8,128)(2,1)S(1)}, bf16[2,672,512]{2,1,0:T(8,128)(2,1)}, u32[]{:S(2)}, u32[]{:S(2)}) collective-permute-start(bf16[2,672,512]{2,1,0:T(8,128)(2,1)S(1)} %get-tuple-element.250.refs_0_), channel_id=1, source_target_pairs={{0,4},{4,0},{8,12},{12,8},{16,20},{20,16},{24,28},{28,24},{1,5},{5... | collective-permute-start | bytes 4128776 | tf_op jit(solution)/shard_map/ppermute | solution.py:925
  43.0 36.9 %collective-permute-start.2 = (bf16[4,2,128,256]{3,2,1,0:T(8,128)(2,1)S(1)}, bf16[4,2,128,256]{3,2,1,0:T(8,128)(2,1)S(1)}, u32[]{:S(2)}, u32[]{:S(2)}) collective-permute-start(bf16[4,2,128,256]{3,2,1,0:T(8,128)(2,1)S(1)} %get-tuple-element.498), channel_id=1, source_target_pairs={{0,8},{4,12},{8,0},{12,4},{16,24},{20,28},{24,16},{28,20},{1,9},{5... | collective-permute-start | bytes 1572872 | tf_op jit(solution)/shard_map/ppermute | solution.py:925
  44.5 35.3 %collective-permute-start.3 = (bf16[4,2,128,256]{3,2,1,0:T(8,128)(2,1)S(1)}, bf16[4,2,128,256]{3,2,1,0:T(8,128)(2,1)S(1)}, u32[]{:S(2)}, u32[]{:S(2)}) collective-permute-start(bf16[4,2,128,256]{3,2,1,0:T(8,128)(2,1)S(1)} %get-tuple-element.497), channel_id=1, source_target_pairs={{0,16},{4,20},{8,24},{12,28},{16,0},{20,4},{24,8},{28,12},{1,17},{... | collective-permute-start | bytes 1572872 | tf_op jit(solution)/shard_map/ppermute | solution.py:925
  80.2 12.7 %collective-permute-start.7 = (bf16[2,672,512]{2,1,0:T(8,128)(2,1)}, bf16[2,672,512]{2,1,0:T(8,128)(2,1)}, u32[]{:S(2)}, u32[]{:S(2)}) collective-permute-start(bf16[2,672,512]{2,1,0:T(8,128)(2,1)} %collective-permute-done.4.refs_1_), channel_id=1, source_target_pairs={{0,4},{4,0},{8,12},{12,8},{16,20},{20,16},{24,28},{28,24},{1,5},{5... | collective-permute-start | bytes 4128776 | tf_op jit(solution)/shard_map/ppermute | solution.py:925
  80.3 14.1 %collective-permute-start.8 = (bf16[2,640,512]{2,1,0:T(8,128)(2,1)}, bf16[2,640,512]{2,1,0:T(8,128)(2,1)}, u32[]{:S(2)}, u32[]{:S(2)}) collective-permute-start(bf16[2,640,512]{2,1,0:T(8,128)(2,1)} %get-tuple-element.251.refs_4_), channel_id=1, source_target_pairs={{0,4},{4,0},{8,12},{12,8},{16,20},{20,16},{24,28},{28,24},{1,5},{5... | collective-permute-start | bytes 3932168 | tf_op jit(solution)/shard_map/ppermute | solution.py:925
  80.8 14.1 %collective-permute-start.9 = (bf16[2,640,512]{2,1,0:T(8,128)(2,1)}, bf16[2,640,512]{2,1,0:T(8,128)(2,1)}, u32[]{:S(2)}, u32[]{:S(2)}) collective-permute-start(bf16[2,640,512]{2,1,0:T(8,128)(2,1)} %collective-permute-done.5.refs_5_), channel_id=1, source_target_pairs={{0,4},{4,0},{8,12},{12,8},{16,20},{20,16},{24,28},{28,24},{1,5},{5... | collective-permute-start | bytes 3932168 | tf_op jit(solution)/shard_map/ppermute | solution.py:925
  80.9 25.6 %collective-permute-start.10 = (bf16[2,4,2,128,256]{4,3,2,1,0:T(8,128)(2,1)S(1)}, bf16[2,4,2,128,256]{4,3,2,1,0:T(8,128)(2,1)}, u32[]{:S(2)}, u32[]{:S(2)}) collective-permute-start(bf16[2,4,2,128,256]{4,3,2,1,0:T(8,128)(2,1)S(1)} %bitcast.169), channel_id=1, source_target_pairs={{0,16},{4,20},{8,24},{12,28},{16,0},{20,4},{24,8},{28,12},{1,17},{... | collective-permute-start | bytes 3145736 | tf_op jit(solution)/shard_map/ppermute | solution.py:925
  82.3 25.3 %collective-permute-start.11 = (bf16[2,4,2,128,256]{4,3,2,1,0:T(8,128)(2,1)S(1)}, bf16[2,4,2,128,256]{4,3,2,1,0:T(8,128)(2,1)}, u32[]{:S(2)}, u32[]{:S(2)}) collective-permute-start(bf16[2,4,2,128,256]{4,3,2,1,0:T(8,128)(2,1)S(1)} %bitcast.163), channel_id=1, source_target_pairs={{0,8},{4,12},{8,0},{12,4},{16,24},{20,28},{24,16},{28,20},{1,9},{5... | collective-permute-start | bytes 3145736 | tf_op jit(solution)/shard_map/ppermute | solution.py:925
  92.9 15.8 %collective-permute-start.12 = (bf16[2,4,2,128,256]{4,3,2,1,0:T(8,128)(2,1)S(1)}, bf16[2,4,2,128,256]{4,3,2,1,0:T(8,128)(2,1)S(1)}, u32[]{:S(2)}, u32[]{:S(2)}) collective-permute-start(bf16[2,4,2,128,256]{4,3,2,1,0:T(8,128)(2,1)S(1)} %bitcast.170), channel_id=1, source_target_pairs={{0,4},{4,0},{8,12},{12,8},{16,20},{20,16},{24,28},{28,24},{1,5},{5... | collective-permute-start | bytes 3145736 | tf_op jit(solution)/shard_map/ppermute | solution.py:925
  94.4 15.3 %collective-permute-start.14 = (bf16[2,4,2,128,256]{4,3,2,1,0:T(8,128)(2,1)S(1)}, bf16[2,4,2,128,256]{4,3,2,1,0:T(8,128)(2,1)S(1)}, u32[]{:S(2)}, u32[]{:S(2)}) collective-permute-start(bf16[2,4,2,128,256]{4,3,2,1,0:T(8,128)(2,1)S(1)} %bitcast.164), channel_id=1, source_target_pairs={{0,4},{4,0},{8,12},{12,8},{16,20},{20,16},{24,28},{28,24},{1,5},{5... | collective-permute-start | bytes 3145736 | tf_op jit(solution)/shard_map/ppermute | solution.py:925
  107.7 7.6 %collective-permute-start.15 = (bf16[2,4,2,128,256]{4,3,2,1,0:T(8,128)(2,1)}, bf16[2,4,2,128,256]{4,3,2,1,0:T(8,128)(2,1)}, u32[]{:S(2)}, u32[]{:S(2)}) collective-permute-start(bf16[2,4,2,128,256]{4,3,2,1,0:T(8,128)(2,1)} %collective-permute-done.11.refs_5_.refs_1_), channel_id=1, source_target_pairs={{0,4},{4,0},{8,12},{12,8},{16,20},{20,16},{24,28},{28,24},{1,5},{5... | collective-permute-start | bytes 3145736 | tf_op jit(solution)/shard_map/ppermute | solution.py:925
  108.2 21.8 %collective-permute-start.16 = (bf16[4,128,512]{2,1,0:T(8,128)(2,1)}, bf16[4,128,512]{2,1,0:T(8,128)(2,1)S(1)}, u32[]{:S(2)}, u32[]{:S(2)}) collective-permute-start(bf16[4,128,512]{2,1,0:T(8,128)(2,1)} %get-tuple-element.488), channel_id=1, source_target_pairs={{0,8},{4,12},{8,0},{12,4},{16,24},{20,28},{24,16},{28,20},{1,9},{5... | collective-permute-start | bytes 1572872 | tf_op jit(solution)/shard_map/ppermute | solution.py:925
  108.7 21.3 %collective-permute-start.17 = (bf16[4,128,512]{2,1,0:T(8,128)(2,1)}, bf16[4,128,512]{2,1,0:T(8,128)(2,1)S(1)}, u32[]{:S(2)}, u32[]{:S(2)}) collective-permute-start(bf16[4,128,512]{2,1,0:T(8,128)(2,1)} %get-tuple-element.489), channel_id=1, source_target_pairs={{0,16},{4,20},{8,24},{12,28},{16,0},{20,4},{24,8},{28,12},{1,17},{... | collective-permute-start | bytes 1572872 | tf_op jit(solution)/shard_map/ppermute | solution.py:925
  109.7 23.8 %collective-permute-start.18 = (bf16[4,128,512]{2,1,0:T(8,128)(2,1)}, bf16[4,128,512]{2,1,0:T(8,128)(2,1)S(1)}, u32[]{:S(2)}, u32[]{:S(2)}) collective-permute-start(bf16[4,128,512]{2,1,0:T(8,128)(2,1)} %get-tuple-element.490), channel_id=1, source_target_pairs={{0,8},{4,12},{8,0},{12,4},{16,24},{20,28},{24,16},{28,20},{1,9},{5... | collective-permute-start | bytes 1572872 | tf_op jit(solution)/shard_map/ppermute | solution.py:925
  111.2 22.5 %collective-permute-start.19 = (bf16[4,128,512]{2,1,0:T(8,128)(2,1)S(1)}, bf16[4,128,512]{2,1,0:T(8,128)(2,1)S(1)}, u32[]{:S(2)}, u32[]{:S(2)}) collective-permute-start(bf16[4,128,512]{2,1,0:T(8,128)(2,1)S(1)} %copy-done.54), channel_id=1, source_target_pairs={{0,16},{4,20},{8,24},{12,28},{16,0},{20,4},{24,8},{28,12},{1,17},{... | collective-permute-start | bytes 1572872 | tf_op jit(solution)/shard_map/ppermute | solution.py:925
  134.8 24.2 %collective-permute-start.20 = (bf16[2,4,128,512]{3,2,1,0:T(8,128)(2,1)S(1)}, bf16[2,4,128,512]{3,2,1,0:T(8,128)(2,1)}, u32[]{:S(2)}, u32[]{:S(2)}) collective-permute-start(bf16[2,4,128,512]{3,2,1,0:T(8,128)(2,1)S(1)} %bitcast.197), channel_id=1, source_target_pairs={{0,16},{4,20},{8,24},{12,28},{16,0},{20,4},{24,8},{28,12},{1,17},{... | collective-permute-start | bytes 3145736 | tf_op jit(solution)/shard_map/ppermute | solution.py:925
  135.4 23.9 %collective-permute-start.21 = (bf16[2,4,128,512]{3,2,1,0:T(8,128)(2,1)}, bf16[2,4,128,512]{3,2,1,0:T(8,128)(2,1)}, u32[]{:S(2)}, u32[]{:S(2)}) collective-permute-start(bf16[2,4,128,512]{3,2,1,0:T(8,128)(2,1)} %bitcast.29.refs_4_), channel_id=1, source_target_pairs={{0,8},{4,12},{8,0},{12,4},{16,24},{20,28},{24,16},{28,20},{1,9},{5... | collective-permute-start | bytes 3145736 | tf_op jit(solution)/shard_map/ppermute | solution.py:925
  136.8 24.9 %collective-permute-start.22 = (bf16[2,4,128,512]{3,2,1,0:T(8,128)(2,1)S(1)}, bf16[2,4,128,512]{3,2,1,0:T(8,128)(2,1)S(1)}, u32[]{:S(2)}, u32[]{:S(2)}) collective-permute-start(bf16[2,4,128,512]{3,2,1,0:T(8,128)(2,1)S(1)} %bitcast.198), channel_id=1, source_target_pairs={{0,4},{4,0},{8,12},{12,8},{16,20},{20,16},{24,28},{28,24},{1,5},{5... | collective-permute-start | bytes 3145736 | tf_op jit(solution)/shard_map/ppermute | solution.py:925
  136.8 39.0 %collective-permute-start.24 = (bf16[2,4,128,512]{3,2,1,0:T(8,128)(2,1)}, bf16[2,4,128,512]{3,2,1,0:T(8,128)(2,1)}, u32[]{:S(2)}, u32[]{:S(2)}) collective-permute-start(bf16[2,4,128,512]{3,2,1,0:T(8,128)(2,1)} %bitcast.29.refs_4_), channel_id=1, source_target_pairs={{0,4},{4,0},{8,12},{12,8},{16,20},{20,16},{24,28},{28,24},{1,5},{5... | collective-permute-start | bytes 3145736 | tf_op jit(solution)/shard_map/ppermute | solution.py:925
  159.4 16.5 %collective-permute-start.23 = (bf16[2,4,128,512]{3,2,1,0:T(8,128)(2,1)}, bf16[2,4,128,512]{3,2,1,0:T(8,128)(2,1)}, u32[]{:S(2)}, u32[]{:S(2)}) collective-permute-start(bf16[2,4,128,512]{3,2,1,0:T(8,128)(2,1)} %collective-permute-done.20.refs_1_), channel_id=1, source_target_pairs={{0,4},{4,0},{8,12},{12,8},{16,20},{20,16},{24,28},{28,24},{1,5},{5... | collective-permute-start | bytes 3145736 | tf_op jit(solution)/shard_map/ppermute | solution.py:925
  159.4 17.0 %collective-permute-start.25 = (bf16[2,4,128,512]{3,2,1,0:T(8,128)(2,1)}, bf16[2,4,128,512]{3,2,1,0:T(8,128)(2,1)}, u32[]{:S(2)}, u32[]{:S(2)}) collective-permute-start(bf16[2,4,128,512]{3,2,1,0:T(8,128)(2,1)} %collective-permute-done.21.refs_5_), channel_id=1, source_target_pairs={{0,4},{4,0},{8,12},{12,8},{16,20},{20,16},{24,28},{28,24},{1,5},{5... | collective-permute-start | bytes 3145736 | tf_op jit(solution)/shard_map/ppermute | solution.py:925
  160.2 56.7 %collective-permute-start.26 = (bf16[2,4,128,512]{3,2,1,0:T(8,128)(2,1)S(1)}, bf16[2,4,128,512]{3,2,1,0:T(8,128)(2,1)S(1)}, u32[]{:S(2)}, u32[]{:S(2)}) collective-permute-start(bf16[2,4,128,512]{3,2,1,0:T(8,128)(2,1)S(1)} %bitcast.191), channel_id=1, source_target_pairs={{0,16},{4,20},{8,24},{12,28},{16,0},{20,4},{24,8},{28,12},{1,17},{... | collective-permute-start | bytes 3145736 | tf_op jit(solution)/shard_map/ppermute | solution.py:925
  162.8 54.2 %collective-permute-start.27 = (bf16[2,4,128,512]{3,2,1,0:T(8,128)(2,1)S(1)}, bf16[2,4,128,512]{3,2,1,0:T(8,128)(2,1)}, u32[]{:S(2)}, u32[]{:S(2)}) collective-permute-start(bf16[2,4,128,512]{3,2,1,0:T(8,128)(2,1)S(1)} %bitcast.194), channel_id=1, source_target_pairs={{0,8},{4,12},{8,0},{12,4},{16,24},{20,28},{24,16},{28,20},{1,9},{5... | collective-permute-start | bytes 3145736 | tf_op jit(solution)/shard_map/ppermute | solution.py:925
  175.8 45.6 %collective-permute-start.28 = (bf16[2,4,128,512]{3,2,1,0:T(8,128)(2,1)S(1)}, bf16[2,4,128,512]{3,2,1,0:T(8,128)(2,1)}, u32[]{:S(2)}, u32[]{:S(2)}) collective-permute-start(bf16[2,4,128,512]{3,2,1,0:T(8,128)(2,1)S(1)} %bitcast.192), channel_id=1, source_target_pairs={{0,4},{4,0},{8,12},{12,8},{16,20},{20,16},{24,28},{28,24},{1,5},{5... | collective-permute-start | bytes 3145736 | tf_op jit(solution)/shard_map/ppermute | solution.py:925
  175.9 45.5 %collective-permute-start.30 = (bf16[2,4,128,512]{3,2,1,0:T(8,128)(2,1)S(1)}, bf16[2,4,128,512]{3,2,1,0:T(8,128)(2,1)}, u32[]{:S(2)}, u32[]{:S(2)}) collective-permute-start(bf16[2,4,128,512]{3,2,1,0:T(8,128)(2,1)S(1)} %bitcast.195), channel_id=1, source_target_pairs={{0,4},{4,0},{8,12},{12,8},{16,20},{20,16},{24,28},{28,24},{1,5},{5... | collective-permute-start | bytes 3145736 | tf_op jit(solution)/shard_map/ppermute | solution.py:925
  217.0 4.4 collective-permute-start.29
  217.1 5.3 collective-permute-start.31
  223.4 41.1 %collective-permute-start.32 = (bf16[4,4,128,512]{3,2,1,0:T(8,128)(2,1)}, bf16[4,4,128,512]{3,2,1,0:T(8,128)(2,1)S(1)}, u32[]{:S(2)}, u32[]{:S(2)}) collective-permute-start(bf16[4,4,128,512]{3,2,1,0:T(8,128)(2,1)} %get-tuple-element.330), channel_id=1, source_target_pairs={{0,4},{4,0},{8,12},{12,8},{16,20},{20,16},{24,28},{28,24},{1,5},{5... | collective-permute-start | bytes 6291464 | tf_op jit(solution)/shard_map/ppermute | solution.py:925
  223.5 41.0 %collective-permute-start.33 = (bf16[4,4,128,512]{3,2,1,0:T(8,128)(2,1)}, bf16[4,4,128,512]{3,2,1,0:T(8,128)(2,1)}, u32[]{:S(2)}, u32[]{:S(2)}) collective-permute-start(bf16[4,4,128,512]{3,2,1,0:T(8,128)(2,1)} %get-tuple-element.331), channel_id=1, source_target_pairs={{0,4},{4,0},{8,12},{12,8},{16,20},{20,16},{24,28},{28,24},{1,5},{5... | collective-permute-start | bytes 6291464 | tf_op jit(solution)/shard_map/ppermute | solution.py:925
  264.5 26.0 %collective-permute-start.34 = (bf16[4,4,128,512]{3,2,1,0:T(8,128)(2,1)}, bf16[4,4,128,512]{3,2,1,0:T(8,128)(2,1)}, u32[]{:S(2)}, u32[]{:S(2)}) collective-permute-start(bf16[4,4,128,512]{3,2,1,0:T(8,128)(2,1)} %get-tuple-element.347), channel_id=1, source_target_pairs={{0,4},{4,0},{8,12},{12,8},{16,20},{20,16},{24,28},{28,24},{1,5},{5... | collective-permute-start | bytes 6291464 | tf_op jit(solution)/shard_map/ppermute | solution.py:925
  264.7 25.8 %collective-permute-start.35 = (bf16[4,4,128,512]{3,2,1,0:T(8,128)(2,1)}, bf16[4,4,128,512]{3,2,1,0:T(8,128)(2,1)}, u32[]{:S(2)}, u32[]{:S(2)}) collective-permute-start(bf16[4,4,128,512]{3,2,1,0:T(8,128)(2,1)} %get-tuple-element.348), channel_id=1, source_target_pairs={{0,4},{4,0},{8,12},{12,8},{16,20},{20,16},{24,28},{28,24},{1,5},{5... | collective-permute-start | bytes 6291464 | tf_op jit(solution)/shard_map/ppermute | solution.py:925
  270.8 46.9 %collective-permute-start.36 = (bf16[2,512,512]{2,1,0:T(8,128)(2,1)}, bf16[2,512,512]{2,1,0:T(8,128)(2,1)S(1)}, u32[]{:S(2)}, u32[]{:S(2)}) collective-permute-start(bf16[2,512,512]{2,1,0:T(8,128)(2,1)} %get-tuple-element.338), channel_id=1, source_target_pairs={{0,16},{4,20},{8,24},{12,28},{16,0},{20,4},{24,8},{28,12},{1,17},{... | collective-permute-start | bytes 3145736 | tf_op jit(solution)/shard_map/ppermute | solution.py:925
  271.3 46.4 %collective-permute-start.37 = (bf16[2,512,512]{2,1,0:T(8,128)(2,1)}, bf16[2,512,512]{2,1,0:T(8,128)(2,1)S(1)}, u32[]{:S(2)}, u32[]{:S(2)}) collective-permute-start(bf16[2,512,512]{2,1,0:T(8,128)(2,1)} %get-tuple-element.339), channel_id=1, source_target_pairs={{0,8},{4,12},{8,0},{12,4},{16,24},{20,28},{24,16},{28,20},{1,9},{5... | collective-permute-start | bytes 3145736 | tf_op jit(solution)/shard_map/ppermute | solution.py:925
  294.6 48.3 %collective-permute-start.40 = (bf16[2,512,512]{2,1,0:T(8,128)(2,1)S(1)}, bf16[2,512,512]{2,1,0:T(8,128)(2,1)S(1)}, u32[]{:S(2)}, u32[]{:S(2)}) collective-permute-start(bf16[2,512,512]{2,1,0:T(8,128)(2,1)S(1)} %get-tuple-element.354), channel_id=1, source_target_pairs={{0,16},{4,20},{8,24},{12,28},{16,0},{20,4},{24,8},{28,12},{1,17},{... | collective-permute-start | bytes 3145736 | tf_op jit(solution)/shard_map/ppermute | solution.py:925
  296.1 46.8 %collective-permute-start.41 = (bf16[2,512,512]{2,1,0:T(8,128)(2,1)S(1)}, bf16[2,512,512]{2,1,0:T(8,128)(2,1)}, u32[]{:S(2)}, u32[]{:S(2)}) collective-permute-start(bf16[2,512,512]{2,1,0:T(8,128)(2,1)S(1)} %get-tuple-element.355), channel_id=1, source_target_pairs={{0,8},{4,12},{8,0},{12,4},{16,24},{20,28},{24,16},{28,20},{1,9},{5... | collective-permute-start | bytes 3145736 | tf_op jit(solution)/shard_map/ppermute | solution.py:925
  320.3 22.5 %collective-permute-start.38 = (bf16[512,512]{1,0:T(8,128)(2,1)S(1)}, bf16[512,512]{1,0:T(8,128)(2,1)S(1)}, u32[]{:S(2)}, u32[]{:S(2)}) collective-permute-start(bf16[512,512]{1,0:T(8,128)(2,1)S(1)} %get-tuple-element.364), channel_id=1, source_target_pairs={{0,8},{4,12},{8,0},{12,4},{16,24},{20,28},{24,16},{28,20},{1,9},{5... | collective-permute-start | bytes 1572872 | tf_op jit(solution)/shard_map/ppermute | solution.py:925
  321.0 21.8 %collective-permute-start.39 = (bf16[512,512]{1,0:T(8,128)(2,1)S(1)}, bf16[512,512]{1,0:T(8,128)(2,1)S(1)}, u32[]{:S(2)}, u32[]{:S(2)}) collective-permute-start(bf16[512,512]{1,0:T(8,128)(2,1)S(1)} %get-tuple-element.365), channel_id=1, source_target_pairs={{0,16},{4,20},{8,24},{12,28},{16,0},{20,4},{24,8},{28,12},{1,17},{... | collective-permute-start | bytes 1572872 | tf_op jit(solution)/shard_map/ppermute | solution.py:925
  346.8 16.6 %collective-permute-start.42 = (bf16[512,512]{1,0:T(8,128)(2,1)S(1)}, bf16[512,512]{1,0:T(8,128)(2,1)S(1)}, u32[]{:S(2)}, u32[]{:S(2)}) collective-permute-start(bf16[512,512]{1,0:T(8,128)(2,1)S(1)} %get-tuple-element.381), channel_id=1, source_target_pairs={{0,8},{4,12},{8,0},{12,4},{16,24},{20,28},{24,16},{28,20},{1,9},{5... | collective-permute-start | bytes 1572872 | tf_op jit(solution)/shard_map/ppermute | solution.py:925
  348.3 15.2 %collective-permute-start.43 = (bf16[512,512]{1,0:T(8,128)(2,1)S(1)}, bf16[512,512]{1,0:T(8,128)(2,1)S(1)}, u32[]{:S(2)}, u32[]{:S(2)}) collective-permute-start(bf16[512,512]{1,0:T(8,128)(2,1)S(1)} %get-tuple-element.382), channel_id=1, source_target_pairs={{0,16},{4,20},{8,24},{12,28},{16,0},{20,4},{24,8},{28,12},{1,17},{... | collective-permute-start | bytes 1572872 | tf_op jit(solution)/shard_map/ppermute | solution.py:925
  363.5 16.7 %collective-permute-start.44 = (bf16[4,4,2,128,256]{4,3,2,1,0:T(8,128)(2,1)}, bf16[4,4,2,128,256]{4,3,2,1,0:T(8,128)(2,1)S(1)}, u32[]{:S(2)}, u32[]{:S(2)}) collective-permute-start(bf16[4,4,2,128,256]{4,3,2,1,0:T(8,128)(2,1)} %get-tuple-element.402), channel_id=1, source_target_pairs={{0,4},{4,0},{8,12},{12,8},{16,20},{20,16},{24,28},{28,24},{1,5},{5... | collective-permute-start | bytes 6291464 | tf_op jit(solution)/shard_map/ppermute | solution.py:925
  363.6 16.6 %collective-permute-start.45 = (bf16[4,4,2,128,256]{4,3,2,1,0:T(8,128)(2,1)}, bf16[4,4,2,128,256]{4,3,2,1,0:T(8,128)(2,1)S(1)}, u32[]{:S(2)}, u32[]{:S(2)}) collective-permute-start(bf16[4,4,2,128,256]{4,3,2,1,0:T(8,128)(2,1)} %get-tuple-element.403), channel_id=1, source_target_pairs={{0,4},{4,0},{8,12},{12,8},{16,20},{20,16},{24,28},{28,24},{1,5},{5... | collective-permute-start | bytes 6291464 | tf_op jit(solution)/shard_map/ppermute | solution.py:925
  368.6 38.1 %collective-permute-start.48 = (bf16[2,512,512]{2,1,0:T(8,128)(2,1)}, bf16[2,512,512]{2,1,0:T(8,128)(2,1)S(1)}, u32[]{:S(2)}, u32[]{:S(2)}) collective-permute-start(bf16[2,512,512]{2,1,0:T(8,128)(2,1)} %get-tuple-element.398), channel_id=1, source_target_pairs={{0,1},{1,0},{2,3},{3,2},{4,5},{5,4},{6,7},{7,6},{8,9},{9,8},{10,11... | collective-permute-start | bytes 3145736 | tf_op jit(solution)/shard_map/ppermute | solution.py:925
  386.4 24.6 %collective-permute-start.46 = (bf16[2,1024,256]{2,1,0:T(8,128)(2,1)S(1)}, bf16[2,1024,256]{2,1,0:T(8,128)(2,1)S(1)}, u32[]{:S(2)}, u32[]{:S(2)}) collective-permute-start(bf16[2,1024,256]{2,1,0:T(8,128)(2,1)S(1)} %get-tuple-element.409), channel_id=1, source_target_pairs={{0,16},{4,20},{8,24},{12,28},{16,0},{20,4},{24,8},{28,12},{1,17},{... | collective-permute-start | bytes 3145736 | tf_op jit(solution)/shard_map/ppermute | solution.py:925
  387.1 24.2 %collective-permute-start.47 = (bf16[2,1024,256]{2,1,0:T(8,128)(2,1)S(1)}, bf16[2,1024,256]{2,1,0:T(8,128)(2,1)S(1)}, u32[]{:S(2)}, u32[]{:S(2)}) collective-permute-start(bf16[2,1024,256]{2,1,0:T(8,128)(2,1)S(1)} %get-tuple-element.410), channel_id=1, source_target_pairs={{0,8},{4,12},{8,0},{12,4},{16,24},{20,28},{24,16},{28,20},{1,9},{5... | collective-permute-start | bytes 3145736 | tf_op jit(solution)/shard_map/ppermute | solution.py:925
  415.6 4.3 collective-permute-start.49
  416.2 15.6 %collective-permute-start.51 = (bf16[1024,256]{1,0:T(8,128)(2,1)S(1)}, bf16[1024,256]{1,0:T(8,128)(2,1)S(1)}, u32[]{:S(2)}, u32[]{:S(2)}) collective-permute-start(bf16[1024,256]{1,0:T(8,128)(2,1)S(1)} %get-tuple-element.423), channel_id=1, source_target_pairs={{0,8},{4,12},{8,0},{12,4},{16,24},{20,28},{24,16},{28,20},{1,9},{5... | collective-permute-start | bytes 1572872 | tf_op jit(solution)/shard_map/ppermute | solution.py:925
  416.9 15.0 %collective-permute-start.52 = (bf16[1024,256]{1,0:T(8,128)(2,1)S(1)}, bf16[1024,256]{1,0:T(8,128)(2,1)S(1)}, u32[]{:S(2)}, u32[]{:S(2)}) collective-permute-start(bf16[1024,256]{1,0:T(8,128)(2,1)S(1)} %get-tuple-element.424), channel_id=1, source_target_pairs={{0,16},{4,20},{8,24},{12,28},{16,0},{20,4},{24,8},{28,12},{1,17},{... | collective-permute-start | bytes 1572872 | tf_op jit(solution)/shard_map/ppermute | solution.py:925
  420.0 5.8 %collective-permute-start.50 = (f32[16,1024]{1,0:T(8,128)S(1)}, f32[16,1024]{1,0:T(8,128)S(1)}, u32[]{:S(2)}, u32[]{:S(2)}) collective-permute-start(f32[16,1024]{1,0:T(8,128)S(1)} %pad_maximum_fusion.3), channel_id=1, source_target_pairs={{0,2},{1,3},{2,0},{3,1},{4,6},{5,7},{6,4},{7,5},{8,10},{9,11},{10,... | collective-permute-start | bytes 196616 | tf_op jit(solution)/shard_map/ppermute | solution.py:925
  429.8 21.6 %collective-permute-start.54 = (bf16[512,512]{1,0:T(8,128)(2,1)}, bf16[512,512]{1,0:T(8,128)(2,1)S(1)}, u32[]{:S(2)}, u32[]{:S(2)}) collective-permute-start(bf16[512,512]{1,0:T(8,128)(2,1)} %get-tuple-element.436), channel_id=1, source_target_pairs={{0,2},{1,3},{2,0},{3,1},{4,6},{5,7},{6,4},{7,5},{8,10},{9,11},{10,... | collective-permute-start | bytes 1572872 | tf_op jit(solution)/shard_map/ppermute | solution.py:925
  436.0 20.9 %collective-permute-start.53 = (bf16[2,512,256]{2,1,0:T(8,128)(2,1)}, bf16[2,512,256]{2,1,0:T(8,128)(2,1)S(1)}, u32[]{:S(2)}, u32[]{:S(2)}) collective-permute-start(bf16[2,512,256]{2,1,0:T(8,128)(2,1)} %get-tuple-element.443), channel_id=1, source_target_pairs={{0,1},{1,0},{2,3},{3,2},{4,5},{5,4},{6,7},{7,6},{8,9},{9,8},{10,11... | collective-permute-start | bytes 1572872 | tf_op jit(solution)/shard_map/ppermute | solution.py:925
  461.4 11.0 %collective-permute-start.56 = (bf16[512,256]{1,0:T(8,128)(2,1)}, bf16[512,256]{1,0:T(8,128)(2,1)S(1)}, u32[]{:S(2)}, u32[]{:S(2)}) collective-permute-start(bf16[512,256]{1,0:T(8,128)(2,1)} %get-tuple-element.453), channel_id=1, source_target_pairs={{0,2},{1,3},{2,0},{3,1},{4,6},{5,7},{6,4},{7,5},{8,10},{9,11},{10,... | collective-permute-start | bytes 786440 | tf_op jit(solution)/shard_map/ppermute | solution.py:925
  461.8 8.7 %collective-permute-start.55 = (bf16[1,82,1024]{2,1,0:T(8,128)(2,1)S(1)}, bf16[1,82,1024]{2,1,0:T(8,128)(2,1)S(1)}, u32[]{:S(2)}, u32[]{:S(2)}) collective-permute-start(bf16[1,82,1024]{2,1,0:T(8,128)(2,1)S(1)} %bitcast.207), channel_id=1, source_target_pairs={{0,8},{4,12},{8,0},{12,4},{16,24},{20,28},{24,16},{28,20},{1,9},{5... | collective-permute-start | bytes 503816 | tf_op jit(solution)/shard_map/ppermute | solution.py:925
  472.5 9.2 %collective-permute-start.57 = (bf16[2,82,1024]{2,1,0:T(8,128)(2,1)S(1)}, bf16[2,82,1024]{2,1,0:T(8,128)(2,1)S(1)}, u32[]{:S(2)}, u32[]{:S(2)}) collective-permute-start(bf16[2,82,1024]{2,1,0:T(8,128)(2,1)S(1)} %pad_maximum_fusion.2), channel_id=1, source_target_pairs={{0,16},{4,20},{8,24},{12,28},{16,0},{20,4},{24,8},{28,12},{1,17},{... | collective-permute-start | bytes 1007624 | tf_op jit(solution)/shard_map/ppermute | solution.py:925
  482.3 5.6 %collective-permute-start.58 = (bf16[4,82,1024]{2,0,1:T(4,128)(2,1)S(1)}, bf16[4,82,1024]{2,0,1:T(4,128)(2,1)S(1)}, u32[]{:S(2)}, u32[]{:S(2)}) collective-permute-start(bf16[4,82,1024]{2,0,1:T(4,128)(2,1)S(1)} %copy.84), channel_id=1, source_target_pairs={{0,4},{4,0},{8,12},{12,8},{16,20},{20,16},{24,28},{28,24},{1,5},{5... | collective-permute-start | bytes 2015240 | tf_op jit(solution)/shard_map/ppermute | solution.py:925
  496.6 4.5 collective-permute-start.62
  501.1 4.4 collective-permute-start.63
  501.1 4.6 collective-permute-start.64
  503.2 5.4 %collective-permute-start.65 = (f32[8,128]{1,0:T(8,128)S(1)}, f32[8,128]{1,0:T(8,128)S(1)}, u32[]{:S(2)}, u32[]{:S(2)}) collective-permute-start(f32[8,128]{1,0:T(8,128)S(1)} %add_add_fusion.1), channel_id=1, source_target_pairs={{0,3},{1,2},{2,1},{3,0},{4,7},{5,6},{6,5},{7,4},{8,11},{9,10},{10,... | collective-permute-start | bytes 12296 | tf_op jit(solution)/shard_map/ppermute | solution.py:925
  (75 other events, 655.6 us)
Sparse Core Ops, SparseCore 0:
  10.4 31.1 all-gather.4
  43.7 45.4 all-gather.6

commit v2 on v1

--- a/solution.py
+++ b/solution.py
@@ -420,23 +420,6 @@
     )
 
 
-def plain_order_kernel(info_ref, in_ref, out_ref):
-    out_ref[...] = permuted(in_ref, info_ref, BLOCKS)
-
-
-def plain_order(info, values):
-    return call(
-        plain_order_kernel,
-        info,
-        (values,),
-        (1,),
-        [kept(*values.shape)],
-        [kept(*values.shape)],
-        [shaped(f32, *values.shape)],
-        "plain_order",
-    )[0]
-
-
 def finish_kernel(count, info_ref, *refs):
     in_refs, row_ref, out_ref = refs[:count], refs[count], refs[-1]
     frames = in_refs[0].shape[0]
@@ -499,7 +482,7 @@
 
 
 def project_kernel(
-    info_ref, x_ref, msg_ref, gain_ref, shift_ref, bq_ref, bv_ref, *refs
+    info_ref, x_ref, msg_ref, rel_ref, bias_ref, *refs
 ):
     a_refs, b_refs, (q_ref, k_ref, v_ref, h_ref) = refs[:4], refs[4:8], refs[8:]
     frames = x_ref.shape[0]
@@ -508,13 +491,13 @@
     def _():
         for f in range(frames):
             rows = with_message(x_ref, msg_ref, info_ref, f)
-            normed = norm_rows(rows, gain_ref[...], shift_ref[...])[0].astype(bf16)
+            normed = norm_rows(rows, rel_ref[0:1], rel_ref[1:2])[0].astype(bf16)
             h_ref[pl.ds(f * ROWS, ROWS)] = normed
 
     for out_ref, weights, bias in (
-        (q_ref, halves(a_refs, 0, 0, 0), bq_ref[...]),
+        (q_ref, halves(a_refs, 0, 0, 0), bias_ref[10:11]),
         (k_ref, halves(a_refs, 0, 0, 1), 0.0),
-        (v_ref, halves(b_refs, 1, 0, 0), bv_ref[...]),
+        (v_ref, halves(b_refs, 1, 0, 0), bias_ref[11:12]),
     ):
         rows = dot(h_ref[...], jnp.concatenate(weights, 0)) + bias
         for f in range(frames):
@@ -524,16 +507,17 @@
 def project(info, x, message, vec_rel, vectors, attn):
     frames = x.shape[0]
     n, z, _, part, width = attn[0].shape
-    bias = pl.BlockSpec((1, width), lambda j, info_ref: (0, j))
+    columns = vectors.shape[0]
+    bias = pl.BlockSpec((columns, width), lambda j, info_ref: (0, j))
     a_spec = pl.BlockSpec((n, 1, 2, part, width), lambda j, info_ref: (0, j, 0, 0, 0))
     b_spec = pl.BlockSpec((n, 1, 1, part, width), lambda j, info_ref: (0, j, 0, 0, 0))
     out = pl.BlockSpec((frames, ROWS, width), lambda j, info_ref: (0, 0, j))
     return call(
         project_kernel,
         info,
-        (x, message, vec_rel[0:1], vec_rel[1:2], vectors[10:11], vectors[11:12], *attn),
+        (x, message, vec_rel, vectors, *attn),
         (z,),
-        [once(frames, ROWS, D), once(FRAMES, D), once(1, D), once(1, D), bias, bias]
+        [once(frames, ROWS, D), once(FRAMES, D), once(columns, D), bias]
         + [a_spec] * 4
         + [b_spec] * 4,
         [out] * 3 + [kept(frames * ROWS, D)],
@@ -848,8 +832,8 @@
     )
 
 
-def message_backward_kernel(info_ref, dmsg_ref, first_ref, pack_ref, vec_ref, *refs):
-    weights, (class_ref, sent_ref, sums_ref, hold_ref) = refs[:8], refs[8:]
+def message_backward_kernel(info_ref, dmsg_ref, table_ref, cls_ref, first_ref, pack_ref, vec_ref, *refs):
+    weights, (class_ref, sent_ref, hold_ref, rows_ref) = refs[:8], refs[8:]
     frames = dmsg_ref.shape[1]
     for i in range(dmsg_ref.shape[0]):
         place = lax.bitwise_xor(info_ref[2 * BLOCKS], i)
@@ -881,25 +865,38 @@
     dfirst = (dmsg + back).astype(bf16)
     class_ref[...] = message_times_t(dfirst, weights, 0)
     sent = [rows.astype(f32) for rows in (dfirst, dq, dk, dv, dmsg)]
-    for i, rows in enumerate(sent):
-        sent_ref[i] = rows
+    hold_ref[...] = jnp.zeros_like(hold_ref)
+    hold_ref[0:TABLE_REL] = table_ref[0:TABLE_REL]
+    table = permuted(hold_ref, info_ref, BLOCKS)
+    rows_ref[...] = jnp.zeros_like(rows_ref)
+    for i, rows in enumerate([cls_ref[...], pack_ref[0], pack_ref[1]] + sent):
+        rows_ref[i * FRAMES : (i + 1) * FRAMES] = rows
     sums = [grad * scaled, grad, sent[0], sent[1], sent[3], dmsg]
-    sums_ref[...] = jnp.concatenate([jnp.sum(rows, 0, keepdims=True) for rows in sums], 0)
-
-
-def message_backward(info, dmsg, first, pack, vectors, weights):
+    sums = [jnp.sum(rows, 0, keepdims=True) for rows in sums]
+    here = [table[i : i + 1] for i in range(TABLE_REL)]
+    given = [table_ref[i : i + 1] for i in range(TABLE_REL, table_ref.shape[0])]
+    for i, row in enumerate(here[:4] + sums + given[:2] + here[4:] + given[2:]):
+        rows_ref[8 * FRAMES + i : 8 * FRAMES + i + 1] = row
+    sent_ref[...] = rows_ref[...].astype(bf16)
+
+
+TABLE_REL = 6
+SENT_ROWS = 96
+
+
+def message_backward(info, dmsg, table, class_rows, first, pack, vectors, weights):
     one = kept(FRAMES, D)
     return call(
         message_backward_kernel,
         info,
-        (dmsg, first, pack, vectors, *weights),
+        (dmsg, table, class_rows, first, pack, vectors, *weights),
         (1,),
-        [kept(*dmsg.shape), one, kept(*pack.shape), kept(*vectors.shape)]
+        [kept(*dmsg.shape), kept(*table.shape), one, one, kept(*pack.shape), kept(*vectors.shape)]
         + [once(*w.shape) for w in weights],
-        [one, kept(5, FRAMES, D), kept(6, D)],
-        [shaped(f32, FRAMES, D), shaped(f32, 5, FRAMES, D), shaped(f32, 6, D)],
+        [one, kept(SENT_ROWS, D)],
+        [shaped(f32, FRAMES, D), shaped(bf16, SENT_ROWS, D)],
         "message_backward",
-        [pltpu.VMEM((FRAMES, D), f32)],
+        [pltpu.VMEM((FRAMES, D), f32), pltpu.VMEM((SENT_ROWS, D), f32)],
         10 * FRAMES * D * D,
     )
 
@@ -1118,11 +1115,19 @@
         self.arrived = swap(self.going, "tensor", 1)
 
     def step(self):
-        if self.direct:
-            return self.held
-        self.held, going = add_and_single(self.info, self.held, self.arrived)
-        self.arrived = swap(going, "tensor", 2)
-        return going
+        self.add()
+        return self.send()
+
+    def add(self):
+        if not self.direct:
+            self.held, self.going = add_and_single(self.info, self.held, self.arrived)
+        return self.held, self.going
+
+    def send(self, *earlier):
+        if not self.direct:
+            self.going = after(self.going, *earlier) if earlier else self.going
+            self.arrived = swap(self.going, "tensor", 2)
+        return self.going
 
     def result(self):
         return add_low(self.held, self.arrived).reshape((-1,) + self.shape[1:])
@@ -1130,20 +1135,32 @@
 
 class GatherSmall:
     def __init__(self, values):
-        self.values, self.bits = values[None], [2, 4, 1]
+        half = values.shape[0] // 2
+        self.bits = [(2, 4), (4, 2), (1, 1)]
         if relative_order():
-            self.arrived = swap(self.values, "dp", 2)
+            self.values = [values[None, :half], values[None, half:]]
+            self.send()
         else:
-            self.values = self.arrived = lax.all_gather(values, "dp", axis=0)
+            self.values = self.arrived = [lax.all_gather(values, "dp", axis=0)]
+
+    def send(self):
+        self.arrived = [swap(v, "dp", bit) for v, bit in zip(self.values, self.bits[0])]
 
     def step(self):
+        if relative_order():
+            pairs = zip(self.values, self.arrived)
+            self.values = [jnp.concatenate(pair, 0) for pair in pairs]
+            self.bits = self.bits[1:]
+            if self.bits:
+                self.send()
+        return self.values
+
+    def result(self):
         if not relative_order():
-            return self.values
-        self.values = jnp.concatenate([self.values, self.arrived], 0)
-        self.bits = self.bits[1:]
-        if self.bits:
-            self.arrived = swap(self.values, "dp", self.bits[0])
-        return self.values
+            return self.values[0]
+        first, second = self.values
+        order = (0, 2, 1, 3, 4, 6, 5, 7)
+        return jnp.concatenate([first, jnp.stack([second[i] for i in order])], 1)
 
 
 def sum_everywhere(values):
@@ -1159,14 +1176,23 @@
     return values
 
 
-def gather_and_sum_videos(values, sums):
-    values, count = values[None], sums.shape[0]
-    for bit in bits_of("tensor"):
-        rows = jnp.concatenate([sums, values.reshape(-1, D)], 0)
-        arrived = swap(rows, "tensor", bit)
-        sums = sums + arrived[:count]
-        values = jnp.concatenate([values, arrived[count:].reshape(values.shape)], 0)
-    return values, sums
+class VideoRows:
+    def __init__(self, values, sums):
+        self.values, self.sums, self.bits = values[None], sums, bits_of("tensor")
+        self.send()
+
+    def send(self):
+        rows = jnp.concatenate([self.sums, self.values.reshape(-1, D)], 0)
+        self.arrived = swap(rows, "tensor", self.bits[0])
+
+    def step(self):
+        count = self.sums.shape[0]
+        self.sums = self.sums + self.arrived[:count]
+        others = self.arrived[count:].reshape(self.values.shape)
+        self.values = jnp.concatenate([self.values, others], 0)
+        self.bits = self.bits[1:]
+        if self.bits:
+            self.send()
 
 
 def adam_step(weight, first_moment, second_moment, gradient, factor, step_rate, decay_rate):
@@ -1235,15 +1261,15 @@
     beside(sent_attn, msg_go)
     sent_msg = msg_go.step()
     mlp_z = after(mlp_z, *sent_msg)
-    mlp_go = [
-        Gather(*[mlp_z[:, i, :, j * half_ff : (j + 1) * half_ff] for i in range(2)])
-        for j in range(2)
+    mlp_half = [
+        [mlp_z[:, i, :, j * half_ff : (j + 1) * half_ff] for i in range(2)] for j in range(2)
     ]
+    mlp_go = [Gather(*mlp_half[0])]
     msg_w = msg_go.result()
     vec_rel = jnp.concatenate(msg_w[:4], 0)[:, 5 * part : 5 * part + vec_count, :part]
     vec_rel = jnp.moveaxis(vec_rel, 0, 1).reshape(-1, D).astype(f32)
 
-    sent_mlp = mlp_go[0].own + mlp_go[1].own
+    sent_mlp = mlp_go[0].own + mlp_half[1]
     vectors, message, first_msg, msg_pack = beside(
         message_forward(info, after(class_rows, *sent_mlp).astype(f32), vec_rel, msg_w), attn_go
     )
@@ -1251,15 +1277,18 @@
     attn_go.step()
     attn_w = attn_go.result()
     projected = project(info, x, message, vec_rel, vectors, attn_w)
-    queries, key_rows, value_rows, normed = beside(projected, *mlp_go)
+    queries, key_rows, value_rows, normed = beside(projected, mlp_go[0])
     sent_mlp = mlp_go[0].step()
     attended, totals = beside(
         attend_forward(after(queries, *sent_mlp), key_rows, value_rows), mlp_go[0]
     )
-    sent_mlp = mlp_go[0].step() + mlp_go[1].step()
+    sent_mlp = mlp_go[0].step()
+    mlp_go.append(Gather(*after(mlp_half[1], attended)))
     middle, n2, n2_t = beside(
-        combine(info, x, after(attended, *sent_mlp), vec_rel, attn_w), mlp_go[0]
-    )
+        combine(info, x, after(attended, *sent_mlp), vec_rel, attn_w), *mlp_go
+    )
+    sent_mlp = mlp_go[1].step()
+    n2 = after(n2, *sent_mlp)
 
     def feed(j, n2):
         return feed_forward(n2, n2_t, grads, grads_t, ff_bias[:, j], mlp_go[j].result())
@@ -1312,32 +1341,47 @@
     ).reshape(FF // D, D)
     table = jnp.concatenate([sums_one, sums_two, grad_sum, sum_q, sum_v, ff_bias_grad], 0)
     dmsg = dmsg[:, 0].astype(bf16).astype(f32)
-    dmsg, table = gather_and_sum_videos(after(dmsg, *going), table)
-    mlp_go.arrived = after(mlp_go.arrived, dmsg)
-    sent_mlp = mlp_go.step()
-    dmsg = beside(after(dmsg, sent_mlp), sums_attn)
+    rows = VideoRows(after(dmsg, *going), table)
+    mlp_go.held, mlp_go.going = beside(mlp_go.add(), rows)
+    rows.step()
+    rows.arrived = after(rows.arrived, mlp_go.going)
+    rows.step()
+    sent_mlp = mlp_go.send(rows.values)
+    dmsg = beside(after(rows.values, sent_mlp), sums_attn)
     attn_go = ScatterVideos(info, sums_attn)
-    grad_class, sent, sums_msg = beside(
-        message_backward(info, after(dmsg, attn_go.going), first_msg, msg_pack, vectors, msg_w),
+    grad_class, sent = beside(
+        message_backward(
+            info,
+            after(dmsg, attn_go.going),
+            rows.sums,
+            class_rows.astype(f32),
+            first_msg,
+            msg_pack,
+            vectors,
+            msg_w,
+        ),
         attn_go,
         mlp_go,
     )
     mlp_sum = mlp_go.result()
     going = attn_go.step()
 
-    plain = plain_order(info, table[:6])
-    table = jnp.concatenate([plain[:4], sums_msg, table[6:8], plain[4:], table[8:]], 0)
-    sent = jnp.concatenate([msg_pack[:2], sent], 0).astype(bf16).reshape(7 * FRAMES, D)
-    sent = jnp.concatenate([class_rows, sent, table.astype(bf16)], 0)
     small = GatherSmall(after(sent, going))
     input_grad = beside(
-        finish(info, [after(ing, small.values)], grad_class, "input_grad"), small, attn_go
+        finish(info, [after(ing, *small.values)], grad_class, "input_grad"), small, attn_go
     )
     small.step()
     attn_grad = attn_go.result()
+    mlp_grad = jnp.concatenate([mlp_sum[:2], mlp_sum[2:]], 2)
+    mlp_grad = jnp.swapaxes(mlp_grad, 0, 1).astype(f32)
+    attn_grad = jnp.swapaxes(attn_grad.reshape(4, part, local_width), 0, 1).astype(f32)
+    squares = jnp.sum(attn_grad * attn_grad) + jnp.sum(mlp_grad * mlp_grad)
+    squares = beside(squares, small)
     small.step()
-    everyone = small.step()
-    tables = lax.dynamic_slice_in_dim(everyone[:, 8 * FRAMES :], dp_index * part, part, 2)
+    small.step()
+    everyone = small.result()
+    tables = everyone[:, 8 * FRAMES : 8 * FRAMES + vec_count]
+    tables = lax.dynamic_slice_in_dim(tables, dp_index * part, part, 2)
     vec_grad = jnp.sum(tables.astype(f32), 0).T
     everyone = everyone[:, : 8 * FRAMES].reshape(-1, 8, FRAMES, D)
     everyone = jnp.moveaxis(everyone, 0, 1).reshape(8, -1, D)
@@ -1353,15 +1397,9 @@
         1,
     )
 
-    attn_grad = jnp.swapaxes(attn_grad.reshape(4, part, local_width), 0, 1).astype(f32)
-    mlp_grad = jnp.concatenate([mlp_sum[:2], mlp_sum[2:]], 2)
-    mlp_grad = jnp.swapaxes(mlp_grad, 0, 1).astype(f32)
-
     keep_share = (z_index == 0).astype(f32)
-    squares = (
-        jnp.sum(attn_grad * attn_grad)
-        + jnp.sum(mlp_grad * mlp_grad)
-        + keep_share * (jnp.sum(msg_grad * msg_grad) + jnp.sum(vec_grad * vec_grad))
+    squares = squares + keep_share * (
+        jnp.sum(msg_grad * msg_grad) + jnp.sum(vec_grad * vec_grad)
     )
     squares = sum_everywhere(jnp.broadcast_to(squares, (8, 128)))[0, 0]
     grad_norm = jnp.sqrt(squares)

time: 544 us -> 536 us (0.985)
  waiting for transfers between devices: 88.5 us -> 82.5 us
    ppermute x66 -> x69, waiting for transfers between devices: 81.1 us -> 74.1 us  [swap(): return lax.ppermute(values, axis, pairs)]
    ppermute x66 -> x69, starting transfers between devices: 55.6 us -> 60.2 us  [swap(): return lax.ppermute(values, axis, pairs)]
    pallas_call x16 -> x15, Pallas kernels: 139 us -> 137 us  [call(): pl.pallas_call(kernel, grid_spec=pltpu.PrefetchScalarGridSpec(num_scalar_...]
    unnamed x145 -> x154, local copies, waits for them, and re-layouts: 24.9 us -> 23.7 us
  transfers between devices with their start and end apart: 68 -> 71, of which waited for: 23 -> 26; matrix products, arithmetic and copies ran while one was open for 4% -> 4% of each run, Pallas kernels for 55% -> 55%
where the time goes in v2:
time: 536 us; the launch traced here: 528 us
  Pallas kernels  297 us (55%)
  waiting for transfers between devices  82.5 us (15%)
  starting transfers between devices  60.2 us (11%)
  local copies, waits for them, and re-layouts  35.1 us (7%)
  other arithmetic  31.1 us (6%)
  between operations  20.3 us (4%)
    pallas_call x15, Pallas kernels, call(): pl.pallas_call(kernel, grid_spec=pltpu.PrefetchScalarGridSpec(num_scalar_...  137 us
    pallas_call x2, Pallas kernels, feed_forward(): pl.pallas_call(feed_kernel, grid=(steps,), in_specs=[pl.BlockSpec((frames...  81 us
    ppermute x69, waiting for transfers between devices, swap(): return lax.ppermute(values, axis, pairs)  74.1 us
    ppermute x69, starting transfers between devices, swap(): return lax.ppermute(values, axis, pairs)  60.2 us
    pallas_call x2, Pallas kernels, attend_backward(): pl.pallas_call(attend_backward_kernel, grid=(frames,), in_specs=[spec] *...  40 us
    unnamed x154, local copies, waits for them, and re-layouts  23.7 us
    pallas_call x6, Pallas kernels, add_and_split(): pl.pallas_call(functools.partial(add_kernel, axes), grid=(steps,), in_spe...  18.9 us
    pallas_call x1, Pallas kernels, attend_forward(): pl.pallas_call(attend_forward_kernel, grid=(frames,), in_specs=[spec] * 3...  18.5 us
  transfers between devices with their start and end apart: 71, of which 26 were waited for; matrix products, arithmetic and copies ran while one was open for 4% of the time, Pallas kernels for 55%

profile of v2, /device:TPU:0, one launch (start us, length us, event | category | flops | bytes accessed | tf_op | source)
XLA Modules:
  0.0 527.7 jit_solution(5076964805764270759)
XLA Ops:
  10.2 1.9 convert_element_type.83
  12.3 3.0 collective-permute-start
  15.3 1.5 collective-permute-start.1
  18.6 8.6 %prepare.1 = (bf16[2,592,1024]{2,1,0:T(8,128)(2,1)}, bf16[2,592,1024]{2,1,0:T(8,128)(2,1)}, bf16[1024,1280]{1,0:T(8,128)(2,1)}, f32[1,1024]{1,0:T(1,128)}) custom-call(s32[17]{0:T(128)} %pad_add_fusion.info_ref, bf16[1154,1024]{1,0:T(8,128)(2,1)} %tokens_ref.1, bf16[1154,1024]{1,0:T(8,128)(2,1)} %cot_ref.1), custom_call_target="tpu_custom_call" | custom-call | bytes 762624 | tf_op jit(solution)/shard_map/prepare/pallas_call | solution.py:334
  27.2 4.3 collective-permute-done.1.refs_3_
  36.6 1.5 collective-permute-start.4
  38.6 2.8 all-gather.5.cloned.1.call-done
  42.8 1.5 collective-permute-start.2
  44.4 1.5 collective-permute-start.3
  45.9 32.8 %collective-permute-done.2 = bf16[4,2,128,256]{3,2,1,0:T(8,128)(2,1)S(1)} collective-permute-done((bf16[4,2,128,256]{3,2,1,0:T(8,128)(2,1)S(1)}, bf16[4,2,128,256]{3,2,1,0:T(8,128)(2,1)S(1)}, u32[]{:S(2)}, u32[]{:S(2)}) %collective-permute-start.2) | collective-permute-done | bytes 524320 | tf_op jit(solution)/shard_map/ppermute | solution.py:922
  79.7 1.5 collective-permute-start.10
  83.5 5.6 %all-gather.7.cloned.1.call-done = bf16[8,128,1024]{2,1,0:T(8,128)(2,1)} async-done(((bf16[2,128,1024]{2,1,0:T(8,128)(2,1)}), bf16[8,128,1024]{2,1,0:T(8,128)(2,1)}) %all-gather.7.cloned.1.call-update) | async-done | bytes 2097168 | tf_op jit(solution)/shard_map/all_gather | solution.py:1247
  89.1 2.9 fusion.30
  94.2 8.0 %message_forward.1 = (f32[18,1024]{1,0:T(8,128)}, f32[8,1024]{1,0:T(8,128)}, f32[8,1024]{1,0:T(8,128)}, f32[5,8,1024]{2,1,0:T(8,128)}) custom-call(s32[17]{0:T(128)} %pad_add_fusion.info_ref, f32[8,1024]{1,0:T(8,128)} %convert_element_type.90.cls_ref, f32[18,1024]{1,0:T(8,128)} %bitcast.241, bf16[2,672,512]{2,1,0:T(8,128)(2,1)} %copy-done.4, ...), custom_call_target="tpu_custom_call" | custom-call | flops 5242880 | bytes 697344 | tf_op jit(solution)/shard_map/message_forward/pallas_call | solution.py:334
  102.2 3.2 collective-permute-done.10.refs_1_
  108.2 2.8 collective-permute-done.13.refs_3_
  112.0 14.6 %project.1 = (bf16[2,592,1024]{2,1,0:T(8,128)(2,1)}, bf16[2,592,1024]{2,1,0:T(8,128)(2,1)}, bf16[2,592,1024]{2,1,0:T(8,128)(2,1)}, bf16[1184,1024]{1,0:T(8,128)(2,1)}) custom-call(s32[17]{0:T(128)} %pad_add_fusion.info_ref, bf16[2,592,1024]{2,1,0:T(8,128)(2,1)} %get-tuple-element.423.x_ref, f32[8,1024]{1,0:T(8,128)} %get-tuple-element.272.msg_ref, ...), custom_call_target="tpu_custom_call" | custom-call | flops 465567744 | bytes 1293312 | tf_op jit(solution)/shard_map/project/pallas_call | solution.py:334
  128.7 1.7 copy-done
  130.4 18.5 %attend_forward.1 = (bf16[2,592,1024]{2,1,0:T(8,128)(2,1)S(1)}, f32[2,8,2,592]{3,2,1,0:T(2,128)S(1)}) custom-call(bf16[2,592,1024]{2,1,0:T(8,128)(2,1)S(1)} %copy-done, bf16[2,592,1024]{2,1,0:T(8,128)(2,1)} %get-tuple-element.286.k_ref, bf16[2,592,1024]{2,1,0:T(8,128)(2,1)} %get-tuple-element.287.v_ref), custom_call_target="tpu_custom_call" | custom-call | flops 358875136 | bytes 1212416 | tf_op jit(solution)/shard_map/attend_forward/pallas_call | solution.py:192
  150.3 1.9 collective-permute-done.18.refs_1_
  155.0 1.5 slice_bitcast_fusion.16
  156.6 10.1 %combine.1 = (f32[2,592,1024]{2,1,0:T(8,128)}, bf16[2,592,1024]{2,1,0:T(8,128)(2,1)}, bf16[1024,1280]{1,0:T(8,128)(2,1)}) custom-call(s32[17]{0:T(128)} %pad_add_fusion.info_ref, bf16[2,592,1024]{2,1,0:T(8,128)(2,1)} %get-tuple-element.423.x_ref, bf16[2,592,1024]{2,1,0:T(8,128)(2,1)} %copy-done.5, f32[1,1024]{1,0:T(1,128)} %get-tuple-element.521.bias_ref, ...), custom_call_target="tpu_custom_call" | custom-call | flops 155189248 | bytes 1184512 | tf_op jit(solution)/shard_map/combine/pallas_call | solution.py:334
  169.0 1.5 collective-permute-start.27
  172.5 40.5 %feed_forward.2 = (f32[2,592,1024]{2,1,0:T(8,128)}, f32[2,592,1024]{2,1,0:T(8,128)}, bf16[4,4,128,512]{3,2,1,0:T(8,128)(2,1)}, bf16[4,4,128,512]{3,2,1,0:T(8,128...) custom-call(bf16[2,592,1024]{2,1,0:T(8,128)(2,1)} %get-tuple-element.330.n2_ref, ...), custom_call_target="tpu_custom_call" | custom-call | flops 1862270976 | bytes 2260992 | tf_op jit(solution)/shard_map/feed_forward/pallas_call | solution.py:288
  213.6 3.9 transposed.1.ht_ref
  219.9 40.6 %feed_forward.3 = (f32[2,592,1024]{2,1,0:T(8,128)}, f32[2,592,1024]{2,1,0:T(8,128)}, bf16[4,4,128,512]{3,2,1,0:T(8,128)(2,1)}, bf16[4,4,128,512]{3,2,1,0:T(8,128...) custom-call(bf16[2,592,1024]{2,1,0:T(8,128)(2,1)} %get-tuple-element.330.n2_ref, ...), custom_call_target="tpu_custom_call" | custom-call | flops 1862270976 | bytes 2260992 | tf_op jit(solution)/shard_map/feed_forward/pallas_call | solution.py:288
  261.8 4.9 add.268
  268.0 18.6 %between.1 = (bf16[2,592,1024]{2,1,0:T(8,128)(2,1)}, bf16[2,592,1024]{2,1,0:T(8,128)(2,1)}, bf16[4,4,128,256]{3,2,1,0:T(8,128)(2,1)}, bf16[4,4,128,256]{3,2,1,0:T(8,128)(2,1)}, f32[3,1024]{1,0:T(4,128)}) custom-call(s32[17]{0:T(128)} %pad_add_fusion.info_ref, f32[2,592,1024]{2,1,0:T(8,128)} %get-tuple-element.352.ea_ref, ...), custom_call_target="tpu_custom_call" | custom-call | flops 310378496 | bytes 1909760 | tf_op jit(solution)/shard_map/between/pallas_call | solution.py:334
  286.5 4.1 add.269
  292.1 1.5 collective-permute-start.41
  293.6 20.1 %attend_backward.2 = (bf16[2,592,1024]{2,1,0:T(8,128)(2,1)S(1)}, bf16[2,592,1024]{2,1,0:T(8,128)(2,1)S(1)}, bf16[2,592,1024]{2,1,0:T(8,128)(2,1)}) custom-call(bf16[2,592,1024]{2,1,0:T(8,128)(2,1)} %get-tuple-element.285.q_ref, bf16[2,592,1024]{2,1,0:T(8,128)(2,1)} %get-tuple-element.286.k_ref, bf16[2,592,1024]{2,1,0:T(8,128)(2,1)} %get-tuple-element.287.v_ref, ...), custom_call_target="tpu_custom_call" | custom-call | flops 358875136 | bytes 1212416 | tf_op jit(solution)/shard_map/attend_backward/pallas_call | solution.py:212
  314.6 1.7 add.270
  317.6 19.8 %attend_backward.3 = (bf16[2,592,1024]{2,1,0:T(8,128)(2,1)S(1)}, bf16[2,592,1024]{2,1,0:T(8,128)(2,1)S(1)}, bf16[2,592,1024]{2,1,0:T(8,128)(2,1)}) custom-call(bf16[2,592,1024]{2,1,0:T(8,128)(2,1)} %get-tuple-element.285.q_ref, bf16[2,592,1024]{2,1,0:T(8,128)(2,1)} %get-tuple-element.286.k_ref, ...), custom_call_target="tpu_custom_call", output_to_operand_aliasing={{0}: (5, {}), {1}: (6, {}), {2}: (7, {})} | custom-call | flops 358875136 | bytes 1212416 | tf_op jit(solution)/shard_map/attend_backward/pallas_call | solution.py:212
  338.9 2.4 add.271
  344.3 1.5 collective-permute-start.43
  345.7 13.7 %project_grads.1 = (bf16[4,4,2,128,256]{4,3,2,1,0:T(8,128)(2,1)}, bf16[4,4,2,128,256]{4,3,2,1,0:T(8,128)(2,1)}, bf16[4,4,2,128,256]{4,3,2,1,0:T(8,128)(2,1)}, bf...) custom-call(s32[17]{0:T(128)} %pad_add_fusion.info_ref, ...), custom_call_target="tpu_custom_call" | custom-call | flops 465567744 | bytes 1274368 | tf_op jit(solution)/shard_map/project_grads/pallas_call | solution.py:334
  360.4 4.2 add_and_pair.2
  364.6 1.5 collective-permute-start.48
  366.1 9.9 %block_output.1 = f32[1154,1024]{1,0:T(8,128)} custom-call(s32[17]{0:T(128)} %pad_add_fusion.info_ref, f32[2,592,1024]{2,1,0:T(8,128)} %get-tuple-element.411.mid_ref.refs_0_, f32[2,592,1024]{2,1,0:T(8,128)} %get-tuple-element.412.refs_1_, f32[2,592,1024]{2,1,0:T(8,128)} %get-tuple-element.413.refs_2_, f32[1,1024]{1,0:T(1,128)} %get-tuple-element.518.refs_3_), custom_call_target="tpu_custom_call" | custom-call | bytes 1204992 | tf_op jit(solution)/shard_map/block_output/pallas_call | solution.py:334
  378.0 4.2 add.272
  383.6 19.0 %project_back.1 = (f32[2,592,1024]{2,1,0:T(8,128)}, f32[2,1,1024]{2,1,0:T(1,128)}, f32[2,1024]{1,0:T(2,128)}) custom-call(s32[17]{0:T(128)} %pad_add_fusion.info_ref, bf16[2,592,1024]{2,1,0:T(8,128)(2,1)} %get-tuple-element.423.x_ref, f32[8,1024]{1,0:T(8,128)} %get-tuple-element.272.msg_ref, bf16[2,592,1024]{2,1,0:T(8,128)(2,1)} %get-tuple-element.424.dmid_ref, ...), custom_call_target="tpu_custom_call" | custom-call | flops 465567744 | bytes 1588480 | tf_op jit(solution)/shard_map/project_back/pallas_call | solution.py:334
  402.7 4.2 collective-permute-done.46.refs_1_
  408.2 1.7 add.273
  414.3 3.3 add_and_single.2
  417.6 2.6 collective-permute-start.50
  420.3 2.6 collective-permute-done.50
  423.5 2.6 collective-permute-start.54
  427.1 3.2 add_and_pair.3
  430.3 2.1 collective-permute-start.53
  433.7 9.1 %message_backward.1 = (f32[8,1024]{1,0:T(8,128)}, bf16[96,1024]{1,0:T(8,128)(2,1)}) custom-call(s32[17]{0:T(128)} %pad_add_fusion.info_ref, f32[4,2,1024]{2,1,0:T(2,128)} %pad_maximum_fusion.12.dmsg_ref, f32[12,1024]{1,0:T(8,128)} %slice_add_fusion.table_ref, f32[8,1024]{1,0:T(8,128)} %convert_element_type.97.cls_ref, ...), custom_call_target="tpu_custom_call" | custom-call | flops 5242880 | bytes 710144 | tf_op jit(solution)/shard_map/message_backward/pallas_call | solution.py:334
  442.8 3.7 collective-permute-done.54
  446.6 4.2 collective-permute-done.53.ao_ref.ap_ref
  451.5 2.7 add_and_single.3
  454.2 1.6 collective-permute-start.57
  461.4 8.0 %input_grad.1 = f32[1154,1024]{1,0:T(8,128)} custom-call(s32[17]{0:T(128)} %pad_add_fusion.info_ref, f32[2,592,1024]{2,1,0:T(8,128)} %get-tuple-element.469.refs_0_, f32[8,1024]{1,0:T(8,128)} %get-tuple-element.470.refs_1_), custom_call_target="tpu_custom_call" | custom-call | bytes 600576 | tf_op jit(solution)/shard_map/input_grad/pallas_call | solution.py:334
  469.4 2.6 multiply_reduce_fusion.1
  475.8 1.9 collective-permute-done.58
  490.4 2.4 collective-permute-done.65
  494.0 3.6 collective-permute-start.68
  497.6 1.8 collective-permute-done.68
  499.4 1.8 collective-permute-done.66
  502.6 7.9 %multiply_add_fusion = (f32[128,5,1024]{2,0,1:T(8,128)}, f32[128,5,1024]{2,0,1:T(8,128)}, f32[128,5,1024]{2,0,1:T(8,128)}, f32[128,5,1024]{2,0,1:T(8,128)}) fusion(f32[128,5,1024]{2,0,1:T(8,128)} %param.31, f32[128,5,1024]{2,0,1:T(8,128)} %param.28, f32[128,5,1024]{2,0,1:T(8,128)S(1)} %fusion.2, f32[]{:T(128)S(6)} %div.81, f32[128,5,1024]{2,0,1:T(8,128)} %param.30, ...), kind=kLoop, calls=%fused_computation.2 | loop fusion | flops 12451840 | bytes 23592964 | tf_op jit(solution)/shard_map/add | solution.py:1410
  511.3 2.3 multiply_add_fusion.4
  513.6 5.7 %multiply_add_fusion.2 = (f32[128,2,1024]{2,1,0:T(2,128)}, f32[128,2,1024]{2,1,0:T(2,128)}, f32[128,2,1024]{2,1,0:T(2,128)}, f32[128,2,1024]{2,1,0:T(2,128)}) fusion(f32[128,2,1024]{2,1,0:T(2,128)S(1)} %copy-done.40, f32[128,2,1024]{2,1,0:T(2,128)S(1)} %copy-done.26, f32[128,2,1024]{2,1,0:T(2,128)S(1)} %copy-done.27, f32[]{:T(128)S(6)} %div.81, ...), kind=kLoop, calls=%fused_computation.28 | loop fusion | flops 4980736 | bytes 9437188 | tf_op jit(solution)/shard_map/add | solution.py:1410
  (335 shorter events, 80.7 us)
Async XLA Ops:
  7.2 34.3 %all-gather.5.cloned.1.call-start = ((), (), s32[]{:S(2)}) async-start(), calls=%async_computation | async-start | bytes 1351680 | tf_op jit(solution)/shard_map/all_gather | solution.py:1246
  10.1 78.9 %all-gather.7.cloned.1.call-start = ((), (), s32[]{:S(2)}) async-start(), calls=%async_computation.1 | async-start | bytes 2621440 | tf_op jit(solution)/shard_map/all_gather | solution.py:1247
  12.3 20.0 %collective-permute-start = (bf16[672,512]{1,0:T(8,128)(2,1)S(1)}, bf16[672,512]{1,0:T(8,128)(2,1)S(1)}, u32[]{:S(2)}, u32[]{:S(2)}) collective-permute-start(bf16[672,512]{1,0:T(8,128)(2,1)S(1)} %fusion.9.refs_0_), channel_id=1, source_target_pairs={{0,8},{4,12},{8,0},{12,4},{16,24},{20,28},{24,16},{28,20},{1,9},{5... | collective-permute-start | bytes 2064392 | tf_op jit(solution)/shard_map/ppermute | solution.py:922
  15.3 16.2 %collective-permute-start.1 = (bf16[640,512]{1,0:T(8,128)(2,1)S(1)}, bf16[640,512]{1,0:T(8,128)(2,1)S(1)}, u32[]{:S(2)}, u32[]{:S(2)}) collective-permute-start(bf16[640,512]{1,0:T(8,128)(2,1)S(1)} %get-tuple-element.509.refs_2_), channel_id=1, source_target_pairs={{0,16},{4,20},{8,24},{12,28},{16,0},{20,4},{24,8},{28,12},{1,17},{... | collective-permute-start | bytes 1966088 | tf_op jit(solution)/shard_map/ppermute | solution.py:922
  36.6 42.5 %collective-permute-start.4 = (bf16[2,672,512]{2,1,0:T(8,128)(2,1)S(1)}, bf16[2,672,512]{2,1,0:T(8,128)(2,1)}, u32[]{:S(2)}, u32[]{:S(2)}) collective-permute-start(bf16[2,672,512]{2,1,0:T(8,128)(2,1)S(1)} %get-tuple-element.259.refs_0_), channel_id=1, source_target_pairs={{0,16},{4,20},{8,24},{12,28},{16,0},{20,4},{24,8},{28,12},{1,17},{... | collective-permute-start | bytes 4128776 | tf_op jit(solution)/shard_map/ppermute | solution.py:922
  38.1 40.9 %collective-permute-start.5 = (bf16[2,640,512]{2,1,0:T(8,128)(2,1)}, bf16[2,640,512]{2,1,0:T(8,128)(2,1)}, u32[]{:S(2)}, u32[]{:S(2)}) collective-permute-start(bf16[2,640,512]{2,1,0:T(8,128)(2,1)} %get-tuple-element.260.refs_4_), channel_id=1, source_target_pairs={{0,8},{4,12},{8,0},{12,4},{16,24},{20,28},{24,16},{28,20},{1,9},{5... | collective-permute-start | bytes 3932168 | tf_op jit(solution)/shard_map/ppermute | solution.py:922
  38.6 42.5 %collective-permute-start.6 = (bf16[2,672,512]{2,1,0:T(8,128)(2,1)S(1)}, bf16[2,672,512]{2,1,0:T(8,128)(2,1)}, u32[]{:S(2)}, u32[]{:S(2)}) collective-permute-start(bf16[2,672,512]{2,1,0:T(8,128)(2,1)S(1)} %get-tuple-element.259.refs_0_), channel_id=1, source_target_pairs={{0,4},{4,0},{8,12},{12,8},{16,20},{20,16},{24,28},{28,24},{1,5},{5... | collective-permute-start | bytes 4128776 | tf_op jit(solution)/shard_map/ppermute | solution.py:922
  42.8 35.8 %collective-permute-start.2 = (bf16[4,2,128,256]{3,2,1,0:T(8,128)(2,1)S(1)}, bf16[4,2,128,256]{3,2,1,0:T(8,128)(2,1)S(1)}, u32[]{:S(2)}, u32[]{:S(2)}) collective-permute-start(bf16[4,2,128,256]{3,2,1,0:T(8,128)(2,1)S(1)} %get-tuple-element.512), channel_id=1, source_target_pairs={{0,8},{4,12},{8,0},{12,4},{16,24},{20,28},{24,16},{28,20},{1,9},{5... | collective-permute-start | bytes 1572872 | tf_op jit(solution)/shard_map/ppermute | solution.py:922
  44.4 34.3 %collective-permute-start.3 = (bf16[4,2,128,256]{3,2,1,0:T(8,128)(2,1)S(1)}, bf16[4,2,128,256]{3,2,1,0:T(8,128)(2,1)S(1)}, u32[]{:S(2)}, u32[]{:S(2)}) collective-permute-start(bf16[4,2,128,256]{3,2,1,0:T(8,128)(2,1)S(1)} %get-tuple-element.511), channel_id=1, source_target_pairs={{0,16},{4,20},{8,24},{12,28},{16,0},{20,4},{24,8},{28,12},{1,17},{... | collective-permute-start | bytes 1572872 | tf_op jit(solution)/shard_map/ppermute | solution.py:922
  79.1 15.0 %collective-permute-start.8 = (bf16[2,640,512]{2,1,0:T(8,128)(2,1)}, bf16[2,640,512]{2,1,0:T(8,128)(2,1)}, u32[]{:S(2)}, u32[]{:S(2)}) collective-permute-start(bf16[2,640,512]{2,1,0:T(8,128)(2,1)} %get-tuple-element.260.refs_4_), channel_id=1, source_target_pairs={{0,4},{4,0},{8,12},{12,8},{16,20},{20,16},{24,28},{28,24},{1,5},{5... | collective-permute-start | bytes 3932168 | tf_op jit(solution)/shard_map/ppermute | solution.py:922
  79.6 14.6 %collective-permute-start.9 = (bf16[2,640,512]{2,1,0:T(8,128)(2,1)}, bf16[2,640,512]{2,1,0:T(8,128)(2,1)}, u32[]{:S(2)}, u32[]{:S(2)}) collective-permute-start(bf16[2,640,512]{2,1,0:T(8,128)(2,1)} %collective-permute-done.5.refs_5_), channel_id=1, source_target_pairs={{0,4},{4,0},{8,12},{12,8},{16,20},{20,16},{24,28},{28,24},{1,5},{5... | collective-permute-start | bytes 3932168 | tf_op jit(solution)/shard_map/ppermute | solution.py:922
  79.7 25.6 %collective-permute-start.10 = (bf16[2,4,2,128,256]{4,3,2,1,0:T(8,128)(2,1)S(1)}, bf16[2,4,2,128,256]{4,3,2,1,0:T(8,128)(2,1)}, u32[]{:S(2)}, u32[]{:S(2)}) collective-permute-start(bf16[2,4,2,128,256]{4,3,2,1,0:T(8,128)(2,1)S(1)} %bitcast.171), channel_id=1, source_target_pairs={{0,16},{4,20},{8,24},{12,28},{16,0},{20,4},{24,8},{28,12},{1,17},{... | collective-permute-start | bytes 3145736 | tf_op jit(solution)/shard_map/ppermute | solution.py:922
  81.2 25.3 %collective-permute-start.11 = (bf16[2,4,2,128,256]{4,3,2,1,0:T(8,128)(2,1)S(1)}, bf16[2,4,2,128,256]{4,3,2,1,0:T(8,128)(2,1)}, u32[]{:S(2)}, u32[]{:S(2)}) collective-permute-start(bf16[2,4,2,128,256]{4,3,2,1,0:T(8,128)(2,1)S(1)} %bitcast.165), channel_id=1, source_target_pairs={{0,8},{4,12},{8,0},{12,4},{16,24},{20,28},{24,16},{28,20},{1,9},{5... | collective-permute-start | bytes 3145736 | tf_op jit(solution)/shard_map/ppermute | solution.py:922
  82.6 25.0 %collective-permute-start.12 = (bf16[2,4,2,128,256]{4,3,2,1,0:T(8,128)(2,1)S(1)}, bf16[2,4,2,128,256]{4,3,2,1,0:T(8,128)(2,1)}, u32[]{:S(2)}, u32[]{:S(2)}) collective-permute-start(bf16[2,4,2,128,256]{4,3,2,1,0:T(8,128)(2,1)S(1)} %bitcast.172), channel_id=1, source_target_pairs={{0,4},{4,0},{8,12},{12,8},{16,20},{20,16},{24,28},{28,24},{1,5},{5... | collective-permute-start | bytes 3145736 | tf_op jit(solution)/shard_map/ppermute | solution.py:922
  94.1 14.1 %collective-permute-start.14 = (bf16[2,4,2,128,256]{4,3,2,1,0:T(8,128)(2,1)S(1)}, bf16[2,4,2,128,256]{4,3,2,1,0:T(8,128)(2,1)S(1)}, u32[]{:S(2)}, u32[]{:S(2)}) collective-permute-start(bf16[2,4,2,128,256]{4,3,2,1,0:T(8,128)(2,1)S(1)} %bitcast.166), channel_id=1, source_target_pairs={{0,4},{4,0},{8,12},{12,8},{16,20},{20,16},{24,28},{28,24},{1,5},{5... | collective-permute-start | bytes 3145736 | tf_op jit(solution)/shard_map/ppermute | solution.py:922
  106.5 4.5 collective-permute-start.13
  106.5 4.5 collective-permute-start.15
  107.0 19.5 %collective-permute-start.16 = (bf16[4,128,512]{2,1,0:T(8,128)(2,1)}, bf16[4,128,512]{2,1,0:T(8,128)(2,1)S(1)}, u32[]{:S(2)}, u32[]{:S(2)}) collective-permute-start(bf16[4,128,512]{2,1,0:T(8,128)(2,1)} %get-tuple-element.504), channel_id=1, source_target_pairs={{0,8},{4,12},{8,0},{12,4},{16,24},{20,28},{24,16},{28,20},{1,9},{5... | collective-permute-start | bytes 1572872 | tf_op jit(solution)/shard_map/ppermute | solution.py:922
  107.6 19.0 %collective-permute-start.17 = (bf16[4,128,512]{2,1,0:T(8,128)(2,1)S(1)}, bf16[4,128,512]{2,1,0:T(8,128)(2,1)S(1)}, u32[]{:S(2)}, u32[]{:S(2)}) collective-permute-start(bf16[4,128,512]{2,1,0:T(8,128)(2,1)S(1)} %copy-done.55), channel_id=1, source_target_pairs={{0,16},{4,20},{8,24},{12,28},{16,0},{20,4},{24,8},{28,12},{1,17},{... | collective-permute-start | bytes 1572872 | tf_op jit(solution)/shard_map/ppermute | solution.py:922
  127.0 25.3 %collective-permute-start.18 = (bf16[2,4,128,512]{3,2,1,0:T(8,128)(2,1)S(1)}, bf16[2,4,128,512]{3,2,1,0:T(8,128)(2,1)S(1)}, u32[]{:S(2)}, u32[]{:S(2)}) collective-permute-start(bf16[2,4,128,512]{3,2,1,0:T(8,128)(2,1)S(1)} %bitcast.193), channel_id=1, source_target_pairs={{0,16},{4,20},{8,24},{12,28},{16,0},{20,4},{24,8},{28,12},{1,17},{... | collective-permute-start | bytes 3145736 | tf_op jit(solution)/shard_map/ppermute | solution.py:922
  127.6 24.9 %collective-permute-start.19 = (bf16[2,4,128,512]{3,2,1,0:T(8,128)(2,1)S(1)}, bf16[2,4,128,512]{3,2,1,0:T(8,128)(2,1)S(1)}, u32[]{:S(2)}, u32[]{:S(2)}) collective-permute-start(bf16[2,4,128,512]{3,2,1,0:T(8,128)(2,1)S(1)} %bitcast.196), channel_id=1, source_target_pairs={{0,8},{4,12},{8,0},{12,4},{16,24},{20,28},{24,16},{28,20},{1,9},{5... | collective-permute-start | bytes 3145736 | tf_op jit(solution)/shard_map/ppermute | solution.py:922
  128.2 25.4 %collective-permute-start.20 = (bf16[2,4,128,512]{3,2,1,0:T(8,128)(2,1)S(1)}, bf16[2,4,128,512]{3,2,1,0:T(8,128)(2,1)S(1)}, u32[]{:S(2)}, u32[]{:S(2)}) collective-permute-start(bf16[2,4,128,512]{3,2,1,0:T(8,128)(2,1)S(1)} %bitcast.194), channel_id=1, source_target_pairs={{0,4},{4,0},{8,12},{12,8},{16,20},{20,16},{24,28},{28,24},{1,5},{5... | collective-permute-start | bytes 3145736 | tf_op jit(solution)/shard_map/ppermute | solution.py:922
  128.2 38.5 %collective-permute-start.22 = (bf16[2,4,128,512]{3,2,1,0:T(8,128)(2,1)S(1)}, bf16[2,4,128,512]{3,2,1,0:T(8,128)(2,1)}, u32[]{:S(2)}, u32[]{:S(2)}) collective-permute-start(bf16[2,4,128,512]{3,2,1,0:T(8,128)(2,1)S(1)} %bitcast.197), channel_id=1, source_target_pairs={{0,4},{4,0},{8,12},{12,8},{16,20},{20,16},{24,28},{28,24},{1,5},{5... | collective-permute-start | bytes 3145736 | tf_op jit(solution)/shard_map/ppermute | solution.py:922
  152.5 14.7 %collective-permute-start.21 = (bf16[2,4,128,512]{3,2,1,0:T(8,128)(2,1)S(1)}, bf16[2,4,128,512]{3,2,1,0:T(8,128)(2,1)}, u32[]{:S(2)}, u32[]{:S(2)}) collective-permute-start(bf16[2,4,128,512]{3,2,1,0:T(8,128)(2,1)S(1)} %collective-permute-done.18.refs_1_), channel_id=1, source_target_pairs={{0,4},{4,0},{8,12},{12,8},{16,20},{20,16},{24,28},{28,24},{1,5},{5... | collective-permute-start | bytes 3145736 | tf_op jit(solution)/shard_map/ppermute | solution.py:922
  152.5 14.7 %collective-permute-start.23 = (bf16[2,4,128,512]{3,2,1,0:T(8,128)(2,1)S(1)}, bf16[2,4,128,512]{3,2,1,0:T(8,128)(2,1)}, u32[]{:S(2)}, u32[]{:S(2)}) collective-permute-start(bf16[2,4,128,512]{3,2,1,0:T(8,128)(2,1)S(1)} %collective-permute-done.19.refs_5_), channel_id=1, source_target_pairs={{0,4},{4,0},{8,12},{12,8},{16,20},{20,16},{24,28},{28,24},{1,5},{5... | collective-permute-start | bytes 3145736 | tf_op jit(solution)/shard_map/ppermute | solution.py:922
  153.0 13.8 %collective-permute-start.24 = (bf16[4,128,512]{2,1,0:T(8,128)(2,1)S(1)}, bf16[4,128,512]{2,1,0:T(8,128)(2,1)S(1)}, u32[]{:S(2)}, u32[]{:S(2)}) collective-permute-start(bf16[4,128,512]{2,1,0:T(8,128)(2,1)S(1)} %get-tuple-element.297), channel_id=1, source_target_pairs={{0,8},{4,12},{8,0},{12,4},{16,24},{20,28},{24,16},{28,20},{1,9},{5... | collective-permute-start | bytes 1572872 | tf_op jit(solution)/shard_map/ppermute | solution.py:922
  153.6 13.6 %collective-permute-start.25 = (bf16[4,128,512]{2,1,0:T(8,128)(2,1)S(1)}, bf16[4,128,512]{2,1,0:T(8,128)(2,1)S(1)}, u32[]{:S(2)}, u32[]{:S(2)}) collective-permute-start(bf16[4,128,512]{2,1,0:T(8,128)(2,1)S(1)} %get-tuple-element.298), channel_id=1, source_target_pairs={{0,16},{4,20},{8,24},{12,28},{16,0},{20,4},{24,8},{28,12},{1,17},{... | collective-permute-start | bytes 1572872 | tf_op jit(solution)/shard_map/ppermute | solution.py:922
  167.5 45.4 %collective-permute-start.26 = (bf16[2,4,128,512]{3,2,1,0:T(8,128)(2,1)S(1)}, bf16[2,4,128,512]{3,2,1,0:T(8,128)(2,1)S(1)}, u32[]{:S(2)}, u32[]{:S(2)}) collective-permute-start(bf16[2,4,128,512]{3,2,1,0:T(8,128)(2,1)S(1)} %bitcast.199), channel_id=1, source_target_pairs={{0,16},{4,20},{8,24},{12,28},{16,0},{20,4},{24,8},{28,12},{1,17},{... | collective-permute-start | bytes 3145736 | tf_op jit(solution)/shard_map/ppermute | solution.py:922
  169.0 44.0 %collective-permute-start.27 = (bf16[2,4,128,512]{3,2,1,0:T(8,128)(2,1)S(1)}, bf16[2,4,128,512]{3,2,1,0:T(8,128)(2,1)}, u32[]{:S(2)}, u32[]{:S(2)}) collective-permute-start(bf16[2,4,128,512]{3,2,1,0:T(8,128)(2,1)S(1)} %bitcast.202), channel_id=1, source_target_pairs={{0,8},{4,12},{8,0},{12,4},{16,24},{20,28},{24,16},{28,20},{1,9},{5... | collective-permute-start | bytes 3145736 | tf_op jit(solution)/shard_map/ppermute | solution.py:922
  172.0 45.5 %collective-permute-start.28 = (bf16[2,4,128,512]{3,2,1,0:T(8,128)(2,1)S(1)}, bf16[2,4,128,512]{3,2,1,0:T(8,128)(2,1)}, u32[]{:S(2)}, u32[]{:S(2)}) collective-permute-start(bf16[2,4,128,512]{3,2,1,0:T(8,128)(2,1)S(1)} %bitcast.200), channel_id=1, source_target_pairs={{0,4},{4,0},{8,12},{12,8},{16,20},{20,16},{24,28},{28,24},{1,5},{5... | collective-permute-start | bytes 3145736 | tf_op jit(solution)/shard_map/ppermute | solution.py:922
  172.0 45.5 %collective-permute-start.30 = (bf16[2,4,128,512]{3,2,1,0:T(8,128)(2,1)S(1)}, bf16[2,4,128,512]{3,2,1,0:T(8,128)(2,1)}, u32[]{:S(2)}, u32[]{:S(2)}) collective-permute-start(bf16[2,4,128,512]{3,2,1,0:T(8,128)(2,1)S(1)} %bitcast.203), channel_id=1, source_target_pairs={{0,4},{4,0},{8,12},{12,8},{16,20},{20,16},{24,28},{28,24},{1,5},{5... | collective-permute-start | bytes 3145736 | tf_op jit(solution)/shard_map/ppermute | solution.py:922
  213.0 4.4 collective-permute-start.29
  213.1 5.4 %collective-permute-start.31 = (bf16[2,4,128,512]{3,2,1,0:T(8,128)(2,1)}, bf16[2,4,128,512]{3,2,1,0:T(8,128)(2,1)S(1)}, u32[]{:S(2)}, u32[]{:S(2)}) collective-permute-start(bf16[2,4,128,512]{3,2,1,0:T(8,128)(2,1)} %collective-permute-done.27.refs_5_), channel_id=1, source_target_pairs={{0,4},{4,0},{8,12},{12,8},{16,20},{20,16},{24,28},{28,24},{1,5},{5... | collective-permute-start | bytes 3145736 | tf_op jit(solution)/shard_map/ppermute | solution.py:922
  219.4 41.1 %collective-permute-start.32 = (bf16[4,4,128,512]{3,2,1,0:T(8,128)(2,1)}, bf16[4,4,128,512]{3,2,1,0:T(8,128)(2,1)S(1)}, u32[]{:S(2)}, u32[]{:S(2)}) collective-permute-start(bf16[4,4,128,512]{3,2,1,0:T(8,128)(2,1)} %get-tuple-element.342), channel_id=1, source_target_pairs={{0,4},{4,0},{8,12},{12,8},{16,20},{20,16},{24,28},{28,24},{1,5},{5... | collective-permute-start | bytes 6291464 | tf_op jit(solution)/shard_map/ppermute | solution.py:922
  219.5 41.0 %collective-permute-start.33 = (bf16[4,4,128,512]{3,2,1,0:T(8,128)(2,1)}, bf16[4,4,128,512]{3,2,1,0:T(8,128)(2,1)}, u32[]{:S(2)}, u32[]{:S(2)}) collective-permute-start(bf16[4,4,128,512]{3,2,1,0:T(8,128)(2,1)} %get-tuple-element.343), channel_id=1, source_target_pairs={{0,4},{4,0},{8,12},{12,8},{16,20},{20,16},{24,28},{28,24},{1,5},{5... | collective-permute-start | bytes 6291464 | tf_op jit(solution)/shard_map/ppermute | solution.py:922
  260.5 26.0 %collective-permute-start.34 = (bf16[4,4,128,512]{3,2,1,0:T(8,128)(2,1)}, bf16[4,4,128,512]{3,2,1,0:T(8,128)(2,1)}, u32[]{:S(2)}, u32[]{:S(2)}) collective-permute-start(bf16[4,4,128,512]{3,2,1,0:T(8,128)(2,1)} %get-tuple-element.359), channel_id=1, source_target_pairs={{0,4},{4,0},{8,12},{12,8},{16,20},{20,16},{24,28},{28,24},{1,5},{5... | collective-permute-start | bytes 6291464 | tf_op jit(solution)/shard_map/ppermute | solution.py:922
  260.7 25.8 %collective-permute-start.35 = (bf16[4,4,128,512]{3,2,1,0:T(8,128)(2,1)}, bf16[4,4,128,512]{3,2,1,0:T(8,128)(2,1)}, u32[]{:S(2)}, u32[]{:S(2)}) collective-permute-start(bf16[4,4,128,512]{3,2,1,0:T(8,128)(2,1)} %get-tuple-element.360), channel_id=1, source_target_pairs={{0,4},{4,0},{8,12},{12,8},{16,20},{20,16},{24,28},{28,24},{1,5},{5... | collective-permute-start | bytes 6291464 | tf_op jit(solution)/shard_map/ppermute | solution.py:922
  266.8 46.9 %collective-permute-start.36 = (bf16[2,512,512]{2,1,0:T(8,128)(2,1)}, bf16[2,512,512]{2,1,0:T(8,128)(2,1)S(1)}, u32[]{:S(2)}, u32[]{:S(2)}) collective-permute-start(bf16[2,512,512]{2,1,0:T(8,128)(2,1)} %get-tuple-element.350), channel_id=1, source_target_pairs={{0,16},{4,20},{8,24},{12,28},{16,0},{20,4},{24,8},{28,12},{1,17},{... | collective-permute-start | bytes 3145736 | tf_op jit(solution)/shard_map/ppermute | solution.py:922
  267.3 46.4 %collective-permute-start.37 = (bf16[2,512,512]{2,1,0:T(8,128)(2,1)}, bf16[2,512,512]{2,1,0:T(8,128)(2,1)S(1)}, u32[]{:S(2)}, u32[]{:S(2)}) collective-permute-start(bf16[2,512,512]{2,1,0:T(8,128)(2,1)} %get-tuple-element.351), channel_id=1, source_target_pairs={{0,8},{4,12},{8,0},{12,4},{16,24},{20,28},{24,16},{28,20},{1,9},{5... | collective-permute-start | bytes 3145736 | tf_op jit(solution)/shard_map/ppermute | solution.py:922
  290.6 48.3 %collective-permute-start.40 = (bf16[2,512,512]{2,1,0:T(8,128)(2,1)S(1)}, bf16[2,512,512]{2,1,0:T(8,128)(2,1)S(1)}, u32[]{:S(2)}, u32[]{:S(2)}) collective-permute-start(bf16[2,512,512]{2,1,0:T(8,128)(2,1)S(1)} %get-tuple-element.366), channel_id=1, source_target_pairs={{0,16},{4,20},{8,24},{12,28},{16,0},{20,4},{24,8},{28,12},{1,17},{... | collective-permute-start | bytes 3145736 | tf_op jit(solution)/shard_map/ppermute | solution.py:922
  292.1 46.8 %collective-permute-start.41 = (bf16[2,512,512]{2,1,0:T(8,128)(2,1)S(1)}, bf16[2,512,512]{2,1,0:T(8,128)(2,1)}, u32[]{:S(2)}, u32[]{:S(2)}) collective-permute-start(bf16[2,512,512]{2,1,0:T(8,128)(2,1)S(1)} %get-tuple-element.367), channel_id=1, source_target_pairs={{0,8},{4,12},{8,0},{12,4},{16,24},{20,28},{24,16},{28,20},{1,9},{5... | collective-permute-start | bytes 3145736 | tf_op jit(solution)/shard_map/ppermute | solution.py:922
  316.3 22.5 %collective-permute-start.38 = (bf16[512,512]{1,0:T(8,128)(2,1)S(1)}, bf16[512,512]{1,0:T(8,128)(2,1)S(1)}, u32[]{:S(2)}, u32[]{:S(2)}) collective-permute-start(bf16[512,512]{1,0:T(8,128)(2,1)S(1)} %get-tuple-element.376), channel_id=1, source_target_pairs={{0,8},{4,12},{8,0},{12,4},{16,24},{20,28},{24,16},{28,20},{1,9},{5... | collective-permute-start | bytes 1572872 | tf_op jit(solution)/shard_map/ppermute | solution.py:922
  316.9 21.9 %collective-permute-start.39 = (bf16[512,512]{1,0:T(8,128)(2,1)S(1)}, bf16[512,512]{1,0:T(8,128)(2,1)S(1)}, u32[]{:S(2)}, u32[]{:S(2)}) collective-permute-start(bf16[512,512]{1,0:T(8,128)(2,1)S(1)} %get-tuple-element.377), channel_id=1, source_target_pairs={{0,16},{4,20},{8,24},{12,28},{16,0},{20,4},{24,8},{28,12},{1,17},{... | collective-permute-start | bytes 1572872 | tf_op jit(solution)/shard_map/ppermute | solution.py:922
  342.9 16.6 %collective-permute-start.42 = (bf16[512,512]{1,0:T(8,128)(2,1)S(1)}, bf16[512,512]{1,0:T(8,128)(2,1)S(1)}, u32[]{:S(2)}, u32[]{:S(2)}) collective-permute-start(bf16[512,512]{1,0:T(8,128)(2,1)S(1)} %get-tuple-element.393), channel_id=1, source_target_pairs={{0,8},{4,12},{8,0},{12,4},{16,24},{20,28},{24,16},{28,20},{1,9},{5... | collective-permute-start | bytes 1572872 | tf_op jit(solution)/shard_map/ppermute | solution.py:922
  344.3 15.2 %collective-permute-start.43 = (bf16[512,512]{1,0:T(8,128)(2,1)S(1)}, bf16[512,512]{1,0:T(8,128)(2,1)S(1)}, u32[]{:S(2)}, u32[]{:S(2)}) collective-permute-start(bf16[512,512]{1,0:T(8,128)(2,1)S(1)} %get-tuple-element.394), channel_id=1, source_target_pairs={{0,16},{4,20},{8,24},{12,28},{16,0},{20,4},{24,8},{28,12},{1,17},{... | collective-permute-start | bytes 1572872 | tf_op jit(solution)/shard_map/ppermute | solution.py:922
  359.5 16.6 %collective-permute-start.44 = (bf16[4,4,2,128,256]{4,3,2,1,0:T(8,128)(2,1)}, bf16[4,4,2,128,256]{4,3,2,1,0:T(8,128)(2,1)S(1)}, u32[]{:S(2)}, u32[]{:S(2)}) collective-permute-start(bf16[4,4,2,128,256]{4,3,2,1,0:T(8,128)(2,1)} %get-tuple-element.414), channel_id=1, source_target_pairs={{0,4},{4,0},{8,12},{12,8},{16,20},{20,16},{24,28},{28,24},{1,5},{5... | collective-permute-start | bytes 6291464 | tf_op jit(solution)/shard_map/ppermute | solution.py:922
  359.5 16.5 %collective-permute-start.45 = (bf16[4,4,2,128,256]{4,3,2,1,0:T(8,128)(2,1)}, bf16[4,4,2,128,256]{4,3,2,1,0:T(8,128)(2,1)S(1)}, u32[]{:S(2)}, u32[]{:S(2)}) collective-permute-start(bf16[4,4,2,128,256]{4,3,2,1,0:T(8,128)(2,1)} %get-tuple-element.415), channel_id=1, source_target_pairs={{0,4},{4,0},{8,12},{12,8},{16,20},{20,16},{24,28},{28,24},{1,5},{5... | collective-permute-start | bytes 6291464 | tf_op jit(solution)/shard_map/ppermute | solution.py:922
  364.6 38.0 %collective-permute-start.48 = (bf16[2,512,512]{2,1,0:T(8,128)(2,1)}, bf16[2,512,512]{2,1,0:T(8,128)(2,1)S(1)}, u32[]{:S(2)}, u32[]{:S(2)}) collective-permute-start(bf16[2,512,512]{2,1,0:T(8,128)(2,1)} %get-tuple-element.410), channel_id=1, source_target_pairs={{0,1},{1,0},{2,3},{3,2},{4,5},{5,4},{6,7},{7,6},{8,9},{9,8},{10,11... | collective-permute-start | bytes 3145736 | tf_op jit(solution)/shard_map/ppermute | solution.py:922
  382.3 24.6 %collective-permute-start.46 = (bf16[2,1024,256]{2,1,0:T(8,128)(2,1)S(1)}, bf16[2,1024,256]{2,1,0:T(8,128)(2,1)S(1)}, u32[]{:S(2)}, u32[]{:S(2)}) collective-permute-start(bf16[2,1024,256]{2,1,0:T(8,128)(2,1)S(1)} %get-tuple-element.421), channel_id=1, source_target_pairs={{0,16},{4,20},{8,24},{12,28},{16,0},{20,4},{24,8},{28,12},{1,17},{... | collective-permute-start | bytes 3145736 | tf_op jit(solution)/shard_map/ppermute | solution.py:922
  382.9 24.2 %collective-permute-start.47 = (bf16[2,1024,256]{2,1,0:T(8,128)(2,1)S(1)}, bf16[2,1024,256]{2,1,0:T(8,128)(2,1)S(1)}, u32[]{:S(2)}, u32[]{:S(2)}) collective-permute-start(bf16[2,1024,256]{2,1,0:T(8,128)(2,1)S(1)} %get-tuple-element.422), channel_id=1, source_target_pairs={{0,8},{4,12},{8,0},{12,4},{16,24},{20,28},{24,16},{28,20},{1,9},{5... | collective-permute-start | bytes 3145736 | tf_op jit(solution)/shard_map/ppermute | solution.py:922
  411.5 6.0 %collective-permute-start.49 = (f32[14,1024]{1,0:T(8,128)S(1)}, f32[14,1024]{1,0:T(8,128)S(1)}, u32[]{:S(2)}, u32[]{:S(2)}) collective-permute-start(f32[14,1024]{1,0:T(8,128)S(1)} %concatenate.61), channel_id=1, source_target_pairs={{0,1},{1,0},{2,3},{3,2},{4,5},{5,4},{6,7},{7,6},{8,9},{9,8},{10,11... | collective-permute-start | bytes 172040 | tf_op jit(solution)/shard_map/ppermute | solution.py:922
  412.2 14.0 %collective-permute-start.51 = (bf16[1024,256]{1,0:T(8,128)(2,1)S(1)}, bf16[1024,256]{1,0:T(8,128)(2,1)S(1)}, u32[]{:S(2)}, u32[]{:S(2)}) collective-permute-start(bf16[1024,256]{1,0:T(8,128)(2,1)S(1)} %get-tuple-element.434), channel_id=1, source_target_pairs={{0,8},{4,12},{8,0},{12,4},{16,24},{20,28},{24,16},{28,20},{1,9},{5... | collective-permute-start | bytes 1572872 | tf_op jit(solution)/shard_map/ppermute | solution.py:922
  412.9 13.3 %collective-permute-start.52 = (bf16[1024,256]{1,0:T(8,128)(2,1)S(1)}, bf16[1024,256]{1,0:T(8,128)(2,1)S(1)}, u32[]{:S(2)}, u32[]{:S(2)}) collective-permute-start(bf16[1024,256]{1,0:T(8,128)(2,1)S(1)} %get-tuple-element.435), channel_id=1, source_target_pairs={{0,16},{4,20},{8,24},{12,28},{16,0},{20,4},{24,8},{28,12},{1,17},{... | collective-permute-start | bytes 1572872 | tf_op jit(solution)/shard_map/ppermute | solution.py:922
  417.6 5.2 collective-permute-start.50
  423.5 23.0 %collective-permute-start.54 = (bf16[512,512]{1,0:T(8,128)(2,1)}, bf16[512,512]{1,0:T(8,128)(2,1)}, u32[]{:S(2)}, u32[]{:S(2)}) collective-permute-start(bf16[512,512]{1,0:T(8,128)(2,1)} %get-tuple-element.451), channel_id=1, source_target_pairs={{0,2},{1,3},{2,0},{3,1},{4,6},{5,7},{6,4},{7,5},{8,10},{9,11},{10,... | collective-permute-start | bytes 1572872 | tf_op jit(solution)/shard_map/ppermute | solution.py:922
  430.3 20.4 %collective-permute-start.53 = (bf16[2,512,256]{2,1,0:T(8,128)(2,1)}, bf16[2,512,256]{2,1,0:T(8,128)(2,1)S(1)}, u32[]{:S(2)}, u32[]{:S(2)}) collective-permute-start(bf16[2,512,256]{2,1,0:T(8,128)(2,1)} %get-tuple-element.458), channel_id=1, source_target_pairs={{0,1},{1,0},{2,3},{3,2},{4,5},{5,4},{6,7},{7,6},{8,9},{9,8},{10,11... | collective-permute-start | bytes 1572872 | tf_op jit(solution)/shard_map/ppermute | solution.py:922
  454.2 17.8 %collective-permute-start.57 = (bf16[512,256]{1,0:T(8,128)(2,1)}, bf16[512,256]{1,0:T(8,128)(2,1)S(1)}, u32[]{:S(2)}, u32[]{:S(2)}) collective-permute-start(bf16[512,256]{1,0:T(8,128)(2,1)} %get-tuple-element.467), channel_id=1, source_target_pairs={{0,2},{1,3},{2,0},{3,1},{4,6},{5,7},{6,4},{7,5},{8,10},{9,11},{10,... | collective-permute-start | bytes 786440 | tf_op jit(solution)/shard_map/ppermute | solution.py:922
  456.7 15.3 %collective-permute-start.55 = (bf16[1,48,1024]{2,1,0:T(8,128)(2,1)S(1)}, bf16[1,48,1024]{2,1,0:T(8,128)(2,1)S(1)}, u32[]{:S(2)}, u32[]{:S(2)}) collective-permute-start(bf16[1,48,1024]{2,1,0:T(8,128)(2,1)S(1)} %get-tuple-element.516), channel_id=1, source_target_pairs={{0,8},{4,12},{8,0},{12,4},{16,24},{20,28},{24,16},{28,20},{1,9},{5... | collective-permute-start | bytes 294920 | tf_op jit(solution)/shard_map/ppermute | solution.py:922
  458.1 13.9 %collective-permute-start.56 = (bf16[1,48,1024]{2,1,0:T(8,128)(2,1)S(1)}, bf16[1,48,1024]{2,1,0:T(8,128)(2,1)S(1)}, u32[]{:S(2)}, u32[]{:S(2)}) collective-permute-start(bf16[1,48,1024]{2,1,0:T(8,128)(2,1)S(1)} %get-tuple-element.515), channel_id=1, source_target_pairs={{0,16},{4,20},{8,24},{12,28},{16,0},{20,4},{24,8},{28,12},{1,17},{... | collective-permute-start | bytes 294920 | tf_op jit(solution)/shard_map/ppermute | solution.py:922
  472.0 5.7 %collective-permute-start.58 = (bf16[2,48,1024]{2,1,0:T(8,128)(2,1)S(1)}, bf16[2,48,1024]{2,1,0:T(8,128)(2,1)S(1)}, u32[]{:S(2)}, u32[]{:S(2)}) collective-permute-start(bf16[2,48,1024]{2,1,0:T(8,128)(2,1)S(1)} %pad_maximum_fusion.6), channel_id=1, source_target_pairs={{0,16},{4,20},{8,24},{12,28},{16,0},{20,4},{24,8},{28,12},{1,17},{... | collective-permute-start | bytes 589832 | tf_op jit(solution)/shard_map/ppermute | solution.py:922
  472.7 5.7 %collective-permute-start.59 = (bf16[2,48,1024]{2,1,0:T(8,128)(2,1)S(1)}, bf16[2,48,1024]{2,1,0:T(8,128)(2,1)S(1)}, u32[]{:S(2)}, u32[]{:S(2)}) collective-permute-start(bf16[2,48,1024]{2,1,0:T(8,128)(2,1)S(1)} %pad_maximum_fusion.7), channel_id=1, source_target_pairs={{0,8},{4,12},{8,0},{12,4},{16,24},{20,28},{24,16},{28,20},{1,9},{5... | collective-permute-start | bytes 589832 | tf_op jit(solution)/shard_map/ppermute | solution.py:922
  488.3 4.5 collective-permute-start.65
  492.8 4.8 collective-permute-start.67
  494.0 5.4 %collective-permute-start.68 = (f32[8,128]{1,0:T(8,128)S(1)}, f32[8,128]{1,0:T(8,128)S(1)}, u32[]{:S(2)}, u32[]{:S(2)}) collective-permute-start(f32[8,128]{1,0:T(8,128)S(1)} %add_add_fusion.1), channel_id=1, source_target_pairs={{0,3},{1,2},{2,1},{3,0},{4,7},{5,6},{6,5},{7,4},{8,11},{9,10},{10,... | collective-permute-start | bytes 12296 | tf_op jit(solution)/shard_map/ppermute | solution.py:922
  (78 other events, 698.1 us)
Sparse Core Ops, SparseCore 0:
  10.2 31.1 all-gather.4
  43.6 45.4 all-gather.6

commit v3 on v2

--- a/solution.py
+++ b/solution.py
@@ -1244,14 +1244,16 @@
     attn_low = jnp.swapaxes(attn_master, 0, 1).astype(bf16).reshape(4 * part, local_width)
     attn_rows = pad_rows(jnp.concatenate([attn_low, class_own], 0), 4 * part + 16)
     attn_z = lax.all_gather(attn_rows, "tensor", axis=0)
-    mlp_z = lax.all_gather(jnp.swapaxes(mlp_master, 0, 1).astype(bf16), "tensor", axis=0)
     class_rows = attn_z[:, 4 * part : 4 * part + class_own.shape[0]].reshape(FRAMES, D)
     attn_z = attn_z[:, : 4 * part].reshape(z_count, 4, part, local_width)
 
     msg_low = jnp.swapaxes(msg_master, 0, 1).astype(bf16).reshape(5 * part, D)
     vec_count = vec_master.shape[1]
     vec_low = jnp.pad(vec_master.astype(bf16).T, ((0, 32 - vec_count), (0, D // 2 - part)))
-    msg_go = Gather(jnp.concatenate([msg_low[:, : D // 2], vec_low], 0), msg_low[:, D // 2 :])
+    msg_half = [jnp.concatenate([msg_low[:, : D // 2], vec_low], 0), msg_low[:, D // 2 :]]
+    msg_go = Gather(*msg_half)
+    mlp_low = jnp.swapaxes(after(mlp_master, *msg_half), 0, 1).astype(bf16)
+    mlp_z = lax.all_gather(mlp_low, "tensor", axis=0)
     prepared = prepare(info, tokens, cotangent)
     x, grads, grads_t, grad_sum = beside(prepared, msg_go)
     sent_msg = msg_go.step()
@@ -1361,15 +1363,14 @@
             msg_w,
         ),
         attn_go,
-        mlp_go,
-    )
-    mlp_sum = mlp_go.result()
+    )
     going = attn_go.step()
 
     small = GatherSmall(after(sent, going))
     input_grad = beside(
-        finish(info, [after(ing, *small.values)], grad_class, "input_grad"), small, attn_go
-    )
+        finish(info, [after(ing, *small.values)], grad_class, "input_grad"), small, attn_go, mlp_go
+    )
+    mlp_sum = mlp_go.result()
     small.step()
     attn_grad = attn_go.result()
     mlp_grad = jnp.concatenate([mlp_sum[:2], mlp_sum[2:]], 2)

time: 536 us -> 532 us (level)
    unnamed x154 -> x153, local copies, waits for them, and re-layouts: 23.7 us -> 23.4 us
where the time goes in v3:
time: 532 us; the launch traced here: 524 us
  Pallas kernels  297 us (56%)
  waiting for transfers between devices  80.1 us (15%)
  starting transfers between devices  58.9 us (11%)
  local copies, waits for them, and re-layouts  35.8 us (7%)
  other arithmetic  30 us (6%)
  between operations  20.3 us (4%)
    pallas_call x15, Pallas kernels, call(): pl.pallas_call(kernel, grid_spec=pltpu.PrefetchScalarGridSpec(num_scalar_...  137 us
    pallas_call x2, Pallas kernels, feed_forward(): pl.pallas_call(feed_kernel, grid=(steps,), in_specs=[pl.BlockSpec((frames...  81 us
    ppermute x69, waiting for transfers between devices, swap(): return lax.ppermute(values, axis, pairs)  71.6 us
    ppermute x69, starting transfers between devices, swap(): return lax.ppermute(values, axis, pairs)  58.8 us
    pallas_call x2, Pallas kernels, attend_backward(): pl.pallas_call(attend_backward_kernel, grid=(frames,), in_specs=[spec] *...  40 us
    unnamed x153, local copies, waits for them, and re-layouts  23.4 us
    pallas_call x6, Pallas kernels, add_and_split(): pl.pallas_call(functools.partial(add_kernel, axes), grid=(steps,), in_spe...  18.9 us
    pallas_call x1, Pallas kernels, attend_forward(): pl.pallas_call(attend_forward_kernel, grid=(frames,), in_specs=[spec] * 3...  18.5 us
  transfers between devices with their start and end apart: 71, of which 26 were waited for; matrix products, arithmetic and copies ran while one was open for 4% of the time, Pallas kernels for 55%

profile of v3, /device:TPU:0, one launch (start us, length us, event | category | flops | bytes accessed | tf_op | source)
XLA Modules:
  0.0 523.6 jit_solution(15682698735179778452)
XLA Ops:
  10.2 1.9 convert_element_type.83
  12.3 3.0 collective-permute-start
  15.3 1.5 collective-permute-start.1
  18.6 8.6 %prepare.1 = (bf16[2,592,1024]{2,1,0:T(8,128)(2,1)}, bf16[2,592,1024]{2,1,0:T(8,128)(2,1)}, bf16[1024,1280]{1,0:T(8,128)(2,1)}, f32[1,1024]{1,0:T(1,128)}) custom-call(s32[17]{0:T(128)} %pad_add_fusion.info_ref, bf16[1154,1024]{1,0:T(8,128)(2,1)} %tokens_ref.1, bf16[1154,1024]{1,0:T(8,128)(2,1)} %cot_ref.1), custom_call_target="tpu_custom_call" | custom-call | bytes 762624 | tf_op jit(solution)/shard_map/prepare/pallas_call | solution.py:334
  27.2 4.3 collective-permute-done.1.refs_3_
  36.6 1.5 collective-permute-start.4
  38.6 2.8 all-gather.5.cloned.1.call-done
  42.8 1.5 collective-permute-start.2
  44.4 1.5 collective-permute-start.3
  45.9 32.8 %collective-permute-done.2 = bf16[4,2,128,256]{3,2,1,0:T(8,128)(2,1)S(1)} collective-permute-done((bf16[4,2,128,256]{3,2,1,0:T(8,128)(2,1)S(1)}, bf16[4,2,128,256]{3,2,1,0:T(8,128)(2,1)S(1)}, u32[]{:S(2)}, u32[]{:S(2)}) %collective-permute-start.2) | collective-permute-done | bytes 524320 | tf_op jit(solution)/shard_map/ppermute | solution.py:922
  79.7 1.5 collective-permute-start.10
  83.5 5.6 %all-gather.7.cloned.1.call-done = bf16[8,128,1024]{2,1,0:T(8,128)(2,1)} async-done(((bf16[2,128,1024]{2,1,0:T(8,128)(2,1)}), bf16[8,128,1024]{2,1,0:T(8,128)(2,1)}) %all-gather.7.cloned.1.call-update) | async-done | bytes 2097168 | tf_op jit(solution)/shard_map/all_gather | solution.py:1256
  89.1 2.9 fusion.30
  94.2 8.0 %message_forward.1 = (f32[18,1024]{1,0:T(8,128)}, f32[8,1024]{1,0:T(8,128)}, f32[8,1024]{1,0:T(8,128)}, f32[5,8,1024]{2,1,0:T(8,128)}) custom-call(s32[17]{0:T(128)} %pad_add_fusion.info_ref, f32[8,1024]{1,0:T(8,128)} %convert_element_type.90.cls_ref, f32[18,1024]{1,0:T(8,128)} %bitcast.241, bf16[2,672,512]{2,1,0:T(8,128)(2,1)} %copy-done.4, ...), custom_call_target="tpu_custom_call" | custom-call | flops 5242880 | bytes 697344 | tf_op jit(solution)/shard_map/message_forward/pallas_call | solution.py:334
  102.2 3.2 collective-permute-done.10.refs_1_
  108.2 2.8 collective-permute-done.13.refs_3_
  112.0 14.6 %project.1 = (bf16[2,592,1024]{2,1,0:T(8,128)(2,1)}, bf16[2,592,1024]{2,1,0:T(8,128)(2,1)}, bf16[2,592,1024]{2,1,0:T(8,128)(2,1)}, bf16[1184,1024]{1,0:T(8,128)(2,1)}) custom-call(s32[17]{0:T(128)} %pad_add_fusion.info_ref, bf16[2,592,1024]{2,1,0:T(8,128)(2,1)} %get-tuple-element.425.x_ref, f32[8,1024]{1,0:T(8,128)} %get-tuple-element.274.msg_ref, ...), custom_call_target="tpu_custom_call" | custom-call | flops 465567744 | bytes 1293312 | tf_op jit(solution)/shard_map/project/pallas_call | solution.py:334
  128.7 1.7 copy-done
  130.4 18.5 %attend_forward.1 = (bf16[2,592,1024]{2,1,0:T(8,128)(2,1)S(1)}, f32[2,8,2,592]{3,2,1,0:T(2,128)S(1)}) custom-call(bf16[2,592,1024]{2,1,0:T(8,128)(2,1)S(1)} %copy-done, bf16[2,592,1024]{2,1,0:T(8,128)(2,1)} %get-tuple-element.288.k_ref, bf16[2,592,1024]{2,1,0:T(8,128)(2,1)} %get-tuple-element.289.v_ref), custom_call_target="tpu_custom_call" | custom-call | flops 358875136 | bytes 1212416 | tf_op jit(solution)/shard_map/attend_forward/pallas_call | solution.py:192
  150.3 1.9 collective-permute-done.18.refs_1_
  155.0 1.5 slice_bitcast_fusion.16
  156.6 10.1 %combine.1 = (f32[2,592,1024]{2,1,0:T(8,128)}, bf16[2,592,1024]{2,1,0:T(8,128)(2,1)}, bf16[1024,1280]{1,0:T(8,128)(2,1)}) custom-call(s32[17]{0:T(128)} %pad_add_fusion.info_ref, bf16[2,592,1024]{2,1,0:T(8,128)(2,1)} %get-tuple-element.425.x_ref, bf16[2,592,1024]{2,1,0:T(8,128)(2,1)} %copy-done.5, f32[1,1024]{1,0:T(1,128)} %get-tuple-element.523.bias_ref, ...), custom_call_target="tpu_custom_call" | custom-call | flops 155189248 | bytes 1184512 | tf_op jit(solution)/shard_map/combine/pallas_call | solution.py:334
  167.5 1.4 collective-permute-start.26
  169.0 1.5 collective-permute-start.27
  172.5 40.5 %feed_forward.2 = (f32[2,592,1024]{2,1,0:T(8,128)}, f32[2,592,1024]{2,1,0:T(8,128)}, bf16[4,4,128,512]{3,2,1,0:T(8,128)(2,1)}, bf16[4,4,128,512]{3,2,1,0:T(8,128...) custom-call(bf16[2,592,1024]{2,1,0:T(8,128)(2,1)} %get-tuple-element.332.n2_ref, ...), custom_call_target="tpu_custom_call" | custom-call | flops 1862270976 | bytes 2260992 | tf_op jit(solution)/shard_map/feed_forward/pallas_call | solution.py:288
  213.6 3.9 transposed.1.ht_ref
  219.9 40.6 %feed_forward.3 = (f32[2,592,1024]{2,1,0:T(8,128)}, f32[2,592,1024]{2,1,0:T(8,128)}, bf16[4,4,128,512]{3,2,1,0:T(8,128)(2,1)}, bf16[4,4,128,512]{3,2,1,0:T(8,128...) custom-call(bf16[2,592,1024]{2,1,0:T(8,128)(2,1)} %get-tuple-element.332.n2_ref, ...), custom_call_target="tpu_custom_call" | custom-call | flops 1862270976 | bytes 2260992 | tf_op jit(solution)/shard_map/feed_forward/pallas_call | solution.py:288
  261.8 4.9 add.268
  268.0 18.6 %between.1 = (bf16[2,592,1024]{2,1,0:T(8,128)(2,1)}, bf16[2,592,1024]{2,1,0:T(8,128)(2,1)}, bf16[4,4,128,256]{3,2,1,0:T(8,128)(2,1)}, bf16[4,4,128,256]{3,2,1,0:T(8,128)(2,1)}, f32[3,1024]{1,0:T(4,128)}) custom-call(s32[17]{0:T(128)} %pad_add_fusion.info_ref, f32[2,592,1024]{2,1,0:T(8,128)} %get-tuple-element.354.ea_ref, ...), custom_call_target="tpu_custom_call" | custom-call | flops 310378496 | bytes 1909760 | tf_op jit(solution)/shard_map/between/pallas_call | solution.py:334
  286.5 4.1 add.269
  290.6 1.4 collective-permute-start.40
  292.1 1.5 collective-permute-start.41
  293.6 20.1 %attend_backward.2 = (bf16[2,592,1024]{2,1,0:T(8,128)(2,1)S(1)}, bf16[2,592,1024]{2,1,0:T(8,128)(2,1)S(1)}, bf16[2,592,1024]{2,1,0:T(8,128)(2,1)}) custom-call(bf16[2,592,1024]{2,1,0:T(8,128)(2,1)} %get-tuple-element.287.q_ref, bf16[2,592,1024]{2,1,0:T(8,128)(2,1)} %get-tuple-element.288.k_ref, bf16[2,592,1024]{2,1,0:T(8,128)(2,1)} %get-tuple-element.289.v_ref, ...), custom_call_target="tpu_custom_call" | custom-call | flops 358875136 | bytes 1212416 | tf_op jit(solution)/shard_map/attend_backward/pallas_call | solution.py:212
  314.6 1.7 add.270
  317.6 19.8 %attend_backward.3 = (bf16[2,592,1024]{2,1,0:T(8,128)(2,1)S(1)}, bf16[2,592,1024]{2,1,0:T(8,128)(2,1)S(1)}, bf16[2,592,1024]{2,1,0:T(8,128)(2,1)}) custom-call(bf16[2,592,1024]{2,1,0:T(8,128)(2,1)} %get-tuple-element.287.q_ref, bf16[2,592,1024]{2,1,0:T(8,128)(2,1)} %get-tuple-element.288.k_ref, ...), custom_call_target="tpu_custom_call", output_to_operand_aliasing={{0}: (5, {}), {1}: (6, {}), {2}: (7, {})} | custom-call | flops 358875136 | bytes 1212416 | tf_op jit(solution)/shard_map/attend_backward/pallas_call | solution.py:212
  338.9 2.4 add.271
  344.3 1.5 collective-permute-start.43
  345.7 13.7 %project_grads.1 = (bf16[4,4,2,128,256]{4,3,2,1,0:T(8,128)(2,1)}, bf16[4,4,2,128,256]{4,3,2,1,0:T(8,128)(2,1)}, bf16[4,4,2,128,256]{4,3,2,1,0:T(8,128)(2,1)}, bf...) custom-call(s32[17]{0:T(128)} %pad_add_fusion.info_ref, ...), custom_call_target="tpu_custom_call" | custom-call | flops 465567744 | bytes 1274368 | tf_op jit(solution)/shard_map/project_grads/pallas_call | solution.py:334
  360.4 4.2 add_and_pair.2
  364.6 1.5 collective-permute-start.48
  366.1 9.9 %block_output.1 = f32[1154,1024]{1,0:T(8,128)} custom-call(s32[17]{0:T(128)} %pad_add_fusion.info_ref, f32[2,592,1024]{2,1,0:T(8,128)} %get-tuple-element.413.mid_ref.refs_0_, f32[2,592,1024]{2,1,0:T(8,128)} %get-tuple-element.414.refs_1_, f32[2,592,1024]{2,1,0:T(8,128)} %get-tuple-element.415.refs_2_, f32[1,1024]{1,0:T(1,128)} %get-tuple-element.520.refs_3_), custom_call_target="tpu_custom_call" | custom-call | bytes 1204992 | tf_op jit(solution)/shard_map/block_output/pallas_call | solution.py:334
  378.0 4.2 add.272
  383.6 19.0 %project_back.1 = (f32[2,592,1024]{2,1,0:T(8,128)}, f32[2,1,1024]{2,1,0:T(1,128)}, f32[2,1024]{1,0:T(2,128)}) custom-call(s32[17]{0:T(128)} %pad_add_fusion.info_ref, bf16[2,592,1024]{2,1,0:T(8,128)(2,1)} %get-tuple-element.425.x_ref, f32[8,1024]{1,0:T(8,128)} %get-tuple-element.274.msg_ref, bf16[2,592,1024]{2,1,0:T(8,128)(2,1)} %get-tuple-element.426.dmid_ref, ...), custom_call_target="tpu_custom_call" | custom-call | flops 465567744 | bytes 1588480 | tf_op jit(solution)/shard_map/project_back/pallas_call | solution.py:334
  402.7 4.2 collective-permute-done.46.refs_1_
  408.2 1.7 add.273
  414.3 3.3 add_and_single.2
  417.6 2.6 collective-permute-start.50
  420.3 2.6 collective-permute-done.50
  425.2 3.2 add_and_pair.3
  428.4 1.5 collective-permute-start.53
  430.5 2.6 collective-permute-start.57
  433.8 9.1 %message_backward.1 = (f32[8,1024]{1,0:T(8,128)}, bf16[96,1024]{1,0:T(8,128)(2,1)}) custom-call(s32[17]{0:T(128)} %pad_add_fusion.info_ref, f32[4,2,1024]{2,1,0:T(2,128)} %pad_maximum_fusion.12.dmsg_ref, f32[12,1024]{1,0:T(8,128)} %slice_add_fusion.table_ref, f32[8,1024]{1,0:T(8,128)} %convert_element_type.97.cls_ref, ...), custom_call_target="tpu_custom_call" | custom-call | flops 5242880 | bytes 710144 | tf_op jit(solution)/shard_map/message_backward/pallas_call | solution.py:334
  442.9 7.2 %collective-permute-done.53.ao_ref.ap_ref = bf16[2,512,256]{2,1,0:T(8,128)(2,1)S(1)} collective-permute-done((bf16[2,512,256]{2,1,0:T(8,128)(2,1)}, bf16[2,512,256]{2,1,0:T(8,128)(2,1)S(1)}, u32[]{:S(2)}, u32[]{:S(2)}) %collective-permute-start.53) | collective-permute-done | bytes 524320 | tf_op jit(solution)/shard_map/ppermute | solution.py:922
  450.9 2.7 add_and_single.3
  456.4 1.5 collective-permute-start.55
  458.8 8.0 %input_grad.1 = f32[1154,1024]{1,0:T(8,128)} custom-call(s32[17]{0:T(128)} %pad_add_fusion.info_ref, f32[2,592,1024]{2,1,0:T(8,128)} %get-tuple-element.471.refs_0_, f32[8,1024]{1,0:T(8,128)} %get-tuple-element.472.refs_1_), custom_call_target="tpu_custom_call" | custom-call | bytes 600576 | tf_op jit(solution)/shard_map/input_grad/pallas_call | solution.py:334
  469.7 2.6 multiply_reduce_fusion.1
  486.6 1.8 collective-permute-done.65
  488.8 2.4 collective-permute-start.67
  491.3 2.3 collective-permute-start.68
  493.6 3.1 collective-permute-done.68
  498.5 7.9 %multiply_add_fusion = (f32[128,5,1024]{2,0,1:T(8,128)}, f32[128,5,1024]{2,0,1:T(8,128)}, f32[128,5,1024]{2,0,1:T(8,128)}, f32[128,5,1024]{2,0,1:T(8,128)}) fusion(f32[128,5,1024]{2,0,1:T(8,128)} %param.31, f32[128,5,1024]{2,0,1:T(8,128)} %param.28, f32[128,5,1024]{2,0,1:T(8,128)S(1)} %fusion.2, f32[]{:T(128)S(6)} %div.81, f32[128,5,1024]{2,0,1:T(8,128)} %param.30, ...), kind=kLoop, calls=%fused_computation.2 | loop fusion | flops 12451840 | bytes 23592964 | tf_op jit(solution)/shard_map/add | solution.py:1411
  507.2 2.3 multiply_add_fusion.4
  509.5 5.7 %multiply_add_fusion.2 = (f32[128,2,1024]{2,1,0:T(2,128)}, f32[128,2,1024]{2,1,0:T(2,128)}, f32[128,2,1024]{2,1,0:T(2,128)}, f32[128,2,1024]{2,1,0:T(2,128)}) fusion(f32[128,2,1024]{2,1,0:T(2,128)S(1)} %copy-done.40, f32[128,2,1024]{2,1,0:T(2,128)S(1)} %copy-done.26, f32[128,2,1024]{2,1,0:T(2,128)S(1)} %copy-done.27, f32[]{:T(128)S(6)} %div.81, ...), kind=kLoop, calls=%fused_computation.28 | loop fusion | flops 4980736 | bytes 9437188 | tf_op jit(solution)/shard_map/add | solution.py:1411
  (335 shorter events, 77.0 us)
Async XLA Ops:
  7.2 34.3 %all-gather.5.cloned.1.call-start = ((), (), s32[]{:S(2)}) async-start(), calls=%async_computation | async-start | bytes 1351680 | tf_op jit(solution)/shard_map/all_gather | solution.py:1246
  10.1 78.9 %all-gather.7.cloned.1.call-start = ((), (), s32[]{:S(2)}) async-start(), calls=%async_computation.1 | async-start | bytes 2621440 | tf_op jit(solution)/shard_map/all_gather | solution.py:1256
  12.3 20.0 %collective-permute-start = (bf16[672,512]{1,0:T(8,128)(2,1)S(1)}, bf16[672,512]{1,0:T(8,128)(2,1)S(1)}, u32[]{:S(2)}, u32[]{:S(2)}) collective-permute-start(bf16[672,512]{1,0:T(8,128)(2,1)S(1)} %fusion.9.refs_0_), channel_id=1, source_target_pairs={{0,8},{4,12},{8,0},{12,4},{16,24},{20,28},{24,16},{28,20},{1,9},{5... | collective-permute-start | bytes 2064392 | tf_op jit(solution)/shard_map/ppermute | solution.py:922
  15.3 16.2 %collective-permute-start.1 = (bf16[640,512]{1,0:T(8,128)(2,1)S(1)}, bf16[640,512]{1,0:T(8,128)(2,1)S(1)}, u32[]{:S(2)}, u32[]{:S(2)}) collective-permute-start(bf16[640,512]{1,0:T(8,128)(2,1)S(1)} %get-tuple-element.511.refs_2_), channel_id=1, source_target_pairs={{0,16},{4,20},{8,24},{12,28},{16,0},{20,4},{24,8},{28,12},{1,17},{... | collective-permute-start | bytes 1966088 | tf_op jit(solution)/shard_map/ppermute | solution.py:922
  36.6 42.5 %collective-permute-start.4 = (bf16[2,672,512]{2,1,0:T(8,128)(2,1)S(1)}, bf16[2,672,512]{2,1,0:T(8,128)(2,1)}, u32[]{:S(2)}, u32[]{:S(2)}) collective-permute-start(bf16[2,672,512]{2,1,0:T(8,128)(2,1)S(1)} %get-tuple-element.261.refs_0_), channel_id=1, source_target_pairs={{0,16},{4,20},{8,24},{12,28},{16,0},{20,4},{24,8},{28,12},{1,17},{... | collective-permute-start | bytes 4128776 | tf_op jit(solution)/shard_map/ppermute | solution.py:922
  38.1 40.9 %collective-permute-start.5 = (bf16[2,640,512]{2,1,0:T(8,128)(2,1)}, bf16[2,640,512]{2,1,0:T(8,128)(2,1)}, u32[]{:S(2)}, u32[]{:S(2)}) collective-permute-start(bf16[2,640,512]{2,1,0:T(8,128)(2,1)} %get-tuple-element.262.refs_4_), channel_id=1, source_target_pairs={{0,8},{4,12},{8,0},{12,4},{16,24},{20,28},{24,16},{28,20},{1,9},{5... | collective-permute-start | bytes 3932168 | tf_op jit(solution)/shard_map/ppermute | solution.py:922
  38.6 42.5 %collective-permute-start.6 = (bf16[2,672,512]{2,1,0:T(8,128)(2,1)S(1)}, bf16[2,672,512]{2,1,0:T(8,128)(2,1)}, u32[]{:S(2)}, u32[]{:S(2)}) collective-permute-start(bf16[2,672,512]{2,1,0:T(8,128)(2,1)S(1)} %get-tuple-element.261.refs_0_), channel_id=1, source_target_pairs={{0,4},{4,0},{8,12},{12,8},{16,20},{20,16},{24,28},{28,24},{1,5},{5... | collective-permute-start | bytes 4128776 | tf_op jit(solution)/shard_map/ppermute | solution.py:922
  42.8 35.8 %collective-permute-start.2 = (bf16[4,2,128,256]{3,2,1,0:T(8,128)(2,1)S(1)}, bf16[4,2,128,256]{3,2,1,0:T(8,128)(2,1)S(1)}, u32[]{:S(2)}, u32[]{:S(2)}) collective-permute-start(bf16[4,2,128,256]{3,2,1,0:T(8,128)(2,1)S(1)} %get-tuple-element.514), channel_id=1, source_target_pairs={{0,8},{4,12},{8,0},{12,4},{16,24},{20,28},{24,16},{28,20},{1,9},{5... | collective-permute-start | bytes 1572872 | tf_op jit(solution)/shard_map/ppermute | solution.py:922
  44.4 34.3 %collective-permute-start.3 = (bf16[4,2,128,256]{3,2,1,0:T(8,128)(2,1)S(1)}, bf16[4,2,128,256]{3,2,1,0:T(8,128)(2,1)S(1)}, u32[]{:S(2)}, u32[]{:S(2)}) collective-permute-start(bf16[4,2,128,256]{3,2,1,0:T(8,128)(2,1)S(1)} %get-tuple-element.513), channel_id=1, source_target_pairs={{0,16},{4,20},{8,24},{12,28},{16,0},{20,4},{24,8},{28,12},{1,17},{... | collective-permute-start | bytes 1572872 | tf_op jit(solution)/shard_map/ppermute | solution.py:922
  79.1 15.0 %collective-permute-start.8 = (bf16[2,640,512]{2,1,0:T(8,128)(2,1)}, bf16[2,640,512]{2,1,0:T(8,128)(2,1)}, u32[]{:S(2)}, u32[]{:S(2)}) collective-permute-start(bf16[2,640,512]{2,1,0:T(8,128)(2,1)} %get-tuple-element.262.refs_4_), channel_id=1, source_target_pairs={{0,4},{4,0},{8,12},{12,8},{16,20},{20,16},{24,28},{28,24},{1,5},{5... | collective-permute-start | bytes 3932168 | tf_op jit(solution)/shard_map/ppermute | solution.py:922
  79.6 14.6 %collective-permute-start.9 = (bf16[2,640,512]{2,1,0:T(8,128)(2,1)}, bf16[2,640,512]{2,1,0:T(8,128)(2,1)}, u32[]{:S(2)}, u32[]{:S(2)}) collective-permute-start(bf16[2,640,512]{2,1,0:T(8,128)(2,1)} %collective-permute-done.5.refs_5_), channel_id=1, source_target_pairs={{0,4},{4,0},{8,12},{12,8},{16,20},{20,16},{24,28},{28,24},{1,5},{5... | collective-permute-start | bytes 3932168 | tf_op jit(solution)/shard_map/ppermute | solution.py:922
  79.7 25.6 %collective-permute-start.10 = (bf16[2,4,2,128,256]{4,3,2,1,0:T(8,128)(2,1)S(1)}, bf16[2,4,2,128,256]{4,3,2,1,0:T(8,128)(2,1)}, u32[]{:S(2)}, u32[]{:S(2)}) collective-permute-start(bf16[2,4,2,128,256]{4,3,2,1,0:T(8,128)(2,1)S(1)} %bitcast.171), channel_id=1, source_target_pairs={{0,16},{4,20},{8,24},{12,28},{16,0},{20,4},{24,8},{28,12},{1,17},{... | collective-permute-start | bytes 3145736 | tf_op jit(solution)/shard_map/ppermute | solution.py:922
  81.2 25.3 %collective-permute-start.11 = (bf16[2,4,2,128,256]{4,3,2,1,0:T(8,128)(2,1)S(1)}, bf16[2,4,2,128,256]{4,3,2,1,0:T(8,128)(2,1)}, u32[]{:S(2)}, u32[]{:S(2)}) collective-permute-start(bf16[2,4,2,128,256]{4,3,2,1,0:T(8,128)(2,1)S(1)} %bitcast.165), channel_id=1, source_target_pairs={{0,8},{4,12},{8,0},{12,4},{16,24},{20,28},{24,16},{28,20},{1,9},{5... | collective-permute-start | bytes 3145736 | tf_op jit(solution)/shard_map/ppermute | solution.py:922
  82.6 25.0 %collective-permute-start.12 = (bf16[2,4,2,128,256]{4,3,2,1,0:T(8,128)(2,1)S(1)}, bf16[2,4,2,128,256]{4,3,2,1,0:T(8,128)(2,1)}, u32[]{:S(2)}, u32[]{:S(2)}) collective-permute-start(bf16[2,4,2,128,256]{4,3,2,1,0:T(8,128)(2,1)S(1)} %bitcast.172), channel_id=1, source_target_pairs={{0,4},{4,0},{8,12},{12,8},{16,20},{20,16},{24,28},{28,24},{1,5},{5... | collective-permute-start | bytes 3145736 | tf_op jit(solution)/shard_map/ppermute | solution.py:922
  94.1 14.1 %collective-permute-start.14 = (bf16[2,4,2,128,256]{4,3,2,1,0:T(8,128)(2,1)S(1)}, bf16[2,4,2,128,256]{4,3,2,1,0:T(8,128)(2,1)S(1)}, u32[]{:S(2)}, u32[]{:S(2)}) collective-permute-start(bf16[2,4,2,128,256]{4,3,2,1,0:T(8,128)(2,1)S(1)} %bitcast.166), channel_id=1, source_target_pairs={{0,4},{4,0},{8,12},{12,8},{16,20},{20,16},{24,28},{28,24},{1,5},{5... | collective-permute-start | bytes 3145736 | tf_op jit(solution)/shard_map/ppermute | solution.py:922
  106.5 4.5 collective-permute-start.13
  106.5 4.5 collective-permute-start.15
  107.0 19.5 %collective-permute-start.16 = (bf16[4,128,512]{2,1,0:T(8,128)(2,1)}, bf16[4,128,512]{2,1,0:T(8,128)(2,1)S(1)}, u32[]{:S(2)}, u32[]{:S(2)}) collective-permute-start(bf16[4,128,512]{2,1,0:T(8,128)(2,1)} %get-tuple-element.506), channel_id=1, source_target_pairs={{0,8},{4,12},{8,0},{12,4},{16,24},{20,28},{24,16},{28,20},{1,9},{5... | collective-permute-start | bytes 1572872 | tf_op jit(solution)/shard_map/ppermute | solution.py:922
  107.6 19.0 %collective-permute-start.17 = (bf16[4,128,512]{2,1,0:T(8,128)(2,1)S(1)}, bf16[4,128,512]{2,1,0:T(8,128)(2,1)S(1)}, u32[]{:S(2)}, u32[]{:S(2)}) collective-permute-start(bf16[4,128,512]{2,1,0:T(8,128)(2,1)S(1)} %copy-done.55), channel_id=1, source_target_pairs={{0,16},{4,20},{8,24},{12,28},{16,0},{20,4},{24,8},{28,12},{1,17},{... | collective-permute-start | bytes 1572872 | tf_op jit(solution)/shard_map/ppermute | solution.py:922
  127.0 25.3 %collective-permute-start.18 = (bf16[2,4,128,512]{3,2,1,0:T(8,128)(2,1)S(1)}, bf16[2,4,128,512]{3,2,1,0:T(8,128)(2,1)S(1)}, u32[]{:S(2)}, u32[]{:S(2)}) collective-permute-start(bf16[2,4,128,512]{3,2,1,0:T(8,128)(2,1)S(1)} %bitcast.193), channel_id=1, source_target_pairs={{0,16},{4,20},{8,24},{12,28},{16,0},{20,4},{24,8},{28,12},{1,17},{... | collective-permute-start | bytes 3145736 | tf_op jit(solution)/shard_map/ppermute | solution.py:922
  127.6 24.9 %collective-permute-start.19 = (bf16[2,4,128,512]{3,2,1,0:T(8,128)(2,1)S(1)}, bf16[2,4,128,512]{3,2,1,0:T(8,128)(2,1)S(1)}, u32[]{:S(2)}, u32[]{:S(2)}) collective-permute-start(bf16[2,4,128,512]{3,2,1,0:T(8,128)(2,1)S(1)} %bitcast.196), channel_id=1, source_target_pairs={{0,8},{4,12},{8,0},{12,4},{16,24},{20,28},{24,16},{28,20},{1,9},{5... | collective-permute-start | bytes 3145736 | tf_op jit(solution)/shard_map/ppermute | solution.py:922
  128.2 25.4 %collective-permute-start.20 = (bf16[2,4,128,512]{3,2,1,0:T(8,128)(2,1)S(1)}, bf16[2,4,128,512]{3,2,1,0:T(8,128)(2,1)S(1)}, u32[]{:S(2)}, u32[]{:S(2)}) collective-permute-start(bf16[2,4,128,512]{3,2,1,0:T(8,128)(2,1)S(1)} %bitcast.194), channel_id=1, source_target_pairs={{0,4},{4,0},{8,12},{12,8},{16,20},{20,16},{24,28},{28,24},{1,5},{5... | collective-permute-start | bytes 3145736 | tf_op jit(solution)/shard_map/ppermute | solution.py:922
  128.2 38.5 %collective-permute-start.22 = (bf16[2,4,128,512]{3,2,1,0:T(8,128)(2,1)S(1)}, bf16[2,4,128,512]{3,2,1,0:T(8,128)(2,1)}, u32[]{:S(2)}, u32[]{:S(2)}) collective-permute-start(bf16[2,4,128,512]{3,2,1,0:T(8,128)(2,1)S(1)} %bitcast.197), channel_id=1, source_target_pairs={{0,4},{4,0},{8,12},{12,8},{16,20},{20,16},{24,28},{28,24},{1,5},{5... | collective-permute-start | bytes 3145736 | tf_op jit(solution)/shard_map/ppermute | solution.py:922
  152.5 14.7 %collective-permute-start.21 = (bf16[2,4,128,512]{3,2,1,0:T(8,128)(2,1)S(1)}, bf16[2,4,128,512]{3,2,1,0:T(8,128)(2,1)}, u32[]{:S(2)}, u32[]{:S(2)}) collective-permute-start(bf16[2,4,128,512]{3,2,1,0:T(8,128)(2,1)S(1)} %collective-permute-done.18.refs_1_), channel_id=1, source_target_pairs={{0,4},{4,0},{8,12},{12,8},{16,20},{20,16},{24,28},{28,24},{1,5},{5... | collective-permute-start | bytes 3145736 | tf_op jit(solution)/shard_map/ppermute | solution.py:922
  152.5 14.7 %collective-permute-start.23 = (bf16[2,4,128,512]{3,2,1,0:T(8,128)(2,1)S(1)}, bf16[2,4,128,512]{3,2,1,0:T(8,128)(2,1)}, u32[]{:S(2)}, u32[]{:S(2)}) collective-permute-start(bf16[2,4,128,512]{3,2,1,0:T(8,128)(2,1)S(1)} %collective-permute-done.19.refs_5_), channel_id=1, source_target_pairs={{0,4},{4,0},{8,12},{12,8},{16,20},{20,16},{24,28},{28,24},{1,5},{5... | collective-permute-start | bytes 3145736 | tf_op jit(solution)/shard_map/ppermute | solution.py:922
  153.0 13.8 %collective-permute-start.24 = (bf16[4,128,512]{2,1,0:T(8,128)(2,1)S(1)}, bf16[4,128,512]{2,1,0:T(8,128)(2,1)S(1)}, u32[]{:S(2)}, u32[]{:S(2)}) collective-permute-start(bf16[4,128,512]{2,1,0:T(8,128)(2,1)S(1)} %get-tuple-element.299), channel_id=1, source_target_pairs={{0,8},{4,12},{8,0},{12,4},{16,24},{20,28},{24,16},{28,20},{1,9},{5... | collective-permute-start | bytes 1572872 | tf_op jit(solution)/shard_map/ppermute | solution.py:922
  153.6 13.6 %collective-permute-start.25 = (bf16[4,128,512]{2,1,0:T(8,128)(2,1)S(1)}, bf16[4,128,512]{2,1,0:T(8,128)(2,1)S(1)}, u32[]{:S(2)}, u32[]{:S(2)}) collective-permute-start(bf16[4,128,512]{2,1,0:T(8,128)(2,1)S(1)} %get-tuple-element.300), channel_id=1, source_target_pairs={{0,16},{4,20},{8,24},{12,28},{16,0},{20,4},{24,8},{28,12},{1,17},{... | collective-permute-start | bytes 1572872 | tf_op jit(solution)/shard_map/ppermute | solution.py:922
  167.5 45.4 %collective-permute-start.26 = (bf16[2,4,128,512]{3,2,1,0:T(8,128)(2,1)S(1)}, bf16[2,4,128,512]{3,2,1,0:T(8,128)(2,1)S(1)}, u32[]{:S(2)}, u32[]{:S(2)}) collective-permute-start(bf16[2,4,128,512]{3,2,1,0:T(8,128)(2,1)S(1)} %bitcast.199), channel_id=1, source_target_pairs={{0,16},{4,20},{8,24},{12,28},{16,0},{20,4},{24,8},{28,12},{1,17},{... | collective-permute-start | bytes 3145736 | tf_op jit(solution)/shard_map/ppermute | solution.py:922
  169.0 44.0 %collective-permute-start.27 = (bf16[2,4,128,512]{3,2,1,0:T(8,128)(2,1)S(1)}, bf16[2,4,128,512]{3,2,1,0:T(8,128)(2,1)}, u32[]{:S(2)}, u32[]{:S(2)}) collective-permute-start(bf16[2,4,128,512]{3,2,1,0:T(8,128)(2,1)S(1)} %bitcast.202), channel_id=1, source_target_pairs={{0,8},{4,12},{8,0},{12,4},{16,24},{20,28},{24,16},{28,20},{1,9},{5... | collective-permute-start | bytes 3145736 | tf_op jit(solution)/shard_map/ppermute | solution.py:922
  172.0 45.5 %collective-permute-start.28 = (bf16[2,4,128,512]{3,2,1,0:T(8,128)(2,1)S(1)}, bf16[2,4,128,512]{3,2,1,0:T(8,128)(2,1)}, u32[]{:S(2)}, u32[]{:S(2)}) collective-permute-start(bf16[2,4,128,512]{3,2,1,0:T(8,128)(2,1)S(1)} %bitcast.200), channel_id=1, source_target_pairs={{0,4},{4,0},{8,12},{12,8},{16,20},{20,16},{24,28},{28,24},{1,5},{5... | collective-permute-start | bytes 3145736 | tf_op jit(solution)/shard_map/ppermute | solution.py:922
  172.0 45.5 %collective-permute-start.30 = (bf16[2,4,128,512]{3,2,1,0:T(8,128)(2,1)S(1)}, bf16[2,4,128,512]{3,2,1,0:T(8,128)(2,1)}, u32[]{:S(2)}, u32[]{:S(2)}) collective-permute-start(bf16[2,4,128,512]{3,2,1,0:T(8,128)(2,1)S(1)} %bitcast.203), channel_id=1, source_target_pairs={{0,4},{4,0},{8,12},{12,8},{16,20},{20,16},{24,28},{28,24},{1,5},{5... | collective-permute-start | bytes 3145736 | tf_op jit(solution)/shard_map/ppermute | solution.py:922
  213.0 4.4 collective-permute-start.29
  213.1 5.4 %collective-permute-start.31 = (bf16[2,4,128,512]{3,2,1,0:T(8,128)(2,1)}, bf16[2,4,128,512]{3,2,1,0:T(8,128)(2,1)S(1)}, u32[]{:S(2)}, u32[]{:S(2)}) collective-permute-start(bf16[2,4,128,512]{3,2,1,0:T(8,128)(2,1)} %collective-permute-done.27.refs_5_), channel_id=1, source_target_pairs={{0,4},{4,0},{8,12},{12,8},{16,20},{20,16},{24,28},{28,24},{1,5},{5... | collective-permute-start | bytes 3145736 | tf_op jit(solution)/shard_map/ppermute | solution.py:922
  219.4 41.1 %collective-permute-start.32 = (bf16[4,4,128,512]{3,2,1,0:T(8,128)(2,1)}, bf16[4,4,128,512]{3,2,1,0:T(8,128)(2,1)S(1)}, u32[]{:S(2)}, u32[]{:S(2)}) collective-permute-start(bf16[4,4,128,512]{3,2,1,0:T(8,128)(2,1)} %get-tuple-element.344), channel_id=1, source_target_pairs={{0,4},{4,0},{8,12},{12,8},{16,20},{20,16},{24,28},{28,24},{1,5},{5... | collective-permute-start | bytes 6291464 | tf_op jit(solution)/shard_map/ppermute | solution.py:922
  219.5 41.0 %collective-permute-start.33 = (bf16[4,4,128,512]{3,2,1,0:T(8,128)(2,1)}, bf16[4,4,128,512]{3,2,1,0:T(8,128)(2,1)}, u32[]{:S(2)}, u32[]{:S(2)}) collective-permute-start(bf16[4,4,128,512]{3,2,1,0:T(8,128)(2,1)} %get-tuple-element.345), channel_id=1, source_target_pairs={{0,4},{4,0},{8,12},{12,8},{16,20},{20,16},{24,28},{28,24},{1,5},{5... | collective-permute-start | bytes 6291464 | tf_op jit(solution)/shard_map/ppermute | solution.py:922
  260.5 26.0 %collective-permute-start.34 = (bf16[4,4,128,512]{3,2,1,0:T(8,128)(2,1)}, bf16[4,4,128,512]{3,2,1,0:T(8,128)(2,1)}, u32[]{:S(2)}, u32[]{:S(2)}) collective-permute-start(bf16[4,4,128,512]{3,2,1,0:T(8,128)(2,1)} %get-tuple-element.361), channel_id=1, source_target_pairs={{0,4},{4,0},{8,12},{12,8},{16,20},{20,16},{24,28},{28,24},{1,5},{5... | collective-permute-start | bytes 6291464 | tf_op jit(solution)/shard_map/ppermute | solution.py:922
  260.7 25.8 %collective-permute-start.35 = (bf16[4,4,128,512]{3,2,1,0:T(8,128)(2,1)}, bf16[4,4,128,512]{3,2,1,0:T(8,128)(2,1)}, u32[]{:S(2)}, u32[]{:S(2)}) collective-permute-start(bf16[4,4,128,512]{3,2,1,0:T(8,128)(2,1)} %get-tuple-element.362), channel_id=1, source_target_pairs={{0,4},{4,0},{8,12},{12,8},{16,20},{20,16},{24,28},{28,24},{1,5},{5... | collective-permute-start | bytes 6291464 | tf_op jit(solution)/shard_map/ppermute | solution.py:922
  266.8 46.9 %collective-permute-start.36 = (bf16[2,512,512]{2,1,0:T(8,128)(2,1)}, bf16[2,512,512]{2,1,0:T(8,128)(2,1)S(1)}, u32[]{:S(2)}, u32[]{:S(2)}) collective-permute-start(bf16[2,512,512]{2,1,0:T(8,128)(2,1)} %get-tuple-element.352), channel_id=1, source_target_pairs={{0,16},{4,20},{8,24},{12,28},{16,0},{20,4},{24,8},{28,12},{1,17},{... | collective-permute-start | bytes 3145736 | tf_op jit(solution)/shard_map/ppermute | solution.py:922
  267.3 46.4 %collective-permute-start.37 = (bf16[2,512,512]{2,1,0:T(8,128)(2,1)}, bf16[2,512,512]{2,1,0:T(8,128)(2,1)S(1)}, u32[]{:S(2)}, u32[]{:S(2)}) collective-permute-start(bf16[2,512,512]{2,1,0:T(8,128)(2,1)} %get-tuple-element.353), channel_id=1, source_target_pairs={{0,8},{4,12},{8,0},{12,4},{16,24},{20,28},{24,16},{28,20},{1,9},{5... | collective-permute-start | bytes 3145736 | tf_op jit(solution)/shard_map/ppermute | solution.py:922
  290.6 48.3 %collective-permute-start.40 = (bf16[2,512,512]{2,1,0:T(8,128)(2,1)S(1)}, bf16[2,512,512]{2,1,0:T(8,128)(2,1)S(1)}, u32[]{:S(2)}, u32[]{:S(2)}) collective-permute-start(bf16[2,512,512]{2,1,0:T(8,128)(2,1)S(1)} %get-tuple-element.368), channel_id=1, source_target_pairs={{0,16},{4,20},{8,24},{12,28},{16,0},{20,4},{24,8},{28,12},{1,17},{... | collective-permute-start | bytes 3145736 | tf_op jit(solution)/shard_map/ppermute | solution.py:922
  292.1 46.8 %collective-permute-start.41 = (bf16[2,512,512]{2,1,0:T(8,128)(2,1)S(1)}, bf16[2,512,512]{2,1,0:T(8,128)(2,1)}, u32[]{:S(2)}, u32[]{:S(2)}) collective-permute-start(bf16[2,512,512]{2,1,0:T(8,128)(2,1)S(1)} %get-tuple-element.369), channel_id=1, source_target_pairs={{0,8},{4,12},{8,0},{12,4},{16,24},{20,28},{24,16},{28,20},{1,9},{5... | collective-permute-start | bytes 3145736 | tf_op jit(solution)/shard_map/ppermute | solution.py:922
  316.3 22.5 %collective-permute-start.38 = (bf16[512,512]{1,0:T(8,128)(2,1)S(1)}, bf16[512,512]{1,0:T(8,128)(2,1)S(1)}, u32[]{:S(2)}, u32[]{:S(2)}) collective-permute-start(bf16[512,512]{1,0:T(8,128)(2,1)S(1)} %get-tuple-element.378), channel_id=1, source_target_pairs={{0,8},{4,12},{8,0},{12,4},{16,24},{20,28},{24,16},{28,20},{1,9},{5... | collective-permute-start | bytes 1572872 | tf_op jit(solution)/shard_map/ppermute | solution.py:922
  316.9 21.9 %collective-permute-start.39 = (bf16[512,512]{1,0:T(8,128)(2,1)S(1)}, bf16[512,512]{1,0:T(8,128)(2,1)S(1)}, u32[]{:S(2)}, u32[]{:S(2)}) collective-permute-start(bf16[512,512]{1,0:T(8,128)(2,1)S(1)} %get-tuple-element.379), channel_id=1, source_target_pairs={{0,16},{4,20},{8,24},{12,28},{16,0},{20,4},{24,8},{28,12},{1,17},{... | collective-permute-start | bytes 1572872 | tf_op jit(solution)/shard_map/ppermute | solution.py:922
  342.9 16.6 %collective-permute-start.42 = (bf16[512,512]{1,0:T(8,128)(2,1)S(1)}, bf16[512,512]{1,0:T(8,128)(2,1)S(1)}, u32[]{:S(2)}, u32[]{:S(2)}) collective-permute-start(bf16[512,512]{1,0:T(8,128)(2,1)S(1)} %get-tuple-element.395), channel_id=1, source_target_pairs={{0,8},{4,12},{8,0},{12,4},{16,24},{20,28},{24,16},{28,20},{1,9},{5... | collective-permute-start | bytes 1572872 | tf_op jit(solution)/shard_map/ppermute | solution.py:922
  344.3 15.2 %collective-permute-start.43 = (bf16[512,512]{1,0:T(8,128)(2,1)S(1)}, bf16[512,512]{1,0:T(8,128)(2,1)S(1)}, u32[]{:S(2)}, u32[]{:S(2)}) collective-permute-start(bf16[512,512]{1,0:T(8,128)(2,1)S(1)} %get-tuple-element.396), channel_id=1, source_target_pairs={{0,16},{4,20},{8,24},{12,28},{16,0},{20,4},{24,8},{28,12},{1,17},{... | collective-permute-start | bytes 1572872 | tf_op jit(solution)/shard_map/ppermute | solution.py:922
  359.5 16.6 %collective-permute-start.44 = (bf16[4,4,2,128,256]{4,3,2,1,0:T(8,128)(2,1)}, bf16[4,4,2,128,256]{4,3,2,1,0:T(8,128)(2,1)S(1)}, u32[]{:S(2)}, u32[]{:S(2)}) collective-permute-start(bf16[4,4,2,128,256]{4,3,2,1,0:T(8,128)(2,1)} %get-tuple-element.416), channel_id=1, source_target_pairs={{0,4},{4,0},{8,12},{12,8},{16,20},{20,16},{24,28},{28,24},{1,5},{5... | collective-permute-start | bytes 6291464 | tf_op jit(solution)/shard_map/ppermute | solution.py:922
  359.5 16.5 %collective-permute-start.45 = (bf16[4,4,2,128,256]{4,3,2,1,0:T(8,128)(2,1)}, bf16[4,4,2,128,256]{4,3,2,1,0:T(8,128)(2,1)S(1)}, u32[]{:S(2)}, u32[]{:S(2)}) collective-permute-start(bf16[4,4,2,128,256]{4,3,2,1,0:T(8,128)(2,1)} %get-tuple-element.417), channel_id=1, source_target_pairs={{0,4},{4,0},{8,12},{12,8},{16,20},{20,16},{24,28},{28,24},{1,5},{5... | collective-permute-start | bytes 6291464 | tf_op jit(solution)/shard_map/ppermute | solution.py:922
  364.6 38.0 %collective-permute-start.48 = (bf16[2,512,512]{2,1,0:T(8,128)(2,1)}, bf16[2,512,512]{2,1,0:T(8,128)(2,1)S(1)}, u32[]{:S(2)}, u32[]{:S(2)}) collective-permute-start(bf16[2,512,512]{2,1,0:T(8,128)(2,1)} %get-tuple-element.412), channel_id=1, source_target_pairs={{0,1},{1,0},{2,3},{3,2},{4,5},{5,4},{6,7},{7,6},{8,9},{9,8},{10,11... | collective-permute-start | bytes 3145736 | tf_op jit(solution)/shard_map/ppermute | solution.py:922
  382.3 24.6 %collective-permute-start.46 = (bf16[2,1024,256]{2,1,0:T(8,128)(2,1)S(1)}, bf16[2,1024,256]{2,1,0:T(8,128)(2,1)S(1)}, u32[]{:S(2)}, u32[]{:S(2)}) collective-permute-start(bf16[2,1024,256]{2,1,0:T(8,128)(2,1)S(1)} %get-tuple-element.423), channel_id=1, source_target_pairs={{0,16},{4,20},{8,24},{12,28},{16,0},{20,4},{24,8},{28,12},{1,17},{... | collective-permute-start | bytes 3145736 | tf_op jit(solution)/shard_map/ppermute | solution.py:922
  382.9 24.2 %collective-permute-start.47 = (bf16[2,1024,256]{2,1,0:T(8,128)(2,1)S(1)}, bf16[2,1024,256]{2,1,0:T(8,128)(2,1)S(1)}, u32[]{:S(2)}, u32[]{:S(2)}) collective-permute-start(bf16[2,1024,256]{2,1,0:T(8,128)(2,1)S(1)} %get-tuple-element.424), channel_id=1, source_target_pairs={{0,8},{4,12},{8,0},{12,4},{16,24},{20,28},{24,16},{28,20},{1,9},{5... | collective-permute-start | bytes 3145736 | tf_op jit(solution)/shard_map/ppermute | solution.py:922
  411.5 6.0 %collective-permute-start.49 = (f32[14,1024]{1,0:T(8,128)S(1)}, f32[14,1024]{1,0:T(8,128)S(1)}, u32[]{:S(2)}, u32[]{:S(2)}) collective-permute-start(f32[14,1024]{1,0:T(8,128)S(1)} %concatenate.61), channel_id=1, source_target_pairs={{0,1},{1,0},{2,3},{3,2},{4,5},{5,4},{6,7},{7,6},{8,9},{9,8},{10,11... | collective-permute-start | bytes 172040 | tf_op jit(solution)/shard_map/ppermute | solution.py:922
  412.2 11.9 %collective-permute-start.51 = (bf16[1024,256]{1,0:T(8,128)(2,1)S(1)}, bf16[1024,256]{1,0:T(8,128)(2,1)S(1)}, u32[]{:S(2)}, u32[]{:S(2)}) collective-permute-start(bf16[1024,256]{1,0:T(8,128)(2,1)S(1)} %get-tuple-element.436), channel_id=1, source_target_pairs={{0,8},{4,12},{8,0},{12,4},{16,24},{20,28},{24,16},{28,20},{1,9},{5... | collective-permute-start | bytes 1572872 | tf_op jit(solution)/shard_map/ppermute | solution.py:922
  412.9 11.5 %collective-permute-start.52 = (bf16[1024,256]{1,0:T(8,128)(2,1)S(1)}, bf16[1024,256]{1,0:T(8,128)(2,1)S(1)}, u32[]{:S(2)}, u32[]{:S(2)}) collective-permute-start(bf16[1024,256]{1,0:T(8,128)(2,1)S(1)} %get-tuple-element.437), channel_id=1, source_target_pairs={{0,16},{4,20},{8,24},{12,28},{16,0},{20,4},{24,8},{28,12},{1,17},{... | collective-permute-start | bytes 1572872 | tf_op jit(solution)/shard_map/ppermute | solution.py:922
  417.6 5.2 collective-permute-start.50
  428.4 21.7 %collective-permute-start.53 = (bf16[2,512,256]{2,1,0:T(8,128)(2,1)}, bf16[2,512,256]{2,1,0:T(8,128)(2,1)S(1)}, u32[]{:S(2)}, u32[]{:S(2)}) collective-permute-start(bf16[2,512,256]{2,1,0:T(8,128)(2,1)} %get-tuple-element.460), channel_id=1, source_target_pairs={{0,1},{1,0},{2,3},{3,2},{4,5},{5,4},{6,7},{7,6},{8,9},{9,8},{10,11... | collective-permute-start | bytes 1572872 | tf_op jit(solution)/shard_map/ppermute | solution.py:922
  430.5 36.3 %collective-permute-start.57 = (bf16[512,512]{1,0:T(8,128)(2,1)S(1)}, bf16[512,512]{1,0:T(8,128)(2,1)S(1)}, u32[]{:S(2)}, u32[]{:S(2)}) collective-permute-start(bf16[512,512]{1,0:T(8,128)(2,1)S(1)} %copy-done.70), channel_id=1, source_target_pairs={{0,2},{1,3},{2,0},{3,1},{4,6},{5,7},{6,4},{7,5},{8,10},{9,11},{10,... | collective-permute-start | bytes 1572872 | tf_op jit(solution)/shard_map/ppermute | solution.py:922
  453.6 13.2 %collective-permute-start.56 = (bf16[512,256]{1,0:T(8,128)(2,1)}, bf16[512,256]{1,0:T(8,128)(2,1)S(1)}, u32[]{:S(2)}, u32[]{:S(2)}) collective-permute-start(bf16[512,256]{1,0:T(8,128)(2,1)} %get-tuple-element.469), channel_id=1, source_target_pairs={{0,2},{1,3},{2,0},{3,1},{4,6},{5,7},{6,4},{7,5},{8,10},{9,11},{10,... | collective-permute-start | bytes 786440 | tf_op jit(solution)/shard_map/ppermute | solution.py:922
  455.1 11.8 %collective-permute-start.54 = (bf16[1,48,1024]{2,1,0:T(8,128)(2,1)S(1)}, bf16[1,48,1024]{2,1,0:T(8,128)(2,1)S(1)}, u32[]{:S(2)}, u32[]{:S(2)}) collective-permute-start(bf16[1,48,1024]{2,1,0:T(8,128)(2,1)S(1)} %get-tuple-element.518), channel_id=1, source_target_pairs={{0,8},{4,12},{8,0},{12,4},{16,24},{20,28},{24,16},{28,20},{1,9},{5... | collective-permute-start | bytes 294920 | tf_op jit(solution)/shard_map/ppermute | solution.py:922
  456.4 10.4 %collective-permute-start.55 = (bf16[1,48,1024]{2,1,0:T(8,128)(2,1)S(1)}, bf16[1,48,1024]{2,1,0:T(8,128)(2,1)S(1)}, u32[]{:S(2)}, u32[]{:S(2)}) collective-permute-start(bf16[1,48,1024]{2,1,0:T(8,128)(2,1)S(1)} %get-tuple-element.517), channel_id=1, source_target_pairs={{0,16},{4,20},{8,24},{12,28},{16,0},{20,4},{24,8},{28,12},{1,17},{... | collective-permute-start | bytes 294920 | tf_op jit(solution)/shard_map/ppermute | solution.py:922
  467.7 6.9 %collective-permute-start.58 = (bf16[2,48,1024]{2,1,0:T(8,128)(2,1)S(1)}, bf16[2,48,1024]{2,1,0:T(8,128)(2,1)S(1)}, u32[]{:S(2)}, u32[]{:S(2)}) collective-permute-start(bf16[2,48,1024]{2,1,0:T(8,128)(2,1)S(1)} %pad_maximum_fusion.6), channel_id=1, source_target_pairs={{0,16},{4,20},{8,24},{12,28},{16,0},{20,4},{24,8},{28,12},{1,17},{... | collective-permute-start | bytes 589832 | tf_op jit(solution)/shard_map/ppermute | solution.py:922
  468.3 6.2 %collective-permute-start.59 = (bf16[2,48,1024]{2,1,0:T(8,128)(2,1)S(1)}, bf16[2,48,1024]{2,1,0:T(8,128)(2,1)S(1)}, u32[]{:S(2)}, u32[]{:S(2)}) collective-permute-start(bf16[2,48,1024]{2,1,0:T(8,128)(2,1)S(1)} %pad_maximum_fusion.7), channel_id=1, source_target_pairs={{0,8},{4,12},{8,0},{12,4},{16,24},{20,28},{24,16},{28,20},{1,9},{5... | collective-permute-start | bytes 589832 | tf_op jit(solution)/shard_map/ppermute | solution.py:922
  483.9 4.5 collective-permute-start.65
  488.8 4.7 collective-permute-start.67
  491.3 5.4 %collective-permute-start.68 = (f32[8,128]{1,0:T(8,128)S(1)}, f32[8,128]{1,0:T(8,128)S(1)}, u32[]{:S(2)}, u32[]{:S(2)}) collective-permute-start(f32[8,128]{1,0:T(8,128)S(1)} %add_add_fusion.1), channel_id=1, source_target_pairs={{0,3},{1,2},{2,1},{3,0},{4,7},{5,6},{6,5},{7,4},{8,11},{9,10},{10,... | collective-permute-start | bytes 12296 | tf_op jit(solution)/shard_map/ppermute | solution.py:922
  (78 other events, 683.1 us)
Sparse Core Ops, SparseCore 0:
  10.2 31.1 all-gather.4
  43.6 45.4 all-gather.6
